TPU v7x, 128 devices: a whole 4x4x4 slice. The times are simulated.
128 devices in a mesh: dp: 32 (over y, x, core), tensor: 4 (over z).
Axes of the slice: x: 4, y: 4, z: 4, core: 2. Of those that a mesh axis runs over, the one named last changes fastest.
Arguments:
- hidden: bfloat16 [8192, 4096], P('dp', 'tensor'), may hold values from -3 to 3
- cotangent: bfloat16 [8192, 4096], P('dp', 'tensor'), may hold values from -3 to 3
- counts: int32 [32, 4], P('dp'), may hold values from 0 to 4, as said below
- slot_of: int32 [32, 4, 4], P('dp'), may hold values from 0 to 31, as said below
- neighbours: bfloat16 [1024, 128, 896], P('dp', 'tensor'), may hold values from -3 to 3
- query_weight: bfloat16 [4096, 2048], P(None, 'tensor'), may hold values from -0.09375 to 0.09375
- key_weight: bfloat16 [896, 2048], P(None, 'tensor'), may hold values from -0.1875 to 0.1875
- value_weight: bfloat16 [896, 2048], P(None, 'tensor'), may hold values from -0.1875 to 0.1875
- out_weight: bfloat16 [2048, 4096], P('tensor'), may hold values from -0.125 to 0.125
- cond_weight: bfloat16 [4096, 1792], P('tensor'), may hold values from -0.09375 to 0.09375
- enc_query: bfloat16 [896, 896], replicated, may hold values from -0.1875 to 0.1875
- enc_out: bfloat16 [896, 896], replicated, may hold values from -0.1875 to 0.1875
Outputs:
- mixed: bfloat16 [8192, 4096], P('dp', 'tensor')
- grad_hidden: bfloat16 [8192, 4096], P('dp', 'tensor')
Inputs may be any that keep to these rules, and one draw needn't show every extreme that they name: `slot_of`: within one sequence the entries are distinct. `counts`: every sequence has a block with 4 neighbours.
All inputs are finite; a program needn't handle non-finite values.
Results may differ from a plain program's by a relative error of at most 0.0095.
Values may be sent and summed in bfloat16 or wider, within the bound.
No kernel may reach another device: no remote copies, remote signals or barrier semaphores. Data moves between devices by JAX's collectives and lax.ppermute only.
A program may use at most 128 MiB of HBM per device.

v0:
```python
import functools
import math

import jax
import jax.numpy as jnp
from jax import lax
from jax.experimental import pallas as pl
from jax.experimental.pallas import tpu as pltpu
from jax.sharding import PartitionSpec as P

HEAD_DIM = 128
ENC_HEAD_DIM = 128
F32 = jnp.float32
BF16 = jnp.bfloat16
PLAIN = (((1,), (0,)), ((), ()))
ROWS_T = (((1,), (1,)), ((), ()))
COLS_T = (((0,), (0,)), ((), ()))
SCALING = 1.0 / math.sqrt(HEAD_DIM)
ENC_SCALING = 1.0 / math.sqrt(ENC_HEAD_DIM)
SLICE = 32


def dot(a, b, dims=PLAIN):
    return lax.dot_general(a, b, dims, preferred_element_type=F32)


def call(kernel, name, grid, in_specs, out_specs, out_shape, scratch, vmem_mib):
    return pl.pallas_call(
        kernel,
        out_shape=out_shape,
        grid_spec=pltpu.PrefetchScalarGridSpec(
            num_scalar_prefetch=1,
            grid=(grid,),
            in_specs=in_specs,
            out_specs=out_specs,
            scratch_shapes=scratch,
        ),
        compiler_params=pltpu.CompilerParams(
            vmem_limit_bytes=vmem_mib * 1024 * 1024, dimension_semantics=("arbitrary",)
        ),
        name=name,
    )


def whole(*shape):
    return pl.BlockSpec(shape, lambda g, s: (0,) * len(shape))


def group(*shape):
    return pl.BlockSpec((1,) + shape, lambda g, s: (g,) + (0,) * len(shape))


def exchange(pieces, position, axis="tensor"):
    size = pieces.shape[0]
    out = [lax.dynamic_index_in_dim(pieces, position, 0, keepdims=False)]
    for k in range(1, size):
        piece = lax.dynamic_index_in_dim(pieces, (position - k) % size, 0, keepdims=False)
        out.append(lax.ppermute(piece, axis, [(i, (i - k) % size) for i in range(size)]))
    return out


def spread(shard, size, axis="tensor"):
    return [shard] + [
        lax.ppermute(shard, axis, [(i, (i - k) % size) for i in range(size)])
        for k in range(1, size)
    ]


def after(value, earlier):
    return lax.optimization_barrier((value, earlier))[0]


def live_columns(count, shape):
    column = lax.broadcasted_iota(jnp.int32, shape, len(shape) - 1)
    return (column // 32) % 4 < count


def by_heads(array, head_dim):
    head = lax.broadcasted_iota(jnp.int32, array.shape, 1) // head_dim
    zero = jnp.zeros_like(array)
    count = array.shape[1] // head_dim
    return jnp.concatenate([jnp.where(head == h, array, zero) for h in range(count)], axis=0)


def head_blocks(array, rows, head_dim):
    count = array.shape[1] // head_dim
    return [
        array[h * rows : (h + 1) * rows, h * head_dim : (h + 1) * head_dim] for h in range(count)
    ]


def cond_kernel(s_ref, hidden_ref, weight_ref, c0, c1, c2, c3, total_ref):
    length = c0.shape[0]
    total_ref[...] = dot(hidden_ref[...], weight_ref[...])
    for k, ref in enumerate((c0, c1, c2, c3)):
        start = pl.multiple_of(((s_ref[0] + 4 - k) % 4) * length, length)
        ref[...] = total_ref[pl.ds(start, length), :].astype(BF16)


def project_kernel(dims, shift, s_ref, p0, p1, p2, p3, weight_ref, *rest):
    out_ref, total_ref = rest[-2:]
    step = pl.program_id(0)
    for k, ref in enumerate((p0, p1, p2, p3)):

        @pl.when(step == k)
        def _(ref=ref, k=k):
            term = dot(ref[: total_ref.shape[0], :], weight_ref[...], dims)
            total_ref[...] = term if k == 0 else total_ref[...] + term

    @pl.when(step == pl.num_programs(0) - 1)
    def _():
        rows = total_ref.shape[0]
        moved = pltpu.roll(total_ref[...], rows - shift, 0)
        index = lax.broadcasted_iota(jnp.int32, moved.shape, 0)
        result = jnp.where(index < rows - shift, moved, 0.0).astype(BF16)
        if len(rest) == 2:
            out_ref[...] = result
        else:
            blocks, _, length, _ = out_ref.shape
            for block in range(blocks):
                span = slice(block * length, (block + 1) * length)
                out_ref[block, 0] = rest[0][span, :]
                out_ref[block, 1] = result[span, :]


def encode_kernel(
    s_ref,
    x_ref,
    c0,
    c1,
    c2,
    c3,
    enc_query_ref,
    enc_out_ref,
    cond_ref,
    queries_ref,
    probs_ref,
    encoded_ref,
):
    width = x_ref.shape[1]
    x = x_ref[...]
    cond = (c0[...].astype(F32) + c1[...].astype(F32)) + (
        c2[...].astype(F32) + c3[...].astype(F32)
    )
    cond = cond.astype(BF16)
    cond_ref[...] = cond
    length = cond.shape[0]
    queries = dot(x, enc_query_ref[...]).astype(BF16)
    queries_ref[...] = queries
    attended = []
    for head in range(width // ENC_HEAD_DIM):
        cols = slice(head * ENC_HEAD_DIM, (head + 1) * ENC_HEAD_DIM)
        vals = slice(width + head * ENC_HEAD_DIM, width + (head + 1) * ENC_HEAD_DIM)
        exponents = jnp.exp(dot(cond[:, cols], queries[:, cols], ROWS_T) * ENC_SCALING)
        probs = exponents / jnp.sum(exponents, axis=0, keepdims=True)
        probs_ref[head * length : (head + 1) * length, :] = probs
        attended.append(dot(probs.astype(BF16), cond[:, vals], COLS_T).astype(BF16))
    attended = jnp.concatenate(attended, axis=1)
    mixing = dot(attended, enc_out_ref[...])
    encoded_ref[...] = (x.astype(F32) + mixing).astype(BF16)


def attention_kernel(
    s_ref,
    encoded_ref,
    key_w_ref,
    val_w_ref,
    query_ref,
    probs_ref,
    d_scores_ref,
    out_ref,
):
    width = encoded_ref.shape[1]
    length = out_ref.shape[1]
    encoded = encoded_ref[...]
    keys = dot(encoded, key_w_ref[...].reshape(-1, key_w_ref.shape[3])[:width]).astype(BF16)
    vals = dot(encoded, val_w_ref[...].reshape(-1, val_w_ref.shape[3])[:width]).astype(BF16)
    count = s_ref[1]
    scores = dot(by_heads(query_ref[0, 0], HEAD_DIM), keys, ROWS_T) * SCALING
    expd = jnp.where(live_columns(count, scores.shape), jnp.exp(scores), 0.0)
    totals = jnp.sum(expd, axis=1, keepdims=True)
    probs = expd / jnp.where(count > 0, totals, 1.0)
    probs_low = probs.astype(BF16)
    probs_ref[0] = probs_low
    ctx = head_blocks(dot(probs_low, vals), length, HEAD_DIM)
    out_ref[0] = jnp.concatenate(ctx, axis=1).astype(BF16)
    weighted = probs * dot(by_heads(query_ref[0, 1], HEAD_DIM), vals, ROWS_T)
    d_scores = (weighted - probs * jnp.sum(weighted, axis=1, keepdims=True)) * SCALING
    d_scores = d_scores.astype(BF16)
    d_scores_ref[0] = d_scores
    d_query = head_blocks(dot(d_scores, keys), length, HEAD_DIM)
    out_ref[1] = jnp.concatenate(d_query, axis=1).astype(BF16)


def encoded_back_kernel(
    s_ref,
    d_scores_ref,
    probs_ref,
    query_ref,
    key_w_ref,
    val_w_ref,
    enc_out_ref,
    enc_probs_ref,
    enc_queries_ref,
    cond_ref,
    d_cond_ref,
    total_ref,
):
    step = pl.program_id(0)
    width = total_ref.shape[1]
    d_keys = dot(d_scores_ref[0], by_heads(query_ref[0, 0], HEAD_DIM), COLS_T).astype(BF16)
    d_vals = dot(probs_ref[0], by_heads(query_ref[0, 1], HEAD_DIM), COLS_T).astype(BF16)
    term = dot(d_keys, key_w_ref[...].reshape(-1, key_w_ref.shape[3])[:width], ROWS_T)
    term = term + dot(d_vals, val_w_ref[...].reshape(-1, val_w_ref.shape[3])[:width], ROWS_T)
    term = term.astype(BF16).astype(F32)

    @pl.when(step == 0)
    def _():
        total_ref[...] = term

    @pl.when(step > 0)
    def _():
        total_ref[...] += term

    @pl.when(step == pl.num_programs(0) - 1)
    def _():
        length = cond_ref.shape[0]
        d_att = dot(total_ref[...].astype(BF16), enc_out_ref[...], ROWS_T).astype(BF16)
        probs = enc_probs_ref[...]
        d_probs = dot(by_heads(cond_ref[:, width:], ENC_HEAD_DIM), d_att, ROWS_T)
        weighted = probs * d_probs
        sums = jnp.sum(weighted.reshape(-1, length, weighted.shape[1]), axis=1, keepdims=True)
        spread_sums = (probs.reshape(-1, length, probs.shape[1]) * sums).reshape(probs.shape)
        d_scores = (weighted - spread_sums) * ENC_SCALING
        live = live_columns(s_ref[1], probs.shape)
        d_scores = jnp.where(live, d_scores, 0.0).astype(BF16)
        low = jnp.where(live, probs, 0.0).astype(BF16)
        d_keys = head_blocks(dot(d_scores, enc_queries_ref[...]), length, ENC_HEAD_DIM)
        d_vals = head_blocks(dot(low, d_att), length, ENC_HEAD_DIM)
        d_cond_ref[...] = jnp.concatenate(d_keys + d_vals, axis=1).astype(BF16)


def placed_rows(rows, by, shift):
    moved = pltpu.roll(rows, by, 0)
    if shift == 0:
        return moved
    index = lax.broadcasted_iota(jnp.int32, rows.shape, 0)
    return jnp.where(index >= shift, moved, 0.0)


def outputs_kernel(
    shift,
    s_ref,
    c0,
    c1,
    c2,
    c3,
    out_w_ref,
    query_w_ref,
    hidden_ref,
    cotangent_ref,
    mixed_ref,
    grad_ref,
    mixed_sum_ref,
    grad_sum_ref,
):
    step = pl.program_id(0)
    half = out_w_ref.shape[2] // 2
    wide = out_w_ref.shape[3]
    length = c0.shape[1]
    parts = (c0, c1, c2, c3)
    ctx = jnp.concatenate([ref[0] for ref in parts], axis=0)
    d_query = jnp.concatenate([ref[1] for ref in parts], axis=0)

    @pl.when(step == 0)
    def _():
        mixed_sum_ref[...] = jnp.zeros_like(mixed_sum_ref)
        grad_sum_ref[...] = jnp.zeros_like(grad_sum_ref)

    for side in range(2):
        weight = out_w_ref[:, :, side * half : (side + 1) * half, :].reshape(-1, wide)
        mixed_sum_ref[:, side * wide : (side + 1) * wide] += dot(ctx, weight)
    grad_sum_ref[...] += dot(d_query, query_w_ref[...].reshape(-1, wide), ROWS_T)

    @pl.when(step == pl.num_programs(0) - 1)
    def _():
        by = (s_ref[0] * length + shift) % mixed_ref.shape[0]
        moved = placed_rows(mixed_sum_ref[...], by, shift)
        mixed_ref[...] = (hidden_ref[...].astype(F32) + moved).astype(mixed_ref.dtype)
        moved = placed_rows(grad_sum_ref[...], by, shift)
        grad_ref[...] = cotangent_ref[...].astype(F32) + moved


def cond_grad_kernel(s_ref, c0, c1, c2, c3, weight_ref, base_ref, out_ref):
    length = c0.shape[0]
    d_cond = jnp.concatenate([c0[...], c1[...], c2[...], c3[...]], axis=0)
    term = dot(d_cond, weight_ref[...], ROWS_T)
    by = s_ref[0] * length
    out_ref[...] = (base_ref[...] + placed_rows(term, by, 0)).astype(out_ref.dtype)


def shards(
    hidden,
    cotangent,
    counts,
    slot_of,
    neighbours,
    query_weight,
    key_weight,
    value_weight,
    out_weight,
    cond_weight,
    enc_query,
    enc_out,
):
    tokens, part_width = hidden.shape
    head_width = query_weight.shape[1]
    blocks = counts.shape[1]
    slots_per = slot_of.shape[2]
    item_total = blocks * slots_per
    slot_total, quarter, enc_width = neighbours.shape
    block_len = tokens // blocks
    shift = block_len - 1
    n_tensor = lax.axis_size("tensor")
    n_dp = lax.axis_size("dp")
    here = lax.axis_index("tensor")
    row = lax.axis_index("dp")
    all_width = head_width * n_tensor
    rows = slots_per * quarter * n_tensor
    enc_rows = enc_width // ENC_HEAD_DIM * block_len
    head_rows = head_width // HEAD_DIM * block_len
    sds = jax.ShapeDtypeStruct

    seq_counts = counts[0]
    count = lax.dynamic_slice_in_dim(seq_counts, here, 1, 0)
    scalars = jnp.concatenate([here.astype(jnp.int32)[None], count])

    wq_part = lax.dynamic_slice_in_dim(
        query_weight.reshape(n_tensor, part_width, head_width), row * SLICE, SLICE, 1
    )
    wo_part = lax.dynamic_slice_in_dim(out_weight, row * (SLICE // 2), SLICE // 2, 0)
    wo_part = wo_part.reshape(SLICE // 2, n_tensor, 2, head_width).transpose(1, 2, 0, 3)
    wo_part = wo_part.reshape(n_tensor, SLICE, head_width)
    kv_part = jnp.concatenate(
        [
            lax.dynamic_slice_in_dim(key_weight, row * SLICE, SLICE, 0),
            lax.dynamic_slice_in_dim(value_weight, row * SLICE, SLICE, 0),
        ],
        axis=0,
    )
    kv_part = jnp.broadcast_to(kv_part[None], (n_tensor, 2 * SLICE, head_width))
    weight_parts = exchange(jnp.concatenate([kv_part, wq_part, wo_part], axis=1), here)
    kv_parts = jnp.stack([part[: 2 * SLICE] for part in weight_parts])
    qo_parts = jnp.stack([part[2 * SLICE :] for part in weight_parts])
    hidden_parts = spread(hidden, n_tensor)
    cot_parts = spread(cotangent, n_tensor)
    near = (hidden_parts[1], hidden_parts[3])
    kv_all = lax.all_gather(after(kv_parts, near), "dp", axis=0)

    def weight_spec(index):
        return pl.BlockSpec((n_dp, 1, SLICE, head_width), lambda g, s: (0, g, index, 0))

    c_spec = whole(block_len, 2 * enc_width)
    own_cond, *to_send = call(
        cond_kernel,
        "cond",
        1,
        [whole(tokens, part_width), whole(part_width, 2 * enc_width)],
        (c_spec,) * 4,
        (sds((block_len, 2 * enc_width), BF16),) * 4,
        [pltpu.VMEM((tokens, 2 * enc_width), F32)],
        20,
    )(scalars, hidden, cond_weight)
    cond_parts = [own_cond] + [
        lax.ppermute(array, "tensor", [(i, (i - k) % n_tensor) for i in range(n_tensor)])
        for k, array in enumerate(to_send, 1)
    ]

    live = jnp.arange(slots_per)[None, :] < after(seq_counts, (hidden_parts[1:], cot_parts[1:]))[:, None]
    slot_flat = slot_of.reshape(item_total)
    matches = (jnp.arange(slot_total)[:, None] == slot_flat[None, :]) & live.reshape(item_total)[
        None, :
    ]
    returned = lax.all_to_all(neighbours, "dp", split_axis=0, concat_axis=0, tiled=True)
    items = jnp.einsum(
        "si,sre->ire", matches.astype(BF16), returned, preferred_element_type=F32
    ).astype(BF16)
    items = items.reshape(blocks, slots_per * quarter, enc_width)
    x = lax.all_to_all(items, "tensor", split_axis=0, concat_axis=0, tiled=True)
    x = x.reshape(rows, enc_width)

    def projected(parts, weight, dims, weight_block, weight_map, name, before=None):
        out = (tokens, head_width)
        if before is not None:
            out = (blocks, 2, block_len, head_width)
        return call(
            functools.partial(project_kernel, dims, shift),
            name,
            n_tensor,
            [whole(*part.shape) for part in parts]
            + [pl.BlockSpec(weight_block, weight_map)]
            + ([] if before is None else [whole(tokens, head_width)]),
            whole(*out),
            sds(out, BF16),
            [pltpu.VMEM((tokens, head_width), F32)],
            16,
        )(scalars, *parts, weight, *([] if before is None else [before]))

    query = projected(
        hidden_parts,
        query_weight,
        PLAIN,
        (part_width, head_width),
        lambda g, s: ((s[0] + g) % 4, 0),
        "query",
    )
    qo_all = lax.all_gather(after(qo_parts, items), "dp", axis=0)
    query_d_ctx = projected(
        cot_parts,
        out_weight,
        ROWS_T,
        (head_width, part_width),
        lambda g, s: (0, (s[0] + g) % 4),
        "d_ctx",
        before=query,
    )
    query_d_ctx = lax.all_to_all(
        after(query_d_ctx, (x, cond_parts[1:])), "tensor", split_axis=0, concat_axis=0, tiled=True
    )

    c_spec = whole(block_len, 2 * enc_width)
    w_spec = whole(enc_width, enc_width)
    r_spec = whole(rows, enc_width)
    p_spec = whole(enc_rows, rows)
    cond, enc_queries, enc_probs, encoded = call(
        encode_kernel,
        "encode",
        1,
        [r_spec] + [c_spec] * 4 + [w_spec] * 2,
        (c_spec, r_spec, p_spec, r_spec),
        (
            sds((block_len, 2 * enc_width), BF16),
            sds((rows, enc_width), BF16),
            sds((enc_rows, rows), F32),
            sds((rows, enc_width), BF16),
        ),
        [],
        60,
    )(scalars, x, *cond_parts, enc_query, enc_out)

    q_spec = pl.BlockSpec((1, 2, block_len, head_width), lambda g, s: ((s[0] + g) % 4, 0, 0, 0))
    both_spec = pl.BlockSpec((2, block_len, head_width), lambda g, s: (0, 0, (s[0] + g) % 4))
    probs, d_scores, both = call(
        attention_kernel,
        "attention",
        n_tensor,
        [r_spec, weight_spec(0), weight_spec(1), q_spec],
        (
            group(head_rows, rows),
            group(head_rows, rows),
            both_spec,
        ),
        (
            sds((n_tensor, head_rows, rows), BF16),
            sds((n_tensor, head_rows, rows), BF16),
            sds((2, block_len, all_width), BF16),
        ),
        [],
        60,
    )(scalars, encoded, kv_all, kv_all, query_d_ctx)
    both_parts = spread(both, n_tensor)

    d_cond = call(
        encoded_back_kernel,
        "encoded_back",
        n_tensor,
        [group(head_rows, rows), group(head_rows, rows)]
        + [q_spec, weight_spec(0), weight_spec(1), w_spec, p_spec, r_spec, c_spec],
        c_spec,
        sds((block_len, 2 * enc_width), BF16),
        [pltpu.VMEM((rows, enc_width), F32)],
        60,
    )(
        scalars,
        d_scores,
        probs,
        query_d_ctx,
        kv_all,
        kv_all,
        enc_out,
        enc_probs,
        enc_queries,
        cond,
    )
    d_cond_parts = spread(d_cond, n_tensor)

    out_spec = whole(tokens, part_width)
    acc = pltpu.VMEM((tokens, part_width), F32)
    mixed, from_query = call(
        functools.partial(outputs_kernel, shift),
        "outputs",
        n_tensor,
        [both_spec] * 4 + [weight_spec(1), weight_spec(0), out_spec, out_spec],
        (out_spec, out_spec),
        (sds((tokens, part_width), BF16), sds((tokens, part_width), F32)),
        [acc, acc],
        60,
    )(scalars, *both_parts, qo_all, qo_all, hidden, cotangent)
    grad_hidden = call(
        cond_grad_kernel,
        "cond_grad",
        1,
        [c_spec] * 4 + [whole(part_width, 2 * enc_width), out_spec],
        out_spec,
        sds((tokens, part_width), BF16),
        [],
        16,
    )(scalars, *d_cond_parts, cond_weight, from_query)
    return (mixed, grad_hidden)


def solution(mesh):
    placed = (
        P("dp", "tensor"),
        P("dp", "tensor"),
        P("dp", None),
        P("dp", None, None),
        P("dp", "tensor", None),
        P(None, "tensor"),
        P(None, "tensor"),
        P(None, "tensor"),
        P("tensor", None),
        P("tensor", None),
        P(),
        P(),
    )
    return jax.shard_map(
        shards,
        mesh=mesh,
        in_specs=placed,
        out_specs=(P("dp", "tensor"), P("dp", "tensor")),
        check_vma=False,
    )
```

profile of v0, /device:TPU:10, one launch (start us, length us, event | category | flops | bytes accessed | tf_op | source)
XLA Modules:
  0.0 191.6 jit_solution(2536090599911908383)
XLA Ops:
  10.2 4.1 %collective-permute-start.9 = (bf16[128,512]{1,0:T(8,128)(2,1)S(1)}, bf16[128,512]{1,0:T(8,128)(2,1)S(1)}, u32[]{:S(2)}, u32[]{:S(2)}) collective-permute-start(bf16[128,512]{1,0:T(8,128)(2,1)S(1)} %get-tuple-element.38), channel_id=1, source_target_pairs={{0,3},{1,0},{2,1},{3,2},{4,7},{5,4},{6,5},{7,6},{8,11},{9,8},{10,9... | collective-permute-start | bytes 393224 | tf_op jit(solution)/shard_map/ppermute | solution.py:58
  16.4 2.5 %collective-permute-start.11 = (bf16[128,512]{1,0:T(8,128)(2,1)S(1)}, bf16[128,512]{1,0:T(8,128)(2,1)S(1)}, u32[]{:S(2)}, u32[]{:S(2)}) collective-permute-start(bf16[128,512]{1,0:T(8,128)(2,1)S(1)} %get-tuple-element.39), channel_id=1, source_target_pairs={{0,1},{1,2},{2,3},{3,0},{4,5},{5,6},{6,7},{7,4},{8,9},{9,10},{10,1... | collective-permute-start | bytes 393224 | tf_op jit(solution)/shard_map/ppermute | solution.py:58
  18.9 13.1 %collective-permute-done.10 = bf16[128,512]{1,0:T(8,128)(2,1)S(1)} collective-permute-done((bf16[128,512]{1,0:T(8,128)(2,1)S(1)}, bf16[128,512]{1,0:T(8,128)(2,1)S(1)}, u32[]{:S(2)}, u32[]{:S(2)}) %collective-permute-start.10) | collective-permute-done | bytes 131104 | tf_op jit(solution)/shard_map/ppermute | solution.py:58
  32.0 2.7 %collective-permute-done.11 = bf16[128,512]{1,0:T(8,128)(2,1)S(1)} collective-permute-done((bf16[128,512]{1,0:T(8,128)(2,1)S(1)}, bf16[128,512]{1,0:T(8,128)(2,1)S(1)}, u32[]{:S(2)}, u32[]{:S(2)}) %collective-permute-start.11) | collective-permute-done | bytes 131104 | tf_op jit(solution)/shard_map/ppermute | solution.py:58
  36.3 7.7 %all-to-all-start = ((bf16[32,32,896]{2,1,0:T(8,128)(2,1)}), bf16[32,32,896]{2,1,0:T(8,128)(2,1)}, u32[]{:S(2)}, u32[]{:S(2)}) async-start(bf16[32,32,896]{2,1,0:T(8,128)(2,1)} %param.16), calls=%async_computation | async-start | bytes 3670016 | tf_op jit(solution)/shard_map/all_to_all | solution.py:384
  44.9 2.3 %collective-permute-start.3 = (bf16[256,1024]{1,0:T(8,128)(2,1)S(1)}, bf16[256,1024]{1,0:T(8,128)(2,1)S(1)}, u32[]{:S(2)}, u32[]{:S(2)}) collective-permute-start(bf16[256,1024]{1,0:T(8,128)(2,1)S(1)} %copy-done.5), channel_id=1, source_target_pairs={{0,3},{1,0},{2,1},{3,2},{4,7},{5,4},{6,5},{7,6},{8,11},{9,8},{10,9... | collective-permute-start | bytes 1572872 | tf_op jit(solution)/shard_map/ppermute | solution.py:64
  49.9 10.7 %collective-permute-done.1.p2 = bf16[256,1024]{1,0:T(8,128)(2,1)} collective-permute-done((bf16[256,1024]{1,0:T(8,128)(2,1)S(1)}, bf16[256,1024]{1,0:T(8,128)(2,1)}, u32[]{:S(2)}, u32[]{:S(2)}) %collective-permute-start.1) | collective-permute-done | bytes 524320 | tf_op jit(solution)/shard_map/ppermute | solution.py:64
  60.6 7.9 %collective-permute-done.3.p1 = bf16[256,1024]{1,0:T(8,128)(2,1)S(1)} collective-permute-done((bf16[256,1024]{1,0:T(8,128)(2,1)S(1)}, bf16[256,1024]{1,0:T(8,128)(2,1)S(1)}, u32[]{:S(2)}, u32[]{:S(2)}) %collective-permute-start.3) | collective-permute-done | bytes 524320 | tf_op jit(solution)/shard_map/ppermute | solution.py:64
  68.5 3.1 %collective-permute-done.4.p2 = bf16[256,1024]{1,0:T(8,128)(2,1)S(1)} collective-permute-done((bf16[256,1024]{1,0:T(8,128)(2,1)S(1)}, bf16[256,1024]{1,0:T(8,128)(2,1)S(1)}, u32[]{:S(2)}, u32[]{:S(2)}) %collective-permute-start.4) | collective-permute-done | bytes 524320 | tf_op jit(solution)/shard_map/ppermute | solution.py:64
  71.7 10.4 %collective-permute-done.5.p3 = bf16[256,1024]{1,0:T(8,128)(2,1)S(1)} collective-permute-done((bf16[256,1024]{1,0:T(8,128)(2,1)S(1)}, bf16[256,1024]{1,0:T(8,128)(2,1)S(1)}, u32[]{:S(2)}, u32[]{:S(2)}) %collective-permute-start.5) | collective-permute-done | bytes 524320 | tf_op jit(solution)/shard_map/ppermute | solution.py:64
  82.2 2.2 %fusion.2 = bf16[16,32,896]{2,0,1:T(8,128)(2,1)S(1)} fusion(bf16[32,32,896]{2,1,0:T(8,128)(2,1)} %all-to-all-done, s32[16]{0:T(128)S(1)} %eq.20, pred[16]{0:T(512)(128)(4,1)S(1)} %lt.60), kind=kOutput, calls=%fused_computation.2 | convolution fusion | flops 29819904 | bytes 2752592 | tf_op jit(solution)/shard_map/si,sre->ire/dot_general | solution.py:385
  85.6 4.2 %all-to-all-start.1 = ((bf16[4,128,896]{2,1,0:T(8,128)(2,1)}), bf16[4,128,896]{2,1,0:T(8,128)(2,1)}, u32[]{:S(2)}, u32[]{:S(2)}) async-start(bf16[4,128,896]{2,1,0:T(8,128)(2,1)} %bitcast.38), calls=%async_computation.1 | async-start | bytes 1835008 | tf_op jit(solution)/shard_map/all_to_all | solution.py:389
  95.9 3.1 %collective-permute-start.6 = (bf16[64,1792]{1,0:T(8,128)(2,1)S(1)}, bf16[64,1792]{1,0:T(8,128)(2,1)S(1)}, u32[]{:S(2)}, u32[]{:S(2)}) collective-permute-start(bf16[64,1792]{1,0:T(8,128)(2,1)S(1)} %get-tuple-element.21), channel_id=1, source_target_pairs={{0,3},{1,0},{2,1},{3,2},{4,7},{5,4},{6,5},{7,6},{8,11},{9,8},{10,9... | collective-permute-start | bytes 688136 | tf_op jit(solution)/shard_map/ppermute | solution.py:375
  102.2 3.5 %query.1.rest_0_ = bf16[256,512]{1,0:T(8,128)(2,1)S(1)} custom-call(s32[2]{0:T(128)S(1)} %pad_add_fusion.s_ref, bf16[256,1024]{1,0:T(8,128)(2,1)S(1)} %copy-done.2, bf16[256,1024]{1,0:T(8,128)(2,1)S(1)} %collective-permute-done.p1, bf16[256,1024]{1,0:T(8,128)(2,1)} %collective-permute-done.1.p2, bf16[256,1024]{1,0:T(8,128)(2,1)S(1)} %copy-done.9, ...), custom_call_target="tpu_custom_call" | custom-call | tf_op jit(solution)/shard_map/query/pallas_call | solution.py:396
  105.7 3.7 %d_ctx.1 = bf16[4,2,64,512]{3,2,1,0:T(8,128)(2,1)} custom-call(s32[2]{0:T(128)S(1)} %pad_add_fusion.s_ref, bf16[256,1024]{1,0:T(8,128)(2,1)S(1)} %copy-done.5, bf16[256,1024]{1,0:T(8,128)(2,1)S(1)} %collective-permute-done.3.p1, bf16[256,1024]{1,0:T(8,128)(2,1)S(1)} %collective-permute-done.4.p2, bf16[256,1024]{1,0:T(8,128)(2,1)S(1)} %collective-permute-done.5.p3, ...), custom_call_target="tpu_custom_call" | custom-call | tf_op jit(solution)/shard_map/d_ctx/pallas_call | solution.py:396
  110.5 3.5 %collective-permute-done.8.c3 = bf16[64,1792]{1,0:T(8,128)(2,1)} collective-permute-done((bf16[64,1792]{1,0:T(8,128)(2,1)S(1)}, bf16[64,1792]{1,0:T(8,128)(2,1)}, u32[]{:S(2)}, u32[]{:S(2)}) %collective-permute-start.8) | collective-permute-done | bytes 229408 | tf_op jit(solution)/shard_map/ppermute | solution.py:375
  114.0 3.7 %all-to-all-start.2 = ((bf16[4,2,64,512]{3,2,1,0:T(8,128)(2,1)}), bf16[4,2,64,512]{3,2,1,0:T(8,128)(2,1)S(1)}, u32[]{:S(2)}, u32[]{:S(2)}) async-start(bf16[4,2,64,512]{3,2,1,0:T(8,128)(2,1)} %d_ctx.1), calls=%async_computation.2 | async-start | bytes 1048576 | tf_op jit(solution)/shard_map/all_to_all | solution.py:427
  117.7 7.6 %encode.1 = (bf16[64,1792]{1,0:T(8,128)(2,1)}, bf16[512,896]{1,0:T(8,128)(2,1)}, f32[448,512]{1,0:T(8,128)}, bf16[512,896]{1,0:T(8,128)(2,1)}) custom-call(s32[2]{0:T(128)} %copy-done.11, bf16[512,896]{1,0:T(8,128)(2,1)} %bitcast.5.x_ref, bf16[64,1792]{1,0:T(8,128)(2,1)} %copy-done.10, bf16[64,1792]{1,0:T(8,128)(2,1)} %copy-done.14, ...), custom_call_target="tpu_custom_call" | custom-call | tf_op jit(solution)/shard_map/encode/pallas_call | solution.py:435
  128.2 11.9 %attention.1 = (bf16[4,256,512]{2,1,0:T(8,128)(2,1)}, bf16[4,256,512]{2,1,0:T(8,128)(2,1)}, bf16[2,64,2048]{2,1,0:T(8,128)(2,1)}) custom-call(s32[2]{0:T(128)} %copy-done.11, bf16[512,896]{1,0:T(8,128)(2,1)} %get-tuple-element.24.encoded_ref, bf16[32,4,64,512]{3,2,1,0:T(8,128)(2,1)} %bitcast.32, bf16[32,4,64,512]{3,2,1,0:T(8,128)(2,1)} %bitcast.33, ...), custom_call_target="tpu_custom_call" | custom-call | tf_op jit(solution)/shard_map/attention/pallas_call | solution.py:453
  142.7 14.3 %encoded_back.1.c0 = bf16[64,1792]{1,0:T(8,128)(2,1)} custom-call(s32[2]{0:T(128)} %copy-done.11, bf16[4,256,512]{2,1,0:T(8,128)(2,1)} %get-tuple-element.30.d_scores_ref, bf16[4,256,512]{2,1,0:T(8,128)(2,1)} %get-tuple-element.31.probs_ref, bf16[4,2,64,512]{3,2,1,0:T(8,128)(2,1)} %copy-done.13, bf16[32,4,64,512]{3,2,1,0:T(8,128)(2,1)} %bitcast.34, ...), custom_call_target="tpu_custom_call" | custom-call | tf_op jit(solution)/shard_map/encoded_back/pallas_call | solution.py:473
  157.0 3.2 %collective-permute-start.15 = (bf16[64,1792]{1,0:T(8,128)(2,1)}, bf16[64,1792]{1,0:T(8,128)(2,1)S(1)}, u32[]{:S(2)}, u32[]{:S(2)}) collective-permute-start(bf16[64,1792]{1,0:T(8,128)(2,1)} %encoded_back.1.c0), channel_id=1, source_target_pairs={{0,3},{1,0},{2,1},{3,2},{4,7},{5,4},{6,5},{7,6},{8,11},{9,8},{10,9... | collective-permute-start | bytes 688136 | tf_op jit(solution)/shard_map/ppermute | solution.py:64
  161.9 7.4 %collective-permute-done.14.c3 = bf16[2,64,2048]{2,1,0:T(8,128)(2,1)} collective-permute-done((bf16[2,64,2048]{2,1,0:T(8,128)(2,1)}, bf16[2,64,2048]{2,1,0:T(8,128)(2,1)}, u32[]{:S(2)}, u32[]{:S(2)}) %collective-permute-start.14) | collective-permute-done | bytes 524320 | tf_op jit(solution)/shard_map/ppermute | solution.py:64
  169.3 9.8 %outputs.1 = (bf16[256,1024]{1,0:T(8,128)(2,1)}, f32[256,1024]{1,0:T(8,128)}) custom-call(s32[2]{0:T(128)} %copy-done.11, bf16[2,64,2048]{2,1,0:T(8,128)(2,1)} %get-tuple-element.27.c0, bf16[2,64,2048]{2,1,0:T(8,128)(2,1)} %collective-permute-done.12.c1, bf16[2,64,2048]{2,1,0:T(8,128)(2,1)} %collective-permute-done.13.c2, ...), custom_call_target="tpu_custom_call" | custom-call | tf_op jit(solution)/shard_map/outputs/pallas_call | solution.py:499
  181.0 3.8 %cond_grad.1 = bf16[256,1024]{1,0:T(8,128)(2,1)} custom-call(s32[2]{0:T(128)S(1)} %copy-done.12, bf16[64,1792]{1,0:T(8,128)(2,1)S(1)} %copy-done.7, bf16[64,1792]{1,0:T(8,128)(2,1)S(1)} %collective-permute-done.15.c1, bf16[64,1792]{1,0:T(8,128)(2,1)} %collective-permute-done.16.c2, bf16[64,1792]{1,0:T(8,128)(2,1)} %collective-permute-done.17.c3, ...), custom_call_target="tpu_custom_call" | custom-call | tf_op jit(solution)/shard_map/cond_grad/pallas_call | solution.py:509
  (90 shorter events, 30.9 us)
Async XLA Ops:
  7.2 120.2 %all-gather.5.cloned.1.call-start = ((), (), s32[]{:S(2)}) async-start(), calls=%async_computation.3 | async-start | bytes 8650752 | tf_op jit(solution)/shard_map/all_gather | solution.py:358
  10.2 8.6 %collective-permute-start.9 = (bf16[128,512]{1,0:T(8,128)(2,1)S(1)}, bf16[128,512]{1,0:T(8,128)(2,1)S(1)}, u32[]{:S(2)}, u32[]{:S(2)}) collective-permute-start(bf16[128,512]{1,0:T(8,128)(2,1)S(1)} %get-tuple-element.38), channel_id=1, source_target_pairs={{0,3},{1,0},{2,1},{3,2},{4,7},{5,4},{6,5},{7,6},{8,11},{9,8},{10,9... | collective-permute-start | bytes 393224 | tf_op jit(solution)/shard_map/ppermute | solution.py:58
  14.3 21.1 %collective-permute-start = (bf16[256,1024]{1,0:T(8,128)(2,1)S(1)}, bf16[256,1024]{1,0:T(8,128)(2,1)S(1)}, u32[]{:S(2)}, u32[]{:S(2)}) collective-permute-start(bf16[256,1024]{1,0:T(8,128)(2,1)S(1)} %copy-done.2), channel_id=1, source_target_pairs={{0,3},{1,0},{2,1},{3,2},{4,7},{5,4},{6,5},{7,6},{8,11},{9,8},{10,9... | collective-permute-start | bytes 1572872 | tf_op jit(solution)/shard_map/ppermute | solution.py:64
  14.7 20.7 %collective-permute-start.2 = (bf16[256,1024]{1,0:T(8,128)(2,1)S(1)}, bf16[256,1024]{1,0:T(8,128)(2,1)S(1)}, u32[]{:S(2)}, u32[]{:S(2)}) collective-permute-start(bf16[256,1024]{1,0:T(8,128)(2,1)S(1)} %copy-done.2), channel_id=1, source_target_pairs={{0,1},{1,2},{2,3},{3,0},{4,5},{5,6},{6,7},{7,4},{8,9},{9,10},{10,1... | collective-permute-start | bytes 1572872 | tf_op jit(solution)/shard_map/ppermute | solution.py:64
  16.4 15.6 %collective-permute-start.10 = (bf16[128,512]{1,0:T(8,128)(2,1)S(1)}, bf16[128,512]{1,0:T(8,128)(2,1)S(1)}, u32[]{:S(2)}, u32[]{:S(2)}) collective-permute-start(bf16[128,512]{1,0:T(8,128)(2,1)S(1)} %get-tuple-element.40), channel_id=1, source_target_pairs={{0,2},{1,3},{2,0},{3,1},{4,6},{5,7},{6,4},{7,5},{8,10},{9,11},{10,... | collective-permute-start | bytes 393224 | tf_op jit(solution)/shard_map/ppermute | solution.py:58
  16.4 18.3 %collective-permute-start.11 = (bf16[128,512]{1,0:T(8,128)(2,1)S(1)}, bf16[128,512]{1,0:T(8,128)(2,1)S(1)}, u32[]{:S(2)}, u32[]{:S(2)}) collective-permute-start(bf16[128,512]{1,0:T(8,128)(2,1)S(1)} %get-tuple-element.39), channel_id=1, source_target_pairs={{0,1},{1,2},{2,3},{3,0},{4,5},{5,6},{6,7},{7,4},{8,9},{9,10},{10,1... | collective-permute-start | bytes 393224 | tf_op jit(solution)/shard_map/ppermute | solution.py:58
  36.3 45.8 %copy-start.17 = (s32[1,4]{1,0:T(1,128)S(1)}, s32[1,4]{1,0:T(1,128)}, u32[]{:S(2)}) copy-start(s32[1,4]{1,0:T(1,128)} %param.14) | copy-start | bytes 52
  36.3 46.0 %all-to-all-start = ((bf16[32,32,896]{2,1,0:T(8,128)(2,1)}), bf16[32,32,896]{2,1,0:T(8,128)(2,1)}, u32[]{:S(2)}, u32[]{:S(2)}) async-start(bf16[32,32,896]{2,1,0:T(8,128)(2,1)} %param.16), calls=%async_computation | async-start | bytes 3670016 | tf_op jit(solution)/shard_map/all_to_all | solution.py:384
  44.0 125.3 %all-gather.7.cloned.1.call-start = ((), (), s32[]{:S(2)}) async-start(), calls=%async_computation.4 | async-start | bytes 8650752 | tf_op jit(solution)/shard_map/all_gather | solution.py:417
  44.0 16.6 %collective-permute-start.1 = (bf16[256,1024]{1,0:T(8,128)(2,1)S(1)}, bf16[256,1024]{1,0:T(8,128)(2,1)}, u32[]{:S(2)}, u32[]{:S(2)}) collective-permute-start(bf16[256,1024]{1,0:T(8,128)(2,1)S(1)} %copy-done.2), channel_id=1, source_target_pairs={{0,2},{1,3},{2,0},{3,1},{4,6},{5,7},{6,4},{7,5},{8,10},{9,11},{10,... | collective-permute-start | bytes 1572872 | tf_op jit(solution)/shard_map/ppermute | solution.py:64
  44.9 23.7 %collective-permute-start.3 = (bf16[256,1024]{1,0:T(8,128)(2,1)S(1)}, bf16[256,1024]{1,0:T(8,128)(2,1)S(1)}, u32[]{:S(2)}, u32[]{:S(2)}) collective-permute-start(bf16[256,1024]{1,0:T(8,128)(2,1)S(1)} %copy-done.5), channel_id=1, source_target_pairs={{0,3},{1,0},{2,1},{3,2},{4,7},{5,4},{6,5},{7,6},{8,11},{9,8},{10,9... | collective-permute-start | bytes 1572872 | tf_op jit(solution)/shard_map/ppermute | solution.py:64
  47.2 24.5 %collective-permute-start.4 = (bf16[256,1024]{1,0:T(8,128)(2,1)S(1)}, bf16[256,1024]{1,0:T(8,128)(2,1)S(1)}, u32[]{:S(2)}, u32[]{:S(2)}) collective-permute-start(bf16[256,1024]{1,0:T(8,128)(2,1)S(1)} %copy-done.5), channel_id=1, source_target_pairs={{0,2},{1,3},{2,0},{3,1},{4,6},{5,7},{6,4},{7,5},{8,10},{9,11},{10,... | collective-permute-start | bytes 1572872 | tf_op jit(solution)/shard_map/ppermute | solution.py:64
  47.7 34.4 %collective-permute-start.5 = (bf16[256,1024]{1,0:T(8,128)(2,1)S(1)}, bf16[256,1024]{1,0:T(8,128)(2,1)S(1)}, u32[]{:S(2)}, u32[]{:S(2)}) collective-permute-start(bf16[256,1024]{1,0:T(8,128)(2,1)S(1)} %copy-done.5), channel_id=1, source_target_pairs={{0,1},{1,2},{2,3},{3,0},{4,5},{5,6},{6,7},{7,4},{8,9},{9,10},{10,1... | collective-permute-start | bytes 1572872 | tf_op jit(solution)/shard_map/ppermute | solution.py:64
  85.6 28.4 %all-to-all-start.1 = ((bf16[4,128,896]{2,1,0:T(8,128)(2,1)}), bf16[4,128,896]{2,1,0:T(8,128)(2,1)}, u32[]{:S(2)}, u32[]{:S(2)}) async-start(bf16[4,128,896]{2,1,0:T(8,128)(2,1)} %bitcast.38), calls=%async_computation.1 | async-start | bytes 1835008 | tf_op jit(solution)/shard_map/all_to_all | solution.py:389
  95.9 13.5 %collective-permute-start.6 = (bf16[64,1792]{1,0:T(8,128)(2,1)S(1)}, bf16[64,1792]{1,0:T(8,128)(2,1)S(1)}, u32[]{:S(2)}, u32[]{:S(2)}) collective-permute-start(bf16[64,1792]{1,0:T(8,128)(2,1)S(1)} %get-tuple-element.21), channel_id=1, source_target_pairs={{0,3},{1,0},{2,1},{3,2},{4,7},{5,4},{6,5},{7,6},{8,11},{9,8},{10,9... | collective-permute-start | bytes 688136 | tf_op jit(solution)/shard_map/ppermute | solution.py:375
  99.0 10.9 %collective-permute-start.7 = (bf16[64,1792]{1,0:T(8,128)(2,1)S(1)}, bf16[64,1792]{1,0:T(8,128)(2,1)S(1)}, u32[]{:S(2)}, u32[]{:S(2)}) collective-permute-start(bf16[64,1792]{1,0:T(8,128)(2,1)S(1)} %get-tuple-element.22), channel_id=1, source_target_pairs={{0,2},{1,3},{2,0},{3,1},{4,6},{5,7},{6,4},{7,5},{8,10},{9,11},{10,... | collective-permute-start | bytes 688136 | tf_op jit(solution)/shard_map/ppermute | solution.py:375
  99.9 14.1 %collective-permute-start.8 = (bf16[64,1792]{1,0:T(8,128)(2,1)S(1)}, bf16[64,1792]{1,0:T(8,128)(2,1)}, u32[]{:S(2)}, u32[]{:S(2)}) collective-permute-start(bf16[64,1792]{1,0:T(8,128)(2,1)S(1)} %get-tuple-element.23), channel_id=1, source_target_pairs={{0,1},{1,2},{2,3},{3,0},{4,5},{5,6},{6,7},{7,4},{8,9},{9,10},{10,1... | collective-permute-start | bytes 688136 | tf_op jit(solution)/shard_map/ppermute | solution.py:375
  114.0 13.4 %all-to-all-start.2 = ((bf16[4,2,64,512]{3,2,1,0:T(8,128)(2,1)}), bf16[4,2,64,512]{3,2,1,0:T(8,128)(2,1)S(1)}, u32[]{:S(2)}, u32[]{:S(2)}) async-start(bf16[4,2,64,512]{3,2,1,0:T(8,128)(2,1)} %d_ctx.1), calls=%async_computation.2 | async-start | bytes 1048576 | tf_op jit(solution)/shard_map/all_to_all | solution.py:427
  140.1 21.0 %collective-permute-start.12 = (bf16[2,64,2048]{2,1,0:T(8,128)(2,1)}, bf16[2,64,2048]{2,1,0:T(8,128)(2,1)}, u32[]{:S(2)}, u32[]{:S(2)}) collective-permute-start(bf16[2,64,2048]{2,1,0:T(8,128)(2,1)} %get-tuple-element.27.c0), channel_id=1, source_target_pairs={{0,3},{1,0},{2,1},{3,2},{4,7},{5,4},{6,5},{7,6},{8,11},{9,8},{10,9... | collective-permute-start | bytes 1572872 | tf_op jit(solution)/shard_map/ppermute | solution.py:64
  141.3 20.6 %collective-permute-start.13 = (bf16[2,64,2048]{2,1,0:T(8,128)(2,1)}, bf16[2,64,2048]{2,1,0:T(8,128)(2,1)}, u32[]{:S(2)}, u32[]{:S(2)}) collective-permute-start(bf16[2,64,2048]{2,1,0:T(8,128)(2,1)} %get-tuple-element.27.c0), channel_id=1, source_target_pairs={{0,2},{1,3},{2,0},{3,1},{4,6},{5,7},{6,4},{7,5},{8,10},{9,11},{10,... | collective-permute-start | bytes 1572872 | tf_op jit(solution)/shard_map/ppermute | solution.py:64
  142.7 26.6 %collective-permute-start.14 = (bf16[2,64,2048]{2,1,0:T(8,128)(2,1)}, bf16[2,64,2048]{2,1,0:T(8,128)(2,1)}, u32[]{:S(2)}, u32[]{:S(2)}) collective-permute-start(bf16[2,64,2048]{2,1,0:T(8,128)(2,1)} %get-tuple-element.27.c0), channel_id=1, source_target_pairs={{0,1},{1,2},{2,3},{3,0},{4,5},{5,6},{6,7},{7,4},{8,9},{9,10},{10,1... | collective-permute-start | bytes 1572872 | tf_op jit(solution)/shard_map/ppermute | solution.py:64
  157.0 22.1 %collective-permute-start.15 = (bf16[64,1792]{1,0:T(8,128)(2,1)}, bf16[64,1792]{1,0:T(8,128)(2,1)S(1)}, u32[]{:S(2)}, u32[]{:S(2)}) collective-permute-start(bf16[64,1792]{1,0:T(8,128)(2,1)} %encoded_back.1.c0), channel_id=1, source_target_pairs={{0,3},{1,0},{2,1},{3,2},{4,7},{5,4},{6,5},{7,6},{8,11},{9,8},{10,9... | collective-permute-start | bytes 688136 | tf_op jit(solution)/shard_map/ppermute | solution.py:64
  160.2 18.9 %collective-permute-start.16 = (bf16[64,1792]{1,0:T(8,128)(2,1)}, bf16[64,1792]{1,0:T(8,128)(2,1)}, u32[]{:S(2)}, u32[]{:S(2)}) collective-permute-start(bf16[64,1792]{1,0:T(8,128)(2,1)} %encoded_back.1.c0), channel_id=1, source_target_pairs={{0,2},{1,3},{2,0},{3,1},{4,6},{5,7},{6,4},{7,5},{8,10},{9,11},{10,... | collective-permute-start | bytes 688136 | tf_op jit(solution)/shard_map/ppermute | solution.py:64
  161.1 18.0 %collective-permute-start.17 = (bf16[64,1792]{1,0:T(8,128)(2,1)}, bf16[64,1792]{1,0:T(8,128)(2,1)}, u32[]{:S(2)}, u32[]{:S(2)}) collective-permute-start(bf16[64,1792]{1,0:T(8,128)(2,1)} %encoded_back.1.c0), channel_id=1, source_target_pairs={{0,1},{1,2},{2,3},{3,0},{4,5},{5,6},{6,7},{7,4},{8,9},{9,10},{10,1... | collective-permute-start | bytes 688136 | tf_op jit(solution)/shard_map/ppermute | solution.py:64
  (17 other events, 90.4 us)
Sparse Core Ops, SparseCore 0:
  36.4 62.9 all-gather.4
  101.6 52.3 all-gather.6
where the time goes:
time: 193 us; the launch traced here: 192 us
  waiting for transfers between devices  61.5 us (32%)
  Pallas kernels  56.2 us (29%)
  starting transfers between devices  41.7 us (22%)
  between operations  14.4 us (7%)
  local copies, waits for them, and re-layouts  13.3 us (7%)
  other arithmetic  2.29 us (1%)
  matrix products  2.24 us (1%)
    ppermute x12, waiting for transfers between devices, spread(): lax.ppermute(shard, axis, [(i, (i - k) % size) for i in range(size)])  39.6 us
    ppermute x3, waiting for transfers between devices, exchange(): lax.ppermute(piece, axis, [(i, (i - k) % size) for i in range(size)])  15.8 us
    ppermute x12, starting transfers between devices, spread(): lax.ppermute(shard, axis, [(i, (i - k) % size) for i in range(size)])  14.6 us
    pallas_call x1, Pallas kernels, shards(): call(encoded_back_kernel, 'encoded_back', n_tensor, [group(head_rows, row...  14.3 us
    pallas_call x1, Pallas kernels, shards(): call(attention_kernel, 'attention', n_tensor, [r_spec, weight_spec(0), we...  11.9 us
    pallas_call x1, Pallas kernels, shards(): call(functools.partial(outputs_kernel, shift), 'outputs', n_tensor, [both...  9.76 us
    unnamed x36, local copies, waits for them, and re-layouts  8.48 us
    all_to_all x1, starting transfers between devices, shards(): lax.all_to_all(neighbours, 'dp', split_axis=0, concat_axis=0, tiled=True)  7.7 us
  transfers between devices with their start and end apart: 23, of which 10 were waited for; matrix products, arithmetic and copies ran while one was open for 3% of the time, Pallas kernels for 27%

commit v1 on v0

--- a/solution.py
+++ b/solution.py
@@ -160,23 +160,38 @@
     encoded_ref[...] = (x.astype(F32) + mixing).astype(BF16)
 
 
+def pick(refs, query_ref, d_ctx_ref):
+    for k, ref in enumerate(refs):
+
+        @pl.when(pl.program_id(0) == k)
+        def _(ref=ref):
+            query_ref[...] = by_heads(ref[0], HEAD_DIM)
+            d_ctx_ref[...] = by_heads(ref[1], HEAD_DIM)
+
+
 def attention_kernel(
     s_ref,
     encoded_ref,
     key_w_ref,
     val_w_ref,
-    query_ref,
+    q0,
+    q1,
+    q2,
+    q3,
     probs_ref,
     d_scores_ref,
     out_ref,
+    query_ref,
+    d_ctx_ref,
 ):
     width = encoded_ref.shape[1]
     length = out_ref.shape[1]
+    pick((q0, q1, q2, q3), query_ref, d_ctx_ref)
     encoded = encoded_ref[...]
     keys = dot(encoded, key_w_ref[...].reshape(-1, key_w_ref.shape[3])[:width]).astype(BF16)
     vals = dot(encoded, val_w_ref[...].reshape(-1, val_w_ref.shape[3])[:width]).astype(BF16)
     count = s_ref[1]
-    scores = dot(by_heads(query_ref[0, 0], HEAD_DIM), keys, ROWS_T) * SCALING
+    scores = dot(query_ref[...], keys, ROWS_T) * SCALING
     expd = jnp.where(live_columns(count, scores.shape), jnp.exp(scores), 0.0)
     totals = jnp.sum(expd, axis=1, keepdims=True)
     probs = expd / jnp.where(count > 0, totals, 1.0)
@@ -184,7 +199,7 @@
     probs_ref[0] = probs_low
     ctx = head_blocks(dot(probs_low, vals), length, HEAD_DIM)
     out_ref[0] = jnp.concatenate(ctx, axis=1).astype(BF16)
-    weighted = probs * dot(by_heads(query_ref[0, 1], HEAD_DIM), vals, ROWS_T)
+    weighted = probs * dot(d_ctx_ref[...], vals, ROWS_T)
     d_scores = (weighted - probs * jnp.sum(weighted, axis=1, keepdims=True)) * SCALING
     d_scores = d_scores.astype(BF16)
     d_scores_ref[0] = d_scores
@@ -196,7 +211,10 @@
     s_ref,
     d_scores_ref,
     probs_ref,
-    query_ref,
+    q0,
+    q1,
+    q2,
+    q3,
     key_w_ref,
     val_w_ref,
     enc_out_ref,
@@ -204,12 +222,15 @@
     enc_queries_ref,
     cond_ref,
     d_cond_ref,
+    query_ref,
+    d_ctx_ref,
     total_ref,
 ):
     step = pl.program_id(0)
     width = total_ref.shape[1]
-    d_keys = dot(d_scores_ref[0], by_heads(query_ref[0, 0], HEAD_DIM), COLS_T).astype(BF16)
-    d_vals = dot(probs_ref[0], by_heads(query_ref[0, 1], HEAD_DIM), COLS_T).astype(BF16)
+    pick((q0, q1, q2, q3), query_ref, d_ctx_ref)
+    d_keys = dot(d_scores_ref[0], query_ref[...], COLS_T).astype(BF16)
+    d_vals = dot(probs_ref[0], d_ctx_ref[...], COLS_T).astype(BF16)
     term = dot(d_keys, key_w_ref[...].reshape(-1, key_w_ref.shape[3])[:width], ROWS_T)
     term = term + dot(d_vals, val_w_ref[...].reshape(-1, val_w_ref.shape[3])[:width], ROWS_T)
     term = term.astype(BF16).astype(F32)
@@ -376,19 +397,6 @@
         for k, array in enumerate(to_send, 1)
     ]
 
-    live = jnp.arange(slots_per)[None, :] < after(seq_counts, (hidden_parts[1:], cot_parts[1:]))[:, None]
-    slot_flat = slot_of.reshape(item_total)
-    matches = (jnp.arange(slot_total)[:, None] == slot_flat[None, :]) & live.reshape(item_total)[
-        None, :
-    ]
-    returned = lax.all_to_all(neighbours, "dp", split_axis=0, concat_axis=0, tiled=True)
-    items = jnp.einsum(
-        "si,sre->ire", matches.astype(BF16), returned, preferred_element_type=F32
-    ).astype(BF16)
-    items = items.reshape(blocks, slots_per * quarter, enc_width)
-    x = lax.all_to_all(items, "tensor", split_axis=0, concat_axis=0, tiled=True)
-    x = x.reshape(rows, enc_width)
-
     def projected(parts, weight, dims, weight_block, weight_map, name, before=None):
         out = (tokens, head_width)
         if before is not None:
@@ -414,9 +422,23 @@
         lambda g, s: ((s[0] + g) % 4, 0),
         "query",
     )
+
+    live = jnp.arange(slots_per)[None, :] < after(seq_counts, (query, own_cond, cot_parts[1], cot_parts[3]))[:, None]
+    slot_flat = slot_of.reshape(item_total)
+    matches = (jnp.arange(slot_total)[:, None] == slot_flat[None, :]) & live.reshape(item_total)[
+        None, :
+    ]
+    returned = lax.all_to_all(neighbours, "dp", split_axis=0, concat_axis=0, tiled=True)
+    items = jnp.einsum(
+        "si,sre->ire", matches.astype(BF16), returned, preferred_element_type=F32
+    ).astype(BF16)
+    items = items.reshape(blocks, slots_per * quarter, enc_width)
+    x = lax.all_to_all(items, "tensor", split_axis=0, concat_axis=0, tiled=True)
+    x = x.reshape(rows, enc_width)
+
     qo_all = lax.all_gather(after(qo_parts, items), "dp", axis=0)
     query_d_ctx = projected(
-        cot_parts,
+        after(tuple(cot_parts), (items, cond_parts[1:])),
         out_weight,
         ROWS_T,
         (head_width, part_width),
@@ -424,9 +446,7 @@
         "d_ctx",
         before=query,
     )
-    query_d_ctx = lax.all_to_all(
-        after(query_d_ctx, (x, cond_parts[1:])), "tensor", split_axis=0, concat_axis=0, tiled=True
-    )
+    query_parts = exchange(query_d_ctx, here)
 
     c_spec = whole(block_len, 2 * enc_width)
     w_spec = whole(enc_width, enc_width)
@@ -448,13 +468,14 @@
         60,
     )(scalars, x, *cond_parts, enc_query, enc_out)
 
-    q_spec = pl.BlockSpec((1, 2, block_len, head_width), lambda g, s: ((s[0] + g) % 4, 0, 0, 0))
+    q_spec = whole(2, block_len, head_width)
+    big = pltpu.VMEM((head_rows, head_width), BF16)
     both_spec = pl.BlockSpec((2, block_len, head_width), lambda g, s: (0, 0, (s[0] + g) % 4))
     probs, d_scores, both = call(
         attention_kernel,
         "attention",
         n_tensor,
-        [r_spec, weight_spec(0), weight_spec(1), q_spec],
+        [r_spec, weight_spec(0), weight_spec(1)] + [q_spec] * 4,
         (
             group(head_rows, rows),
             group(head_rows, rows),
@@ -465,9 +486,9 @@
             sds((n_tensor, head_rows, rows), BF16),
             sds((2, block_len, all_width), BF16),
         ),
-        [],
+        [big, big],
         60,
-    )(scalars, encoded, kv_all, kv_all, query_d_ctx)
+    )(scalars, encoded, kv_all, kv_all, *query_parts)
     both_parts = spread(both, n_tensor)
 
     d_cond = call(
@@ -475,16 +496,17 @@
         "encoded_back",
         n_tensor,
         [group(head_rows, rows), group(head_rows, rows)]
-        + [q_spec, weight_spec(0), weight_spec(1), w_spec, p_spec, r_spec, c_spec],
+        + [q_spec] * 4
+        + [weight_spec(0), weight_spec(1), w_spec, p_spec, r_spec, c_spec],
         c_spec,
         sds((block_len, 2 * enc_width), BF16),
-        [pltpu.VMEM((rows, enc_width), F32)],
+        [big, big, pltpu.VMEM((rows, enc_width), F32)],
         60,
     )(
         scalars,
         d_scores,
         probs,
-        query_d_ctx,
+        *query_parts,
         kv_all,
         kv_all,
         enc_out,

time: 193 us -> 197 us (1.021)
  local copies, waits for them, and re-layouts: 13.3 us -> 18.7 us
  waiting for transfers between devices: 61.5 us -> 58.3 us
    ppermute x12, waiting for transfers between devices: 39.6 us -> 17.6 us  [spread(): lax.ppermute(shard, axis, [(i, (i - k) % size) for i in range(size)])]
    ppermute x3, waiting for transfers between devices: 3.92 us -> 25.5 us  [shards(): lax.ppermute(array, 'tensor', [(i, (i - k) % n_tensor) for i in range(n_t...]
    all_to_all x1 -> x0, starting transfers between devices: 3.65 us -> none  [shards(): lax.all_to_all(after(query_d_ctx, (x, cond_parts[1:])), 'tensor', split_a...]
    unnamed x36 -> x54, local copies, waits for them, and re-layouts: 8.48 us -> 11.9 us
    ppermute x3 -> x6, starting transfers between devices: 6.58 us -> 9.24 us  [exchange(): lax.ppermute(piece, axis, [(i, (i - k) % size) for i in range(size)])]
    all_to_all x1 -> x0, waiting for transfers between devices: 2.14 us -> none  [shards(): lax.all_to_all(after(query_d_ctx, (x, cond_parts[1:])), 'tensor', split_a...]
    ppermute x3 -> x6, waiting for transfers between devices: 15.8 us -> 15.2 us  [exchange(): lax.ppermute(piece, axis, [(i, (i - k) % size) for i in range(size)])]
  transfers between devices with their start and end apart: 23 -> 25, of which waited for: 10 -> 10; matrix products, arithmetic and copies ran while one was open for 3% -> 4% of each run, Pallas kernels for 27% -> 27%
where the time goes in v1:
time: 197 us; the launch traced here: 194 us
  waiting for transfers between devices  58.3 us (30%)
  Pallas kernels  56.1 us (28%)
  starting transfers between devices  41.7 us (21%)
  local copies, waits for them, and re-layouts  18.7 us (9%)
  between operations  14.4 us (7%)
  other arithmetic  2.3 us (1%)
  matrix products  2.2 us (1%)
    ppermute x3, waiting for transfers between devices, shards(): lax.ppermute(array, 'tensor', [(i, (i - k) % n_tensor) for i in range(n_t...  25.5 us
    ppermute x12, waiting for transfers between devices, spread(): lax.ppermute(shard, axis, [(i, (i - k) % size) for i in range(size)])  17.6 us
    ppermute x12, starting transfers between devices, spread(): lax.ppermute(shard, axis, [(i, (i - k) % size) for i in range(size)])  15.6 us
    ppermute x6, waiting for transfers between devices, exchange(): lax.ppermute(piece, axis, [(i, (i - k) % size) for i in range(size)])  15.2 us
    pallas_call x1, Pallas kernels, shards(): call(encoded_back_kernel, 'encoded_back', n_tensor, [group(head_rows, row...  14.6 us
    pallas_call x1, Pallas kernels, shards(): call(attention_kernel, 'attention', n_tensor, [r_spec, weight_spec(0), we...  12.2 us
    unnamed x54, local copies, waits for them, and re-layouts  11.9 us
    pallas_call x1, Pallas kernels, shards(): call(functools.partial(outputs_kernel, shift), 'outputs', n_tensor, [both...  9.81 us
  transfers between devices with their start and end apart: 25, of which 10 were waited for; matrix products, arithmetic and copies ran while one was open for 4% of the time, Pallas kernels for 27%

profile of v1, /device:TPU:10, one launch (start us, length us, event | category | flops | bytes accessed | tf_op | source)
XLA Modules:
  0.0 193.7 jit_solution(2028681881500285941)
XLA Ops:
  10.2 4.1 %collective-permute-start.8 = (bf16[128,512]{1,0:T(8,128)(2,1)S(1)}, bf16[128,512]{1,0:T(8,128)(2,1)S(1)}, u32[]{:S(2)}, u32[]{:S(2)}) collective-permute-start(bf16[128,512]{1,0:T(8,128)(2,1)S(1)} %get-tuple-element.48), channel_id=1, source_target_pairs={{0,3},{1,0},{2,1},{3,2},{4,7},{5,4},{6,5},{7,6},{8,11},{9,8},{10,9... | collective-permute-start | bytes 393224 | tf_op jit(solution)/shard_map/ppermute | solution.py:58
  16.4 2.5 %collective-permute-start.10 = (bf16[128,512]{1,0:T(8,128)(2,1)S(1)}, bf16[128,512]{1,0:T(8,128)(2,1)S(1)}, u32[]{:S(2)}, u32[]{:S(2)}) collective-permute-start(bf16[128,512]{1,0:T(8,128)(2,1)S(1)} %get-tuple-element.49), channel_id=1, source_target_pairs={{0,1},{1,2},{2,3},{3,0},{4,5},{5,6},{6,7},{7,4},{8,9},{9,10},{10,1... | collective-permute-start | bytes 393224 | tf_op jit(solution)/shard_map/ppermute | solution.py:58
  18.9 13.1 %collective-permute-done.9 = bf16[128,512]{1,0:T(8,128)(2,1)S(1)} collective-permute-done((bf16[128,512]{1,0:T(8,128)(2,1)S(1)}, bf16[128,512]{1,0:T(8,128)(2,1)S(1)}, u32[]{:S(2)}, u32[]{:S(2)}) %collective-permute-start.9) | collective-permute-done | bytes 131104 | tf_op jit(solution)/shard_map/ppermute | solution.py:58
  36.1 7.7 %all-to-all-start = ((bf16[32,32,896]{2,1,0:T(8,128)(2,1)}), bf16[32,32,896]{2,1,0:T(8,128)(2,1)}, u32[]{:S(2)}, u32[]{:S(2)}) async-start(bf16[32,32,896]{2,1,0:T(8,128)(2,1)} %param.16), calls=%async_computation | async-start | bytes 3670016 | tf_op jit(solution)/shard_map/all_to_all | solution.py:431
  55.3 5.0 %collective-permute-done.1.p2 = bf16[256,1024]{1,0:T(8,128)(2,1)} collective-permute-done((bf16[256,1024]{1,0:T(8,128)(2,1)S(1)}, bf16[256,1024]{1,0:T(8,128)(2,1)}, u32[]{:S(2)}, u32[]{:S(2)}) %collective-permute-start.1) | collective-permute-done | bytes 524320 | tf_op jit(solution)/shard_map/ppermute | solution.py:64
  60.4 2.2 %copy-done.4 = bf16[4096,512]{1,0:T(8,128)(2,1)S(1)} copy-done((bf16[4096,512]{1,0:T(8,128)(2,1)S(1)}, bf16[4096,512]{1,0:T(8,128)(2,1)}, u32[]{:S(2)}) %copy-start.4) | copy-done | bytes 4194328
  62.6 3.5 %query.1.rest_0_ = bf16[256,512]{1,0:T(8,128)(2,1)S(1)} custom-call(s32[2]{0:T(128)S(1)} %pad_add_fusion.s_ref, bf16[256,1024]{1,0:T(8,128)(2,1)S(1)} %copy-done.2, bf16[256,1024]{1,0:T(8,128)(2,1)S(1)} %collective-permute-done.p1, bf16[256,1024]{1,0:T(8,128)(2,1)} %collective-permute-done.1.p2, bf16[256,1024]{1,0:T(8,128)(2,1)S(1)} %collective-permute-done.2.p3, ...), custom_call_target="tpu_custom_call" | custom-call | tf_op jit(solution)/shard_map/query/pallas_call | solution.py:404
  67.9 2.8 %collective-permute-done.4.p3 = bf16[256,1024]{1,0:T(8,128)(2,1)S(1)} collective-permute-done((bf16[256,1024]{1,0:T(8,128)(2,1)S(1)}, bf16[256,1024]{1,0:T(8,128)(2,1)S(1)}, u32[]{:S(2)}, u32[]{:S(2)}) %collective-permute-start.4) | collective-permute-done | bytes 524320 | tf_op jit(solution)/shard_map/ppermute | solution.py:64
  70.8 2.2 %fusion.2 = bf16[16,32,896]{2,0,1:T(8,128)(2,1)S(1)} fusion(bf16[32,32,896]{2,1,0:T(8,128)(2,1)} %all-to-all-done, s32[16]{0:T(128)S(1)} %eq.23, pred[16]{0:T(512)(128)(4,1)S(1)} %lt.71), kind=kOutput, calls=%fused_computation.2 | convolution fusion | flops 29819904 | bytes 2752592 | tf_op jit(solution)/shard_map/si,sre->ire/dot_general | solution.py:432
  75.6 4.2 %all-to-all-start.1 = ((bf16[4,128,896]{2,1,0:T(8,128)(2,1)}), bf16[4,128,896]{2,1,0:T(8,128)(2,1)}, u32[]{:S(2)}, u32[]{:S(2)}) async-start(bf16[4,128,896]{2,1,0:T(8,128)(2,1)} %bitcast.46), calls=%async_computation.1 | async-start | bytes 1835008 | tf_op jit(solution)/shard_map/all_to_all | solution.py:436
  79.8 3.2 %collective-permute-start.5 = (bf16[64,1792]{1,0:T(8,128)(2,1)S(1)}, bf16[64,1792]{1,0:T(8,128)(2,1)S(1)}, u32[]{:S(2)}, u32[]{:S(2)}) collective-permute-start(bf16[64,1792]{1,0:T(8,128)(2,1)S(1)} %copy-done.16), channel_id=1, source_target_pairs={{0,3},{1,0},{2,1},{3,2},{4,7},{5,4},{6,5},{7,6},{8,11},{9,8},{10,9... | collective-permute-start | bytes 688136 | tf_op jit(solution)/shard_map/ppermute | solution.py:396
  84.7 18.6 %collective-permute-done.5.c1 = bf16[64,1792]{1,0:T(8,128)(2,1)S(1)} collective-permute-done((bf16[64,1792]{1,0:T(8,128)(2,1)S(1)}, bf16[64,1792]{1,0:T(8,128)(2,1)S(1)}, u32[]{:S(2)}, u32[]{:S(2)}) %collective-permute-start.5) | collective-permute-done | bytes 229408 | tf_op jit(solution)/shard_map/ppermute | solution.py:396
  103.3 2.1 %collective-permute-done.6.c2 = bf16[64,1792]{1,0:T(8,128)(2,1)S(1)} collective-permute-done((bf16[64,1792]{1,0:T(8,128)(2,1)S(1)}, bf16[64,1792]{1,0:T(8,128)(2,1)S(1)}, u32[]{:S(2)}, u32[]{:S(2)}) %collective-permute-start.6) | collective-permute-done | bytes 229408 | tf_op jit(solution)/shard_map/ppermute | solution.py:396
  105.4 4.8 %collective-permute-done.7.c3 = bf16[64,1792]{1,0:T(8,128)(2,1)S(1)} collective-permute-done((bf16[64,1792]{1,0:T(8,128)(2,1)S(1)}, bf16[64,1792]{1,0:T(8,128)(2,1)S(1)}, u32[]{:S(2)}, u32[]{:S(2)}) %collective-permute-start.7) | collective-permute-done | bytes 229408 | tf_op jit(solution)/shard_map/ppermute | solution.py:396
  111.0 2.2 %copy-done.3 = bf16[512,4096]{1,0:T(8,128)(2,1)S(1)} copy-done((bf16[512,4096]{1,0:T(8,128)(2,1)S(1)}, bf16[512,4096]{1,0:T(8,128)(2,1)}, u32[]{:S(2)}) %copy-start.3) | copy-done | bytes 4194328
  113.2 2.9 %d_ctx.1 = bf16[4,2,64,512]{3,2,1,0:T(8,128)(2,1)S(1)} custom-call(s32[2]{0:T(128)S(1)} %pad_add_fusion.s_ref, bf16[256,1024]{1,0:T(8,128)(2,1)S(1)} %copy-done.5, bf16[256,1024]{1,0:T(8,128)(2,1)S(1)} %collective-permute-done.3.p1, bf16[256,1024]{1,0:T(8,128)(2,1)S(1)} %collective-permute-done.11.p2, bf16[256,1024]{1,0:T(8,128)(2,1)S(1)} %collective-permute-done.4.p3, ...), custom_call_target="tpu_custom_call" | custom-call | tf_op jit(solution)/shard_map/d_ctx/pallas_call | solution.py:404
  119.5 7.6 %encode.1 = (bf16[64,1792]{1,0:T(8,128)(2,1)}, bf16[512,896]{1,0:T(8,128)(2,1)}, f32[448,512]{1,0:T(8,128)}, bf16[512,896]{1,0:T(8,128)(2,1)}) custom-call(s32[2]{0:T(128)} %copy-done.9, bf16[512,896]{1,0:T(8,128)(2,1)} %bitcast.5.x_ref, bf16[64,1792]{1,0:T(8,128)(2,1)} %copy-done.8, bf16[64,1792]{1,0:T(8,128)(2,1)} %copy-done.22, ...), custom_call_target="tpu_custom_call" | custom-call | tf_op jit(solution)/shard_map/encode/pallas_call | solution.py:455
  127.9 12.2 %attention.1 = (bf16[4,256,512]{2,1,0:T(8,128)(2,1)}, bf16[4,256,512]{2,1,0:T(8,128)(2,1)}, bf16[2,64,2048]{2,1,0:T(8,128)(2,1)}) custom-call(s32[2]{0:T(128)} %copy-done.9, bf16[512,896]{1,0:T(8,128)(2,1)} %get-tuple-element.27.encoded_ref, bf16[32,4,64,512]{3,2,1,0:T(8,128)(2,1)} %bitcast.40, bf16[32,4,64,512]{3,2,1,0:T(8,128)(2,1)} %bitcast.41, ...), custom_call_target="tpu_custom_call" | custom-call | tf_op jit(solution)/shard_map/attention/pallas_call | solution.py:474
  140.1 3.3 %collective-permute-start.15 = (bf16[2,64,2048]{2,1,0:T(8,128)(2,1)}, bf16[2,64,2048]{2,1,0:T(8,128)(2,1)}, u32[]{:S(2)}, u32[]{:S(2)}) collective-permute-start(bf16[2,64,2048]{2,1,0:T(8,128)(2,1)} %get-tuple-element.33.c0), channel_id=1, source_target_pairs={{0,3},{1,0},{2,1},{3,2},{4,7},{5,4},{6,5},{7,6},{8,11},{9,8},{10,9... | collective-permute-start | bytes 1572872 | tf_op jit(solution)/shard_map/ppermute | solution.py:64
  145.0 14.6 %encoded_back.1.c0 = bf16[64,1792]{1,0:T(8,128)(2,1)} custom-call(s32[2]{0:T(128)} %copy-done.9, bf16[4,256,512]{2,1,0:T(8,128)(2,1)} %get-tuple-element.36.d_scores_ref, bf16[4,256,512]{2,1,0:T(8,128)(2,1)} %get-tuple-element.37.probs_ref, bf16[2,64,512]{2,1,0:T(8,128)(2,1)} %get-tuple-element.47.q0, bf16[2,64,512]{2,1,0:T(8,128)(2,1)} %copy-done.17, ...), custom_call_target="tpu_custom_call" | custom-call | tf_op jit(solution)/shard_map/encoded_back/pallas_call | solution.py:494
  163.4 3.2 %collective-permute-done.15.c1 = bf16[2,64,2048]{2,1,0:T(8,128)(2,1)} collective-permute-done((bf16[2,64,2048]{2,1,0:T(8,128)(2,1)}, bf16[2,64,2048]{2,1,0:T(8,128)(2,1)}, u32[]{:S(2)}, u32[]{:S(2)}) %collective-permute-start.15) | collective-permute-done | bytes 524320 | tf_op jit(solution)/shard_map/ppermute | solution.py:64
  166.7 4.6 %collective-permute-done.17.c3 = bf16[2,64,2048]{2,1,0:T(8,128)(2,1)} collective-permute-done((bf16[2,64,2048]{2,1,0:T(8,128)(2,1)}, bf16[2,64,2048]{2,1,0:T(8,128)(2,1)}, u32[]{:S(2)}, u32[]{:S(2)}) %collective-permute-start.17) | collective-permute-done | bytes 524320 | tf_op jit(solution)/shard_map/ppermute | solution.py:64
  171.3 9.8 %outputs.1 = (bf16[256,1024]{1,0:T(8,128)(2,1)}, f32[256,1024]{1,0:T(8,128)}) custom-call(s32[2]{0:T(128)} %copy-done.9, bf16[2,64,2048]{2,1,0:T(8,128)(2,1)} %get-tuple-element.33.c0, bf16[2,64,2048]{2,1,0:T(8,128)(2,1)} %collective-permute-done.15.c1, bf16[2,64,2048]{2,1,0:T(8,128)(2,1)} %collective-permute-done.16.c2, ...), custom_call_target="tpu_custom_call" | custom-call | tf_op jit(solution)/shard_map/outputs/pallas_call | solution.py:521
  183.1 3.8 %cond_grad.1 = bf16[256,1024]{1,0:T(8,128)(2,1)} custom-call(s32[2]{0:T(128)S(1)} %copy-done.10, bf16[64,1792]{1,0:T(8,128)(2,1)S(1)} %copy-done.7, bf16[64,1792]{1,0:T(8,128)(2,1)S(1)} %collective-permute-done.18.c1, bf16[64,1792]{1,0:T(8,128)(2,1)} %collective-permute-done.19.c2, bf16[64,1792]{1,0:T(8,128)(2,1)} %collective-permute-done.20.c3, ...), custom_call_target="tpu_custom_call" | custom-call | tf_op jit(solution)/shard_map/cond_grad/pallas_call | solution.py:531
  (113 shorter events, 39.0 us)
Async XLA Ops:
  7.2 120.0 %all-gather.5.cloned.1.call-start = ((), (), s32[]{:S(2)}) async-start(), calls=%async_computation.2 | async-start | bytes 8650752 | tf_op jit(solution)/shard_map/all_gather | solution.py:379
  10.2 8.6 %collective-permute-start.8 = (bf16[128,512]{1,0:T(8,128)(2,1)S(1)}, bf16[128,512]{1,0:T(8,128)(2,1)S(1)}, u32[]{:S(2)}, u32[]{:S(2)}) collective-permute-start(bf16[128,512]{1,0:T(8,128)(2,1)S(1)} %get-tuple-element.48), channel_id=1, source_target_pairs={{0,3},{1,0},{2,1},{3,2},{4,7},{5,4},{6,5},{7,6},{8,11},{9,8},{10,9... | collective-permute-start | bytes 393224 | tf_op jit(solution)/shard_map/ppermute | solution.py:58
  14.3 21.7 %collective-permute-start = (bf16[256,1024]{1,0:T(8,128)(2,1)S(1)}, bf16[256,1024]{1,0:T(8,128)(2,1)S(1)}, u32[]{:S(2)}, u32[]{:S(2)}) collective-permute-start(bf16[256,1024]{1,0:T(8,128)(2,1)S(1)} %copy-done.2), channel_id=1, source_target_pairs={{0,3},{1,0},{2,1},{3,2},{4,7},{5,4},{6,5},{7,6},{8,11},{9,8},{10,9... | collective-permute-start | bytes 1572872 | tf_op jit(solution)/shard_map/ppermute | solution.py:64
  14.7 21.3 %collective-permute-start.2 = (bf16[256,1024]{1,0:T(8,128)(2,1)S(1)}, bf16[256,1024]{1,0:T(8,128)(2,1)S(1)}, u32[]{:S(2)}, u32[]{:S(2)}) collective-permute-start(bf16[256,1024]{1,0:T(8,128)(2,1)S(1)} %copy-done.2), channel_id=1, source_target_pairs={{0,1},{1,2},{2,3},{3,0},{4,5},{5,6},{6,7},{7,4},{8,9},{9,10},{10,1... | collective-permute-start | bytes 1572872 | tf_op jit(solution)/shard_map/ppermute | solution.py:64
  16.4 15.6 %collective-permute-start.9 = (bf16[128,512]{1,0:T(8,128)(2,1)S(1)}, bf16[128,512]{1,0:T(8,128)(2,1)S(1)}, u32[]{:S(2)}, u32[]{:S(2)}) collective-permute-start(bf16[128,512]{1,0:T(8,128)(2,1)S(1)} %get-tuple-element.50), channel_id=1, source_target_pairs={{0,2},{1,3},{2,0},{3,1},{4,6},{5,7},{6,4},{7,5},{8,10},{9,11},{10,... | collective-permute-start | bytes 393224 | tf_op jit(solution)/shard_map/ppermute | solution.py:58
  16.4 18.3 %collective-permute-start.10 = (bf16[128,512]{1,0:T(8,128)(2,1)S(1)}, bf16[128,512]{1,0:T(8,128)(2,1)S(1)}, u32[]{:S(2)}, u32[]{:S(2)}) collective-permute-start(bf16[128,512]{1,0:T(8,128)(2,1)S(1)} %get-tuple-element.49), channel_id=1, source_target_pairs={{0,1},{1,2},{2,3},{3,0},{4,5},{5,6},{6,7},{7,4},{8,9},{9,10},{10,1... | collective-permute-start | bytes 393224 | tf_op jit(solution)/shard_map/ppermute | solution.py:58
  36.1 34.7 %all-to-all-start = ((bf16[32,32,896]{2,1,0:T(8,128)(2,1)}), bf16[32,32,896]{2,1,0:T(8,128)(2,1)}, u32[]{:S(2)}, u32[]{:S(2)}) async-start(bf16[32,32,896]{2,1,0:T(8,128)(2,1)} %param.16), calls=%async_computation | async-start | bytes 3670016 | tf_op jit(solution)/shard_map/all_to_all | solution.py:431
  43.8 127.5 %all-gather.7.cloned.1.call-start = ((), (), s32[]{:S(2)}) async-start(), calls=%async_computation.3 | async-start | bytes 8650752 | tf_op jit(solution)/shard_map/all_gather | solution.py:439
  43.9 16.5 %collective-permute-start.1 = (bf16[256,1024]{1,0:T(8,128)(2,1)S(1)}, bf16[256,1024]{1,0:T(8,128)(2,1)}, u32[]{:S(2)}, u32[]{:S(2)}) collective-permute-start(bf16[256,1024]{1,0:T(8,128)(2,1)S(1)} %copy-done.2), channel_id=1, source_target_pairs={{0,2},{1,3},{2,0},{3,1},{4,6},{5,7},{6,4},{7,5},{8,10},{9,11},{10,... | collective-permute-start | bytes 1572872 | tf_op jit(solution)/shard_map/ppermute | solution.py:64
  45.2 22.7 %collective-permute-start.3 = (bf16[256,1024]{1,0:T(8,128)(2,1)S(1)}, bf16[256,1024]{1,0:T(8,128)(2,1)S(1)}, u32[]{:S(2)}, u32[]{:S(2)}) collective-permute-start(bf16[256,1024]{1,0:T(8,128)(2,1)S(1)} %copy-done.5), channel_id=1, source_target_pairs={{0,3},{1,0},{2,1},{3,2},{4,7},{5,4},{6,5},{7,6},{8,11},{9,8},{10,9... | collective-permute-start | bytes 1572872 | tf_op jit(solution)/shard_map/ppermute | solution.py:64
  47.0 23.6 %collective-permute-start.4 = (bf16[256,1024]{1,0:T(8,128)(2,1)S(1)}, bf16[256,1024]{1,0:T(8,128)(2,1)S(1)}, u32[]{:S(2)}, u32[]{:S(2)}) collective-permute-start(bf16[256,1024]{1,0:T(8,128)(2,1)S(1)} %copy-done.5), channel_id=1, source_target_pairs={{0,1},{1,2},{2,3},{3,0},{4,5},{5,6},{6,7},{7,4},{8,9},{9,10},{10,1... | collective-permute-start | bytes 1572872 | tf_op jit(solution)/shard_map/ppermute | solution.py:64
  74.2 36.8 %collective-permute-start.11 = (bf16[256,1024]{1,0:T(8,128)(2,1)S(1)}, bf16[256,1024]{1,0:T(8,128)(2,1)S(1)}, u32[]{:S(2)}, u32[]{:S(2)}) collective-permute-start(bf16[256,1024]{1,0:T(8,128)(2,1)S(1)} %copy-done.5), channel_id=1, source_target_pairs={{0,2},{1,3},{2,0},{3,1},{4,6},{5,7},{6,4},{7,5},{8,10},{9,11},{10,... | collective-permute-start | bytes 1572872 | tf_op jit(solution)/shard_map/ppermute | solution.py:64
  75.6 44.0 %all-to-all-start.1 = ((bf16[4,128,896]{2,1,0:T(8,128)(2,1)}), bf16[4,128,896]{2,1,0:T(8,128)(2,1)}, u32[]{:S(2)}, u32[]{:S(2)}) async-start(bf16[4,128,896]{2,1,0:T(8,128)(2,1)} %bitcast.46), calls=%async_computation.1 | async-start | bytes 1835008 | tf_op jit(solution)/shard_map/all_to_all | solution.py:436
  79.8 23.5 %collective-permute-start.5 = (bf16[64,1792]{1,0:T(8,128)(2,1)S(1)}, bf16[64,1792]{1,0:T(8,128)(2,1)S(1)}, u32[]{:S(2)}, u32[]{:S(2)}) collective-permute-start(bf16[64,1792]{1,0:T(8,128)(2,1)S(1)} %copy-done.16), channel_id=1, source_target_pairs={{0,3},{1,0},{2,1},{3,2},{4,7},{5,4},{6,5},{7,6},{8,11},{9,8},{10,9... | collective-permute-start | bytes 688136 | tf_op jit(solution)/shard_map/ppermute | solution.py:396
  83.0 22.4 %collective-permute-start.6 = (bf16[64,1792]{1,0:T(8,128)(2,1)S(1)}, bf16[64,1792]{1,0:T(8,128)(2,1)S(1)}, u32[]{:S(2)}, u32[]{:S(2)}) collective-permute-start(bf16[64,1792]{1,0:T(8,128)(2,1)S(1)} %copy-done.14), channel_id=1, source_target_pairs={{0,2},{1,3},{2,0},{3,1},{4,6},{5,7},{6,4},{7,5},{8,10},{9,11},{10,... | collective-permute-start | bytes 688136 | tf_op jit(solution)/shard_map/ppermute | solution.py:396
  83.8 26.4 %collective-permute-start.7 = (bf16[64,1792]{1,0:T(8,128)(2,1)S(1)}, bf16[64,1792]{1,0:T(8,128)(2,1)S(1)}, u32[]{:S(2)}, u32[]{:S(2)}) collective-permute-start(bf16[64,1792]{1,0:T(8,128)(2,1)S(1)} %copy-done.12), channel_id=1, source_target_pairs={{0,1},{1,2},{2,3},{3,0},{4,5},{5,6},{6,7},{7,4},{8,9},{9,10},{10,1... | collective-permute-start | bytes 688136 | tf_op jit(solution)/shard_map/ppermute | solution.py:396
  116.8 10.3 %collective-permute-start.12 = (bf16[2,64,512]{2,1,0:T(8,128)(2,1)S(1)}, bf16[2,64,512]{2,1,0:T(8,128)(2,1)S(1)}, u32[]{:S(2)}, u32[]{:S(2)}) collective-permute-start(bf16[2,64,512]{2,1,0:T(8,128)(2,1)S(1)} %get-tuple-element.46), channel_id=1, source_target_pairs={{0,3},{1,0},{2,1},{3,2},{4,7},{5,4},{6,5},{7,6},{8,11},{9,8},{10,9... | collective-permute-start | bytes 393224 | tf_op jit(solution)/shard_map/ppermute | solution.py:58
  117.5 9.7 %collective-permute-start.13 = (bf16[2,64,512]{2,1,0:T(8,128)(2,1)S(1)}, bf16[2,64,512]{2,1,0:T(8,128)(2,1)S(1)}, u32[]{:S(2)}, u32[]{:S(2)}) collective-permute-start(bf16[2,64,512]{2,1,0:T(8,128)(2,1)S(1)} %get-tuple-element.45), channel_id=1, source_target_pairs={{0,2},{1,3},{2,0},{3,1},{4,6},{5,7},{6,4},{7,5},{8,10},{9,11},{10,... | collective-permute-start | bytes 393224 | tf_op jit(solution)/shard_map/ppermute | solution.py:58
  140.1 26.6 %collective-permute-start.15 = (bf16[2,64,2048]{2,1,0:T(8,128)(2,1)}, bf16[2,64,2048]{2,1,0:T(8,128)(2,1)}, u32[]{:S(2)}, u32[]{:S(2)}) collective-permute-start(bf16[2,64,2048]{2,1,0:T(8,128)(2,1)} %get-tuple-element.33.c0), channel_id=1, source_target_pairs={{0,3},{1,0},{2,1},{3,2},{4,7},{5,4},{6,5},{7,6},{8,11},{9,8},{10,9... | collective-permute-start | bytes 1572872 | tf_op jit(solution)/shard_map/ppermute | solution.py:64
  143.3 23.3 %collective-permute-start.16 = (bf16[2,64,2048]{2,1,0:T(8,128)(2,1)}, bf16[2,64,2048]{2,1,0:T(8,128)(2,1)}, u32[]{:S(2)}, u32[]{:S(2)}) collective-permute-start(bf16[2,64,2048]{2,1,0:T(8,128)(2,1)} %get-tuple-element.33.c0), channel_id=1, source_target_pairs={{0,2},{1,3},{2,0},{3,1},{4,6},{5,7},{6,4},{7,5},{8,10},{9,11},{10,... | collective-permute-start | bytes 1572872 | tf_op jit(solution)/shard_map/ppermute | solution.py:64
  143.7 27.6 %collective-permute-start.17 = (bf16[2,64,2048]{2,1,0:T(8,128)(2,1)}, bf16[2,64,2048]{2,1,0:T(8,128)(2,1)}, u32[]{:S(2)}, u32[]{:S(2)}) collective-permute-start(bf16[2,64,2048]{2,1,0:T(8,128)(2,1)} %get-tuple-element.33.c0), channel_id=1, source_target_pairs={{0,1},{1,2},{2,3},{3,0},{4,5},{5,6},{6,7},{7,4},{8,9},{9,10},{10,1... | collective-permute-start | bytes 1572872 | tf_op jit(solution)/shard_map/ppermute | solution.py:64
  159.6 21.6 %collective-permute-start.18 = (bf16[64,1792]{1,0:T(8,128)(2,1)}, bf16[64,1792]{1,0:T(8,128)(2,1)S(1)}, u32[]{:S(2)}, u32[]{:S(2)}) collective-permute-start(bf16[64,1792]{1,0:T(8,128)(2,1)} %encoded_back.1.c0), channel_id=1, source_target_pairs={{0,3},{1,0},{2,1},{3,2},{4,7},{5,4},{6,5},{7,6},{8,11},{9,8},{10,9... | collective-permute-start | bytes 688136 | tf_op jit(solution)/shard_map/ppermute | solution.py:64
  161.5 19.6 %collective-permute-start.19 = (bf16[64,1792]{1,0:T(8,128)(2,1)}, bf16[64,1792]{1,0:T(8,128)(2,1)}, u32[]{:S(2)}, u32[]{:S(2)}) collective-permute-start(bf16[64,1792]{1,0:T(8,128)(2,1)} %encoded_back.1.c0), channel_id=1, source_target_pairs={{0,2},{1,3},{2,0},{3,1},{4,6},{5,7},{6,4},{7,5},{8,10},{9,11},{10,... | collective-permute-start | bytes 688136 | tf_op jit(solution)/shard_map/ppermute | solution.py:64
  166.7 14.5 %collective-permute-start.20 = (bf16[64,1792]{1,0:T(8,128)(2,1)}, bf16[64,1792]{1,0:T(8,128)(2,1)}, u32[]{:S(2)}, u32[]{:S(2)}) collective-permute-start(bf16[64,1792]{1,0:T(8,128)(2,1)} %encoded_back.1.c0), channel_id=1, source_target_pairs={{0,1},{1,2},{2,3},{3,0},{4,5},{5,6},{6,7},{7,4},{8,9},{9,10},{10,1... | collective-permute-start | bytes 688136 | tf_op jit(solution)/shard_map/ppermute | solution.py:64
  (28 other events, 193.8 us)
Sparse Core Ops, SparseCore 0:
  36.2 63.4 all-gather.4
  102.5 52.3 all-gather.6

commit v2 on v1

--- a/solution.py
+++ b/solution.py
@@ -66,6 +66,17 @@
     ]
 
 
+def spread_ring(shard, axis="tensor"):
+    down = [(i, (i - 1) % 4) for i in range(4)]
+    up = [(i, (i + 1) % 4) for i in range(4)]
+    half = shard.shape[0] // 2
+    next_one = lax.ppermute(shard, axis, down)
+    last_one = lax.ppermute(shard, axis, up)
+    top = lax.ppermute(next_one[:half], axis, down)
+    bottom = lax.ppermute(last_one[half:], axis, up)
+    return [shard, next_one, top, bottom, last_one]
+
+
 def after(value, earlier):
     return lax.optimization_barrier((value, earlier))[0]
 
@@ -97,15 +108,21 @@
         ref[...] = total_ref[pl.ds(start, length), :].astype(BF16)
 
 
-def project_kernel(dims, shift, s_ref, p0, p1, p2, p3, weight_ref, *rest):
+def project_kernel(dims, shift, s_ref, p0, p1, top, bottom, p3, weight_ref, *rest):
     out_ref, total_ref = rest[-2:]
     step = pl.program_id(0)
-    for k, ref in enumerate((p0, p1, p2, p3)):
+    half = top.shape[0]
+    for k, ref in ((0, p0), (1, p1), (3, p3)):
 
         @pl.when(step == k)
         def _(ref=ref, k=k):
-            term = dot(ref[: total_ref.shape[0], :], weight_ref[...], dims)
+            term = dot(ref[...], weight_ref[...], dims)
             total_ref[...] = term if k == 0 else total_ref[...] + term
+
+    @pl.when(step == 2)
+    def _():
+        total_ref[:half, :] += dot(top[...], weight_ref[...], dims)
+        total_ref[half:, :] += dot(bottom[...], weight_ref[...], dims)
 
     @pl.when(step == pl.num_programs(0) - 1)
     def _():
@@ -312,14 +329,6 @@
         grad_ref[...] = cotangent_ref[...].astype(F32) + moved
 
 
-def cond_grad_kernel(s_ref, c0, c1, c2, c3, weight_ref, base_ref, out_ref):
-    length = c0.shape[0]
-    d_cond = jnp.concatenate([c0[...], c1[...], c2[...], c3[...]], axis=0)
-    term = dot(d_cond, weight_ref[...], ROWS_T)
-    by = s_ref[0] * length
-    out_ref[...] = (base_ref[...] + placed_rows(term, by, 0)).astype(out_ref.dtype)
-
-
 def shards(
     hidden,
     cotangent,
@@ -373,9 +382,9 @@
     weight_parts = exchange(jnp.concatenate([kv_part, wq_part, wo_part], axis=1), here)
     kv_parts = jnp.stack([part[: 2 * SLICE] for part in weight_parts])
     qo_parts = jnp.stack([part[2 * SLICE :] for part in weight_parts])
-    hidden_parts = spread(hidden, n_tensor)
-    cot_parts = spread(cotangent, n_tensor)
-    near = (hidden_parts[1], hidden_parts[3])
+    hidden_parts = spread_ring(hidden)
+    cot_parts = spread_ring(cotangent)
+    near = (hidden_parts[1], hidden_parts[4])
     kv_all = lax.all_gather(after(kv_parts, near), "dp", axis=0)
 
     def weight_spec(index):
@@ -423,7 +432,7 @@
         "query",
     )
 
-    live = jnp.arange(slots_per)[None, :] < after(seq_counts, (query, own_cond, cot_parts[1], cot_parts[3]))[:, None]
+    live = jnp.arange(slots_per)[None, :] < after(seq_counts, (query, cot_parts[1:], cond_parts[1:]))[:, None]
     slot_flat = slot_of.reshape(item_total)
     matches = (jnp.arange(slot_total)[:, None] == slot_flat[None, :]) & live.reshape(item_total)[
         None, :
@@ -514,7 +523,7 @@
         enc_queries,
         cond,
     )
-    d_cond_parts = spread(d_cond, n_tensor)
+    d_cond_parts = spread(after(d_cond, both_parts[1]), n_tensor)
 
     out_spec = whole(tokens, part_width)
     acc = pltpu.VMEM((tokens, part_width), F32)
@@ -528,16 +537,11 @@
         [acc, acc],
         60,
     )(scalars, *both_parts, qo_all, qo_all, hidden, cotangent)
-    grad_hidden = call(
-        cond_grad_kernel,
-        "cond_grad",
-        1,
-        [c_spec] * 4 + [whole(part_width, 2 * enc_width), out_spec],
-        out_spec,
-        sds((tokens, part_width), BF16),
-        [],
-        16,
-    )(scalars, *d_cond_parts, cond_weight, from_query)
+    d_cond_parts = after(d_cond_parts, from_query)
+    d_cond_all = lax.dynamic_slice_in_dim(
+        jnp.stack(d_cond_parts * 2), (n_tensor - here) % n_tensor, n_tensor, 0
+    ).reshape(tokens, 2 * enc_width)
+    grad_hidden = (from_query + dot(d_cond_all, cond_weight, ROWS_T)).astype(BF16)
     return (mixed, grad_hidden)
 
 

time: 197 us -> 177 us (0.90)
  waiting for transfers between devices: 58.3 us -> 33.8 us
  local copies, waits for them, and re-layouts: 18.7 us -> 21.7 us
  Pallas kernels: 56.1 us -> 53.4 us
  starting transfers between devices: 41.7 us -> 44 us
    ppermute x3, waiting for transfers between devices: 25.5 us -> 0.52 us  [shards(): lax.ppermute(array, 'tensor', [(i, (i - k) % n_tensor) for i in range(n_t...]
    ppermute x12 -> x6, waiting for transfers between devices: 17.6 us -> 5.07 us  [spread(): lax.ppermute(shard, axis, [(i, (i - k) % size) for i in range(size)])]
    ppermute x0 -> x8, waiting for transfers between devices: none -> 9.89 us  [the longest x2 9.87 us: spread_ring(): next_one = lax.ppermute(shard, axis, down)]
    ppermute x0 -> x8, starting transfers between devices: none -> 8.3 us  [the longest x2 3.64 us: spread_ring(): last_one = lax.ppermute(shard, axis, up)]
    ppermute x12 -> x6, starting transfers between devices: 15.6 us -> 8.42 us  [spread(): lax.ppermute(shard, axis, [(i, (i - k) % size) for i in range(size)])]
    pallas_call x1 -> x0, Pallas kernels: 3.83 us -> none  [shards(): call(cond_grad_kernel, 'cond_grad', 1, [c_spec] * 4 + [whole(part_width,...]
    unnamed x54 -> x53, local copies, waits for them, and re-layouts: 11.9 us -> 14.6 us
    all_gather x1, waiting for transfers between devices: 0.01 us -> 2.51 us  [shards(): qo_all = lax.all_gather(after(qo_parts, items), 'dp', axis=0)]
  transfers between devices with their start and end apart: 25 -> 27, of which waited for: 10 -> 6; matrix products, arithmetic and copies ran while one was open for 4% -> 5% of each run, Pallas kernels for 27% -> 31%
where the time goes in v2:
time: 177 us; the launch traced here: 174 us
  Pallas kernels  53.4 us (30%)
  starting transfers between devices  44 us (25%)
  waiting for transfers between devices  33.8 us (19%)
  local copies, waits for them, and re-layouts  21.7 us (12%)
  between operations  14.5 us (8%)
  matrix products  4.17 us (2%)
  other arithmetic  2.36 us (1%)
    ppermute x6, waiting for transfers between devices, exchange(): lax.ppermute(piece, axis, [(i, (i - k) % size) for i in range(size)])  15.8 us
    pallas_call x1, Pallas kernels, shards(): call(encoded_back_kernel, 'encoded_back', n_tensor, [group(head_rows, row...  14.8 us
    unnamed x53, local copies, waits for them, and re-layouts  14.6 us
    pallas_call x1, Pallas kernels, shards(): call(attention_kernel, 'attention', n_tensor, [r_spec, weight_spec(0), we...  12.3 us
    ppermute x6, starting transfers between devices, exchange(): lax.ppermute(piece, axis, [(i, (i - k) % size) for i in range(size)])  11.5 us
    ppermute x2, waiting for transfers between devices, spread_ring(): next_one = lax.ppermute(shard, axis, down)  9.87 us
    pallas_call x1, Pallas kernels, shards(): call(functools.partial(outputs_kernel, shift), 'outputs', n_tensor, [both...  9.54 us
    ppermute x6, starting transfers between devices, spread(): lax.ppermute(shard, axis, [(i, (i - k) % size) for i in range(size)])  8.42 us
  transfers between devices with their start and end apart: 27, of which 6 were waited for; matrix products, arithmetic and copies ran while one was open for 5% of the time, Pallas kernels for 31%

profile of v2, /device:TPU:10, one launch (start us, length us, event | category | flops | bytes accessed | tf_op | source)
XLA Modules:
  0.0 174.0 jit_solution(8017951550033876345)
XLA Ops:
  10.2 4.1 %collective-permute-start.11 = (bf16[128,512]{1,0:T(8,128)(2,1)S(1)}, bf16[128,512]{1,0:T(8,128)(2,1)S(1)}, u32[]{:S(2)}, u32[]{:S(2)}) collective-permute-start(bf16[128,512]{1,0:T(8,128)(2,1)S(1)} %get-tuple-element.60), channel_id=1, source_target_pairs={{0,3},{1,0},{2,1},{3,2},{4,7},{5,4},{6,5},{7,6},{8,11},{9,8},{10,9... | collective-permute-start | bytes 393224 | tf_op jit(solution)/shard_map/ppermute | solution.py:58
  16.4 2.5 %collective-permute-start.13 = (bf16[128,512]{1,0:T(8,128)(2,1)S(1)}, bf16[128,512]{1,0:T(8,128)(2,1)S(1)}, u32[]{:S(2)}, u32[]{:S(2)}) collective-permute-start(bf16[128,512]{1,0:T(8,128)(2,1)S(1)} %get-tuple-element.61), channel_id=1, source_target_pairs={{0,1},{1,2},{2,3},{3,0},{4,5},{5,6},{6,7},{7,4},{8,9},{9,10},{10,1... | collective-permute-start | bytes 393224 | tf_op jit(solution)/shard_map/ppermute | solution.py:58
  18.9 13.1 %collective-permute-done.12 = bf16[128,512]{1,0:T(8,128)(2,1)S(1)} collective-permute-done((bf16[128,512]{1,0:T(8,128)(2,1)S(1)}, bf16[128,512]{1,0:T(8,128)(2,1)S(1)}, u32[]{:S(2)}, u32[]{:S(2)}) %collective-permute-start.12) | collective-permute-done | bytes 131104 | tf_op jit(solution)/shard_map/ppermute | solution.py:58
  32.0 2.7 %collective-permute-done.13 = bf16[128,512]{1,0:T(8,128)(2,1)S(1)} collective-permute-done((bf16[128,512]{1,0:T(8,128)(2,1)S(1)}, bf16[128,512]{1,0:T(8,128)(2,1)S(1)}, u32[]{:S(2)}, u32[]{:S(2)}) %collective-permute-start.13) | collective-permute-done | bytes 131104 | tf_op jit(solution)/shard_map/ppermute | solution.py:58
  35.5 7.7 %all-to-all-start = ((bf16[32,32,896]{2,1,0:T(8,128)(2,1)}), bf16[32,32,896]{2,1,0:T(8,128)(2,1)}, u32[]{:S(2)}, u32[]{:S(2)}) async-start(bf16[32,32,896]{2,1,0:T(8,128)(2,1)} %param.16), calls=%async_computation | async-start | bytes 3670016 | tf_op jit(solution)/shard_map/all_to_all | solution.py:440
  48.2 9.9 %collective-permute-done.4.p1 = bf16[256,1024]{1,0:T(8,128)(2,1)S(1)} collective-permute-done((bf16[256,1024]{1,0:T(8,128)(2,1)S(1)}, bf16[256,1024]{1,0:T(8,128)(2,1)S(1)}, u32[]{:S(2)}, u32[]{:S(2)}) %collective-permute-start.4) | collective-permute-done | bytes 524320 | tf_op jit(solution)/shard_map/ppermute | solution.py:73
  62.3 2.0 %copy-done.3 = bf16[1024,1792]{1,0:T(8,128)(2,1)S(1)} copy-done((bf16[1024,1792]{1,0:T(8,128)(2,1)S(1)}, bf16[1024,1792]{1,0:T(8,128)(2,1)}, u32[]{:S(2)}) %copy-start.3) | copy-done | bytes 3670040
  64.4 2.5 %cond.1 = (bf16[64,1792]{1,0:T(8,128)(2,1)S(1)}, bf16[64,1792]{1,0:T(8,128)(2,1)}, bf16[64,1792]{1,0:T(8,128)(2,1)}, bf16[64,1792]{1,0:T(8,128)(2,1)}) custom-call(s32[2]{0:T(128)S(1)} %pad_add_fusion.s_ref, bf16[256,1024]{1,0:T(8,128)(2,1)S(1)} %copy-done, bf16[1024,1792]{1,0:T(8,128)(2,1)S(1)} %copy-done.3), custom_call_target="tpu_custom_call" | custom-call | tf_op jit(solution)/shard_map/cond/pallas_call | solution.py:394
  68.7 2.8 %collective-permute-start.8 = (bf16[64,1792]{1,0:T(8,128)(2,1)}, bf16[64,1792]{1,0:T(8,128)(2,1)}, u32[]{:S(2)}, u32[]{:S(2)}) collective-permute-start(bf16[64,1792]{1,0:T(8,128)(2,1)} %get-tuple-element.28), channel_id=1, source_target_pairs={{0,3},{1,0},{2,1},{3,2},{4,7},{5,4},{6,5},{7,6},{8,11},{9,8},{10,9... | collective-permute-start | bytes 688136 | tf_op jit(solution)/shard_map/ppermute | solution.py:405
  73.7 2.2 %copy-done.2 = bf16[4096,512]{1,0:T(8,128)(2,1)S(1)} copy-done((bf16[4096,512]{1,0:T(8,128)(2,1)S(1)}, bf16[4096,512]{1,0:T(8,128)(2,1)}, u32[]{:S(2)}) %copy-start.2) | copy-done | bytes 4194328
  77.8 2.5 %query.1.rest_0_ = bf16[256,512]{1,0:T(8,128)(2,1)S(1)} custom-call(s32[2]{0:T(128)S(1)} %pad_add_fusion.s_ref, bf16[256,1024]{1,0:T(8,128)(2,1)S(1)} %copy-done, bf16[256,1024]{1,0:T(8,128)(2,1)S(1)} %collective-permute-done.p1, bf16[128,1024]{1,0:T(8,128)(2,1)S(1)} %copy-done.7, bf16[128,1024]{1,0:T(8,128)(2,1)S(1)} %copy-done.9, ...), custom_call_target="tpu_custom_call" | custom-call | tf_op jit(solution)/shard_map/query/pallas_call | solution.py:413
  81.0 2.2 %fusion.2 = bf16[16,32,896]{2,0,1:T(8,128)(2,1)S(1)} fusion(bf16[32,32,896]{2,1,0:T(8,128)(2,1)} %all-to-all-done, s32[16]{0:T(128)S(1)} %eq.24, pred[16]{0:T(512)(128)(4,1)S(1)} %lt.78), kind=kOutput, calls=%fused_computation.2 | convolution fusion | flops 29819904 | bytes 2752592 | tf_op jit(solution)/shard_map/si,sre->ire/dot_general | solution.py:441
  84.4 4.1 %all-to-all-start.1 = ((bf16[4,128,896]{2,1,0:T(8,128)(2,1)}), bf16[4,128,896]{2,1,0:T(8,128)(2,1)S(1)}, u32[]{:S(2)}, u32[]{:S(2)}) async-start(bf16[4,128,896]{2,1,0:T(8,128)(2,1)} %bitcast.4), calls=%async_computation.1 | async-start | bytes 1835008 | tf_op jit(solution)/shard_map/all_to_all | solution.py:445
  88.5 2.4 %copy-done.1 = bf16[512,4096]{1,0:T(8,128)(2,1)S(1)} copy-done((bf16[512,4096]{1,0:T(8,128)(2,1)S(1)}, bf16[512,4096]{1,0:T(8,128)(2,1)}, u32[]{:S(2)}) %copy-start.1) | copy-done | bytes 4194328
  90.9 4.3 %d_ctx.1 = bf16[4,2,64,512]{3,2,1,0:T(8,128)(2,1)S(1)} custom-call(s32[2]{0:T(128)S(1)} %pad_add_fusion.s_ref, bf16[256,1024]{1,0:T(8,128)(2,1)S(1)} %copy-done.5, bf16[256,1024]{1,0:T(8,128)(2,1)S(1)} %collective-permute-done.4.p1, bf16[128,1024]{1,0:T(8,128)(2,1)} %collective-permute-done.5.top, bf16[128,1024]{1,0:T(8,128)(2,1)} %collective-permute-done.7.bottom, ...), custom_call_target="tpu_custom_call" | custom-call | tf_op jit(solution)/shard_map/d_ctx/pallas_call | solution.py:413
  95.9 3.3 %collective-permute-start.14 = (bf16[2,64,512]{2,1,0:T(8,128)(2,1)S(1)}, bf16[2,64,512]{2,1,0:T(8,128)(2,1)S(1)}, u32[]{:S(2)}, u32[]{:S(2)}) collective-permute-start(bf16[2,64,512]{2,1,0:T(8,128)(2,1)S(1)} %get-tuple-element.58), channel_id=1, source_target_pairs={{0,3},{1,0},{2,1},{3,2},{4,7},{5,4},{6,5},{7,6},{8,11},{9,8},{10,9... | collective-permute-start | bytes 393224 | tf_op jit(solution)/shard_map/ppermute | solution.py:58
  101.8 7.5 %encode.1 = (bf16[64,1792]{1,0:T(8,128)(2,1)}, bf16[512,896]{1,0:T(8,128)(2,1)}, f32[448,512]{1,0:T(8,128)}, bf16[512,896]{1,0:T(8,128)(2,1)}) custom-call(s32[2]{0:T(128)} %copy-done.11, bf16[512,896]{1,0:T(8,128)(2,1)} %bitcast.61, bf16[64,1792]{1,0:T(8,128)(2,1)} %copy-done.10, bf16[64,1792]{1,0:T(8,128)(2,1)} %collective-permute-done.8.c1, ...), custom_call_target="tpu_custom_call" | custom-call | tf_op jit(solution)/shard_map/encode/pallas_call | solution.py:464
  110.1 12.3 %attention.1 = (bf16[4,256,512]{2,1,0:T(8,128)(2,1)}, bf16[4,256,512]{2,1,0:T(8,128)(2,1)}, bf16[2,64,2048]{2,1,0:T(8,128)(2,1)}) custom-call(s32[2]{0:T(128)} %copy-done.11, bf16[512,896]{1,0:T(8,128)(2,1)} %get-tuple-element.33.encoded_ref, bf16[32,4,64,512]{3,2,1,0:T(8,128)(2,1)} %bitcast.55, bf16[32,4,64,512]{3,2,1,0:T(8,128)(2,1)} %bitcast.56, ...), custom_call_target="tpu_custom_call" | custom-call | tf_op jit(solution)/shard_map/attention/pallas_call | solution.py:483
  122.4 3.3 %collective-permute-start.17 = (bf16[2,64,2048]{2,1,0:T(8,128)(2,1)}, bf16[2,64,2048]{2,1,0:T(8,128)(2,1)S(1)}, u32[]{:S(2)}, u32[]{:S(2)}) collective-permute-start(bf16[2,64,2048]{2,1,0:T(8,128)(2,1)} %get-tuple-element.40.c0), channel_id=1, source_target_pairs={{0,3},{1,0},{2,1},{3,2},{4,7},{5,4},{6,5},{7,6},{8,11},{9,8},{10,9... | collective-permute-start | bytes 1572872 | tf_op jit(solution)/shard_map/ppermute | solution.py:64
  126.7 14.8 %encoded_back.1 = bf16[64,1792]{1,0:T(8,128)(2,1)} custom-call(s32[2]{0:T(128)} %copy-done.11, bf16[4,256,512]{2,1,0:T(8,128)(2,1)} %get-tuple-element.44.d_scores_ref, bf16[4,256,512]{2,1,0:T(8,128)(2,1)} %get-tuple-element.45.probs_ref, bf16[2,64,512]{2,1,0:T(8,128)(2,1)} %get-tuple-element.59.q0, bf16[2,64,512]{2,1,0:T(8,128)(2,1)} %copy-done.14, ...), custom_call_target="tpu_custom_call" | custom-call | tf_op jit(solution)/shard_map/encoded_back/pallas_call | solution.py:503
  141.5 3.1 %collective-permute-start.20 = (bf16[64,1792]{1,0:T(8,128)(2,1)}, bf16[64,1792]{1,0:T(8,128)(2,1)S(1)}, u32[]{:S(2)}, u32[]{:S(2)}) collective-permute-start(bf16[64,1792]{1,0:T(8,128)(2,1)} %encoded_back.1), channel_id=1, source_target_pairs={{0,3},{1,0},{2,1},{3,2},{4,7},{5,4},{6,5},{7,6},{8,11},{9,8},{10,9... | collective-permute-start | bytes 688136 | tf_op jit(solution)/shard_map/ppermute | solution.py:64
  145.7 5.1 %collective-permute-done.19.c3 = bf16[2,64,2048]{2,1,0:T(8,128)(2,1)S(1)} collective-permute-done((bf16[2,64,2048]{2,1,0:T(8,128)(2,1)}, bf16[2,64,2048]{2,1,0:T(8,128)(2,1)S(1)}, u32[]{:S(2)}, u32[]{:S(2)}) %collective-permute-start.19) | collective-permute-done | bytes 524320 | tf_op jit(solution)/shard_map/ppermute | solution.py:64
  150.7 2.5 %all-gather.7.cloned.1.call-done = bf16[128,64,512]{2,1,0:T(8,128)(2,1)} async-done(((bf16[4,64,512]{2,1,0:T(8,128)(2,1)}), bf16[128,64,512]{2,1,0:T(8,128)(2,1)}) %all-gather.7.cloned.1.call-update) | async-done | bytes 8388624 | tf_op jit(solution)/shard_map/all_gather | solution.py:448
  153.3 9.5 %outputs.1 = (bf16[256,1024]{1,0:T(8,128)(2,1)}, f32[256,1024]{1,0:T(8,128)}) custom-call(s32[2]{0:T(128)} %copy-done.11, bf16[2,64,2048]{2,1,0:T(8,128)(2,1)} %get-tuple-element.40.c0, bf16[2,64,2048]{2,1,0:T(8,128)(2,1)} %copy-done.17, bf16[2,64,2048]{2,1,0:T(8,128)(2,1)} %copy-done.18, bf16[2,64,2048]{2,1,0:T(8,128)(2,1)} %copy-done.19, ...), custom_call_target="tpu_custom_call" | custom-call | tf_op jit(solution)/shard_map/outputs/pallas_call | solution.py:530
  (122 shorter events, 33.2 us)
Async XLA Ops:
  7.2 102.2 %all-gather.5.cloned.1.call-start = ((), (), s32[]{:S(2)}) async-start(), calls=%async_computation.2 | async-start | bytes 8650752 | tf_op jit(solution)/shard_map/all_gather | solution.py:388
  14.3 21.1 %collective-permute-start = (bf16[256,1024]{1,0:T(8,128)(2,1)S(1)}, bf16[256,1024]{1,0:T(8,128)(2,1)S(1)}, u32[]{:S(2)}, u32[]{:S(2)}) collective-permute-start(bf16[256,1024]{1,0:T(8,128)(2,1)S(1)} %copy-done), channel_id=1, source_target_pairs={{0,3},{1,0},{2,1},{3,2},{4,7},{5,4},{6,5},{7,6},{8,11},{9,8},{10,9... | collective-permute-start | bytes 1572872 | tf_op jit(solution)/shard_map/ppermute | solution.py:73
  14.7 20.7 %collective-permute-start.2 = (bf16[256,1024]{1,0:T(8,128)(2,1)S(1)}, bf16[256,1024]{1,0:T(8,128)(2,1)S(1)}, u32[]{:S(2)}, u32[]{:S(2)}) collective-permute-start(bf16[256,1024]{1,0:T(8,128)(2,1)S(1)} %copy-done), channel_id=1, source_target_pairs={{0,1},{1,2},{2,3},{3,0},{4,5},{5,6},{6,7},{7,4},{8,9},{9,10},{10,1... | collective-permute-start | bytes 1572872 | tf_op jit(solution)/shard_map/ppermute | solution.py:74
  16.4 15.6 %collective-permute-start.12 = (bf16[128,512]{1,0:T(8,128)(2,1)S(1)}, bf16[128,512]{1,0:T(8,128)(2,1)S(1)}, u32[]{:S(2)}, u32[]{:S(2)}) collective-permute-start(bf16[128,512]{1,0:T(8,128)(2,1)S(1)} %get-tuple-element.62), channel_id=1, source_target_pairs={{0,2},{1,3},{2,0},{3,1},{4,6},{5,7},{6,4},{7,5},{8,10},{9,11},{10,... | collective-permute-start | bytes 393224 | tf_op jit(solution)/shard_map/ppermute | solution.py:58
  16.4 18.3 %collective-permute-start.13 = (bf16[128,512]{1,0:T(8,128)(2,1)S(1)}, bf16[128,512]{1,0:T(8,128)(2,1)S(1)}, u32[]{:S(2)}, u32[]{:S(2)}) collective-permute-start(bf16[128,512]{1,0:T(8,128)(2,1)S(1)} %get-tuple-element.61), channel_id=1, source_target_pairs={{0,1},{1,2},{2,3},{3,0},{4,5},{5,6},{6,7},{7,4},{8,9},{9,10},{10,1... | collective-permute-start | bytes 393224 | tf_op jit(solution)/shard_map/ppermute | solution.py:58
  35.5 45.5 %all-to-all-start = ((bf16[32,32,896]{2,1,0:T(8,128)(2,1)}), bf16[32,32,896]{2,1,0:T(8,128)(2,1)}, u32[]{:S(2)}, u32[]{:S(2)}) async-start(bf16[32,32,896]{2,1,0:T(8,128)(2,1)} %param.16), calls=%async_computation | async-start | bytes 3670016 | tf_op jit(solution)/shard_map/all_to_all | solution.py:440
  43.2 110.1 %all-gather.7.cloned.1.call-start = ((), (), s32[]{:S(2)}) async-start(), calls=%async_computation.3 | async-start | bytes 8650752 | tf_op jit(solution)/shard_map/all_gather | solution.py:448
  43.2 14.8 %collective-permute-start.4 = (bf16[256,1024]{1,0:T(8,128)(2,1)S(1)}, bf16[256,1024]{1,0:T(8,128)(2,1)S(1)}, u32[]{:S(2)}, u32[]{:S(2)}) collective-permute-start(bf16[256,1024]{1,0:T(8,128)(2,1)S(1)} %copy-done.5), channel_id=1, source_target_pairs={{0,3},{1,0},{2,1},{3,2},{4,7},{5,4},{6,5},{7,6},{8,11},{9,8},{10,9... | collective-permute-start | bytes 1572872 | tf_op jit(solution)/shard_map/ppermute | solution.py:73
  43.3 16.7 %collective-permute-start.6 = (bf16[256,1024]{1,0:T(8,128)(2,1)S(1)}, bf16[256,1024]{1,0:T(8,128)(2,1)S(1)}, u32[]{:S(2)}, u32[]{:S(2)}) collective-permute-start(bf16[256,1024]{1,0:T(8,128)(2,1)S(1)} %copy-done.5), channel_id=1, source_target_pairs={{0,1},{1,2},{2,3},{3,0},{4,5},{5,6},{6,7},{7,4},{8,9},{9,10},{10,1... | collective-permute-start | bytes 1572872 | tf_op jit(solution)/shard_map/ppermute | solution.py:74
  45.4 22.6 %collective-permute-start.1 = (bf16[128,1024]{1,0:T(8,128)(2,1)S(1)}, bf16[128,1024]{1,0:T(8,128)(2,1)S(1)}, u32[]{:S(2)}, u32[]{:S(2)}) collective-permute-start(bf16[128,1024]{1,0:T(8,128)(2,1)S(1)} %slice.50), channel_id=1, source_target_pairs={{0,3},{1,0},{2,1},{3,2},{4,7},{5,4},{6,5},{7,6},{8,11},{9,8},{10,9... | collective-permute-start | bytes 786440 | tf_op jit(solution)/shard_map/ppermute | solution.py:75
  46.7 24.8 %collective-permute-start.3 = (bf16[128,1024]{1,0:T(8,128)(2,1)S(1)}, bf16[128,1024]{1,0:T(8,128)(2,1)S(1)}, u32[]{:S(2)}, u32[]{:S(2)}) collective-permute-start(bf16[128,1024]{1,0:T(8,128)(2,1)S(1)} %slice.51), channel_id=1, source_target_pairs={{0,1},{1,2},{2,3},{3,0},{4,5},{5,6},{6,7},{7,4},{8,9},{9,10},{10,1... | collective-permute-start | bytes 786440 | tf_op jit(solution)/shard_map/ppermute | solution.py:76
  58.8 22.0 %collective-permute-start.5 = (bf16[128,1024]{1,0:T(8,128)(2,1)}, bf16[128,1024]{1,0:T(8,128)(2,1)}, u32[]{:S(2)}, u32[]{:S(2)}) collective-permute-start(bf16[128,1024]{1,0:T(8,128)(2,1)} %slice.52), channel_id=1, source_target_pairs={{0,3},{1,0},{2,1},{3,2},{4,7},{5,4},{6,5},{7,6},{8,11},{9,8},{10,9... | collective-permute-start | bytes 786440 | tf_op jit(solution)/shard_map/ppermute | solution.py:75
  60.7 20.1 %collective-permute-start.7 = (bf16[128,1024]{1,0:T(8,128)(2,1)}, bf16[128,1024]{1,0:T(8,128)(2,1)}, u32[]{:S(2)}, u32[]{:S(2)}) collective-permute-start(bf16[128,1024]{1,0:T(8,128)(2,1)} %slice.53), channel_id=1, source_target_pairs={{0,1},{1,2},{2,3},{3,0},{4,5},{5,6},{6,7},{7,4},{8,9},{9,10},{10,1... | collective-permute-start | bytes 786440 | tf_op jit(solution)/shard_map/ppermute | solution.py:76
  67.6 12.7 %collective-permute-start.10 = (bf16[64,1792]{1,0:T(8,128)(2,1)}, bf16[64,1792]{1,0:T(8,128)(2,1)}, u32[]{:S(2)}, u32[]{:S(2)}) collective-permute-start(bf16[64,1792]{1,0:T(8,128)(2,1)} %get-tuple-element.30), channel_id=1, source_target_pairs={{0,1},{1,2},{2,3},{3,0},{4,5},{5,6},{6,7},{7,4},{8,9},{9,10},{10,1... | collective-permute-start | bytes 688136 | tf_op jit(solution)/shard_map/ppermute | solution.py:405
  68.7 11.6 %collective-permute-start.8 = (bf16[64,1792]{1,0:T(8,128)(2,1)}, bf16[64,1792]{1,0:T(8,128)(2,1)}, u32[]{:S(2)}, u32[]{:S(2)}) collective-permute-start(bf16[64,1792]{1,0:T(8,128)(2,1)} %get-tuple-element.28), channel_id=1, source_target_pairs={{0,3},{1,0},{2,1},{3,2},{4,7},{5,4},{6,5},{7,6},{8,11},{9,8},{10,9... | collective-permute-start | bytes 688136 | tf_op jit(solution)/shard_map/ppermute | solution.py:405
  84.4 16.4 %all-to-all-start.1 = ((bf16[4,128,896]{2,1,0:T(8,128)(2,1)}), bf16[4,128,896]{2,1,0:T(8,128)(2,1)S(1)}, u32[]{:S(2)}, u32[]{:S(2)}) async-start(bf16[4,128,896]{2,1,0:T(8,128)(2,1)} %bitcast.4), calls=%async_computation.1 | async-start | bytes 1835008 | tf_op jit(solution)/shard_map/all_to_all | solution.py:445
  95.9 13.5 %collective-permute-start.14 = (bf16[2,64,512]{2,1,0:T(8,128)(2,1)S(1)}, bf16[2,64,512]{2,1,0:T(8,128)(2,1)S(1)}, u32[]{:S(2)}, u32[]{:S(2)}) collective-permute-start(bf16[2,64,512]{2,1,0:T(8,128)(2,1)S(1)} %get-tuple-element.58), channel_id=1, source_target_pairs={{0,3},{1,0},{2,1},{3,2},{4,7},{5,4},{6,5},{7,6},{8,11},{9,8},{10,9... | collective-permute-start | bytes 393224 | tf_op jit(solution)/shard_map/ppermute | solution.py:58
  99.2 10.2 %collective-permute-start.15 = (bf16[2,64,512]{2,1,0:T(8,128)(2,1)S(1)}, bf16[2,64,512]{2,1,0:T(8,128)(2,1)S(1)}, u32[]{:S(2)}, u32[]{:S(2)}) collective-permute-start(bf16[2,64,512]{2,1,0:T(8,128)(2,1)S(1)} %get-tuple-element.57), channel_id=1, source_target_pairs={{0,2},{1,3},{2,0},{3,1},{4,6},{5,7},{6,4},{7,5},{8,10},{9,11},{10,... | collective-permute-start | bytes 393224 | tf_op jit(solution)/shard_map/ppermute | solution.py:58
  122.4 19.1 %collective-permute-start.17 = (bf16[2,64,2048]{2,1,0:T(8,128)(2,1)}, bf16[2,64,2048]{2,1,0:T(8,128)(2,1)S(1)}, u32[]{:S(2)}, u32[]{:S(2)}) collective-permute-start(bf16[2,64,2048]{2,1,0:T(8,128)(2,1)} %get-tuple-element.40.c0), channel_id=1, source_target_pairs={{0,3},{1,0},{2,1},{3,2},{4,7},{5,4},{6,5},{7,6},{8,11},{9,8},{10,9... | collective-permute-start | bytes 1572872 | tf_op jit(solution)/shard_map/ppermute | solution.py:64
  125.7 19.9 %collective-permute-start.18 = (bf16[2,64,2048]{2,1,0:T(8,128)(2,1)}, bf16[2,64,2048]{2,1,0:T(8,128)(2,1)S(1)}, u32[]{:S(2)}, u32[]{:S(2)}) collective-permute-start(bf16[2,64,2048]{2,1,0:T(8,128)(2,1)} %get-tuple-element.40.c0), channel_id=1, source_target_pairs={{0,2},{1,3},{2,0},{3,1},{4,6},{5,7},{6,4},{7,5},{8,10},{9,11},{10,... | collective-permute-start | bytes 1572872 | tf_op jit(solution)/shard_map/ppermute | solution.py:64
  126.7 24.1 %collective-permute-start.19 = (bf16[2,64,2048]{2,1,0:T(8,128)(2,1)}, bf16[2,64,2048]{2,1,0:T(8,128)(2,1)S(1)}, u32[]{:S(2)}, u32[]{:S(2)}) collective-permute-start(bf16[2,64,2048]{2,1,0:T(8,128)(2,1)} %get-tuple-element.40.c0), channel_id=1, source_target_pairs={{0,1},{1,2},{2,3},{3,0},{4,5},{5,6},{6,7},{7,4},{8,9},{9,10},{10,1... | collective-permute-start | bytes 1572872 | tf_op jit(solution)/shard_map/ppermute | solution.py:64
  141.5 21.3 %collective-permute-start.20 = (bf16[64,1792]{1,0:T(8,128)(2,1)}, bf16[64,1792]{1,0:T(8,128)(2,1)S(1)}, u32[]{:S(2)}, u32[]{:S(2)}) collective-permute-start(bf16[64,1792]{1,0:T(8,128)(2,1)} %encoded_back.1), channel_id=1, source_target_pairs={{0,3},{1,0},{2,1},{3,2},{4,7},{5,4},{6,5},{7,6},{8,11},{9,8},{10,9... | collective-permute-start | bytes 688136 | tf_op jit(solution)/shard_map/ppermute | solution.py:64
  144.6 18.2 %collective-permute-start.21 = (bf16[64,1792]{1,0:T(8,128)(2,1)}, bf16[64,1792]{1,0:T(8,128)(2,1)S(1)}, u32[]{:S(2)}, u32[]{:S(2)}) collective-permute-start(bf16[64,1792]{1,0:T(8,128)(2,1)} %encoded_back.1), channel_id=1, source_target_pairs={{0,2},{1,3},{2,0},{3,1},{4,6},{5,7},{6,4},{7,5},{8,10},{9,11},{10,... | collective-permute-start | bytes 688136 | tf_op jit(solution)/shard_map/ppermute | solution.py:64
  145.7 17.1 %collective-permute-start.22 = (bf16[64,1792]{1,0:T(8,128)(2,1)}, bf16[64,1792]{1,0:T(8,128)(2,1)S(1)}, u32[]{:S(2)}, u32[]{:S(2)}) collective-permute-start(bf16[64,1792]{1,0:T(8,128)(2,1)} %encoded_back.1), channel_id=1, source_target_pairs={{0,1},{1,2},{2,3},{3,0},{4,5},{5,6},{6,7},{7,4},{8,9},{9,10},{10,1... | collective-permute-start | bytes 688136 | tf_op jit(solution)/shard_map/ppermute | solution.py:64
  (26 other events, 134.9 us)
Sparse Core Ops, SparseCore 0:
  35.6 62.8 all-gather.4
  100.8 52.4 all-gather.6

commit v3 on v2

--- a/solution.py
+++ b/solution.py
@@ -72,9 +72,23 @@
     half = shard.shape[0] // 2
     next_one = lax.ppermute(shard, axis, down)
     last_one = lax.ppermute(shard, axis, up)
-    top = lax.ppermute(next_one[:half], axis, down)
-    bottom = lax.ppermute(last_one[half:], axis, up)
-    return [shard, next_one, top, bottom, last_one]
+    far_top = lax.ppermute(next_one[:half], axis, down)
+    far_bottom = lax.ppermute(last_one[half:], axis, up)
+    return [shard, next_one, far_top, far_bottom, last_one]
+
+
+def spread_halves(shard, axis="tensor"):
+    down = [(i, (i - 1) % 4) for i in range(4)]
+    up = [(i, (i + 1) % 4) for i in range(4)]
+    half = shard.shape[0] // 2
+    top, bottom = shard[:half], shard[half:]
+    next_top = lax.ppermute(top, axis, down)
+    last_bottom = lax.ppermute(bottom, axis, up)
+    next_bottom = lax.ppermute(bottom, axis, down)
+    last_top = lax.ppermute(top, axis, up)
+    far_top = lax.ppermute(next_top, axis, down)
+    far_bottom = lax.ppermute(last_bottom, axis, up)
+    return [shard, next_top, next_bottom, far_top, far_bottom, last_top, last_bottom]
 
 
 def after(value, earlier):
@@ -108,21 +122,20 @@
         ref[...] = total_ref[pl.ds(start, length), :].astype(BF16)
 
 
-def project_kernel(dims, shift, s_ref, p0, p1, top, bottom, p3, weight_ref, *rest):
-    out_ref, total_ref = rest[-2:]
+def project_kernel(dims, shift, counts, s_ref, *refs):
+    out_ref, total_ref = refs[-2:]
+    weight_ref = refs[sum(counts)]
+    rest = refs[sum(counts) + 1 :]
     step = pl.program_id(0)
-    half = top.shape[0]
-    for k, ref in ((0, p0), (1, p1), (3, p3)):
+    for k, size in enumerate(counts):
+        first = sum(counts[:k])
+        parts = refs[first : first + size]
 
         @pl.when(step == k)
-        def _(ref=ref, k=k):
-            term = dot(ref[...], weight_ref[...], dims)
+        def _(parts=parts, k=k):
+            part = jnp.concatenate([ref[...] for ref in parts], axis=0)
+            term = dot(part, weight_ref[...], dims)
             total_ref[...] = term if k == 0 else total_ref[...] + term
-
-    @pl.when(step == 2)
-    def _():
-        total_ref[:half, :] += dot(top[...], weight_ref[...], dims)
-        total_ref[half:, :] += dot(bottom[...], weight_ref[...], dims)
 
     @pl.when(step == pl.num_programs(0) - 1)
     def _():
@@ -382,10 +395,8 @@
     weight_parts = exchange(jnp.concatenate([kv_part, wq_part, wo_part], axis=1), here)
     kv_parts = jnp.stack([part[: 2 * SLICE] for part in weight_parts])
     qo_parts = jnp.stack([part[2 * SLICE :] for part in weight_parts])
-    hidden_parts = spread_ring(hidden)
+    hidden_parts = spread_halves(hidden)
     cot_parts = spread_ring(cotangent)
-    near = (hidden_parts[1], hidden_parts[4])
-    kv_all = lax.all_gather(after(kv_parts, near), "dp", axis=0)
 
     def weight_spec(index):
         return pl.BlockSpec((n_dp, 1, SLICE, head_width), lambda g, s: (0, g, index, 0))
@@ -401,17 +412,19 @@
         [pltpu.VMEM((tokens, 2 * enc_width), F32)],
         20,
     )(scalars, hidden, cond_weight)
+    ahead = (hidden_parts[1], hidden_parts[6], own_cond)
+    kv_all = lax.all_gather(after(kv_parts, ahead), "dp", axis=0)
     cond_parts = [own_cond] + [
         lax.ppermute(array, "tensor", [(i, (i - k) % n_tensor) for i in range(n_tensor)])
         for k, array in enumerate(to_send, 1)
     ]
 
-    def projected(parts, weight, dims, weight_block, weight_map, name, before=None):
+    def projected(parts, counts, weight, dims, weight_block, weight_map, name, before=None):
         out = (tokens, head_width)
         if before is not None:
             out = (blocks, 2, block_len, head_width)
         return call(
-            functools.partial(project_kernel, dims, shift),
+            functools.partial(project_kernel, dims, shift, counts),
             name,
             n_tensor,
             [whole(*part.shape) for part in parts]
@@ -425,6 +438,7 @@
 
     query = projected(
         hidden_parts,
+        (1, 2, 2, 2),
         query_weight,
         PLAIN,
         (part_width, head_width),
@@ -447,7 +461,8 @@
 
     qo_all = lax.all_gather(after(qo_parts, items), "dp", axis=0)
     query_d_ctx = projected(
-        after(tuple(cot_parts), (items, cond_parts[1:])),
+        after(cot_parts, (items, cond_parts[1:])),
+        (1, 1, 2, 1),
         out_weight,
         ROWS_T,
         (head_width, part_width),

time: 177 us -> 175 us (0.989)
  waiting for transfers between devices: 33.8 us -> 21.3 us
  local copies, waits for them, and re-layouts: 21.7 us -> 28.8 us
  starting transfers between devices: 44 us -> 50.7 us
  Pallas kernels: 53.4 us -> 50.9 us
    ppermute x6, waiting for transfers between devices: 15.8 us -> 0.02 us  [exchange(): lax.ppermute(piece, axis, [(i, (i - k) % size) for i in range(size)])]
    ppermute x4 -> x8, starting transfers between devices: 4.19 us -> 15.2 us  [the longest x1 4.04 us: spread_halves(): next_top = lax.ppermute(top, axis, down)]
    unnamed x53 -> x65, local copies, waits for them, and re-layouts: 14.6 us -> 18.9 us
    all_to_all x1, waiting for transfers between devices: 0.01 us -> 3.98 us  [shards(): x = lax.all_to_all(items, 'tensor', split_axis=0, concat_axis=0, tiled=True)]
    ppermute x4 -> x8, waiting for transfers between devices: 0.01 us -> 3.88 us  [the longest x1 1.67 us: spread_halves(): far_top = lax.ppermute(next_top, axis, down)]
    ppermute x2 -> x1, waiting for transfers between devices: 9.87 us -> 6.48 us  [spread_ring(): next_one = lax.ppermute(shard, axis, down)]
    ppermute x2 -> x1, starting transfers between devices: 3.64 us -> 0.33 us  [spread_ring(): last_one = lax.ppermute(shard, axis, up)]
    all_gather x1, waiting for transfers between devices: 2.51 us -> 0.01 us  [shards(): qo_all = lax.all_gather(after(qo_parts, items), 'dp', axis=0)]
  transfers between devices with their start and end apart: 27 -> 29, of which waited for: 6 -> 9; matrix products, arithmetic and copies ran while one was open for 5% -> 8% of each run, Pallas kernels for 31% -> 29%
where the time goes in v3:
time: 175 us; the launch traced here: 174 us
  Pallas kernels  50.9 us (29%)
  starting transfers between devices  50.7 us (29%)
  local copies, waits for them, and re-layouts  28.8 us (16%)
  waiting for transfers between devices  21.3 us (12%)
  between operations  14.5 us (8%)
  matrix products  4.19 us (2%)
  other arithmetic  3.18 us (2%)
    unnamed x65, local copies, waits for them, and re-layouts  18.9 us
    pallas_call x1, Pallas kernels, shards(): call(encoded_back_kernel, 'encoded_back', n_tensor, [group(head_rows, row...  14.6 us
    pallas_call x1, Pallas kernels, shards(): call(attention_kernel, 'attention', n_tensor, [r_spec, weight_spec(0), we...  12.2 us
    pallas_call x1, Pallas kernels, shards(): call(functools.partial(outputs_kernel, shift), 'outputs', n_tensor, [both...  9.5 us
    ppermute x6, starting transfers between devices, exchange(): lax.ppermute(piece, axis, [(i, (i - k) % size) for i in range(size)])  9.21 us
    ppermute x6, starting transfers between devices, spread(): lax.ppermute(shard, axis, [(i, (i - k) % size) for i in range(size)])  7.79 us
    all_to_all x1, starting transfers between devices, shards(): lax.all_to_all(neighbours, 'dp', split_axis=0, concat_axis=0, tiled=True)  7.7 us
    pallas_call x1, Pallas kernels, shards(): call(encode_kernel, 'encode', 1, [r_spec] + [c_spec] * 4 + [w_spec] * 2,...  7.58 us
  transfers between devices with their start and end apart: 29, of which 9 were waited for; matrix products, arithmetic and copies ran while one was open for 8% of the time, Pallas kernels for 29%

profile of v3, /device:TPU:10, one launch (start us, length us, event | category | flops | bytes accessed | tf_op | source)
XLA Modules:
  0.0 173.6 jit_solution(7654764920784934023)
XLA Ops:
  9.0 4.0 %collective-permute-start = (bf16[128,1024]{1,0:T(8,128)(2,1)}, bf16[128,1024]{1,0:T(8,128)(2,1)S(1)}, u32[]{:S(2)}, u32[]{:S(2)}) collective-permute-start(bf16[128,1024]{1,0:T(8,128)(2,1)} %get-tuple-element.64), channel_id=1, source_target_pairs={{0,3},{1,0},{2,1},{3,2},{4,7},{5,4},{6,5},{7,6},{8,11},{9,8},{10,9... | collective-permute-start | bytes 786440 | tf_op jit(solution)/shard_map/ppermute | solution.py:85
  15.9 3.3 %collective-permute-start.13 = (bf16[128,512]{1,0:T(8,128)(2,1)S(1)}, bf16[128,512]{1,0:T(8,128)(2,1)S(1)}, u32[]{:S(2)}, u32[]{:S(2)}) collective-permute-start(bf16[128,512]{1,0:T(8,128)(2,1)S(1)} %get-tuple-element.60), channel_id=1, source_target_pairs={{0,3},{1,0},{2,1},{3,2},{4,7},{5,4},{6,5},{7,6},{8,11},{9,8},{10,9... | collective-permute-start | bytes 393224 | tf_op jit(solution)/shard_map/ppermute | solution.py:58
  30.1 7.7 %all-to-all-start = ((bf16[32,32,896]{2,1,0:T(8,128)(2,1)}), bf16[32,32,896]{2,1,0:T(8,128)(2,1)}, u32[]{:S(2)}, u32[]{:S(2)}) async-start(bf16[32,32,896]{2,1,0:T(8,128)(2,1)} %param.16), calls=%async_computation | async-start | bytes 3670016 | tf_op jit(solution)/shard_map/all_to_all | solution.py:454
  37.9 2.4 %collective-permute-start.6 = (bf16[256,1024]{1,0:T(8,128)(2,1)S(1)}, bf16[256,1024]{1,0:T(8,128)(2,1)S(1)}, u32[]{:S(2)}, u32[]{:S(2)}) collective-permute-start(bf16[256,1024]{1,0:T(8,128)(2,1)S(1)} %copy-done.5), channel_id=1, source_target_pairs={{0,3},{1,0},{2,1},{3,2},{4,7},{5,4},{6,5},{7,6},{8,11},{9,8},{10,9... | collective-permute-start | bytes 1572872 | tf_op jit(solution)/shard_map/ppermute | solution.py:73
  40.6 2.9 %collective-permute-start.1 = (bf16[128,1024]{1,0:T(8,128)(2,1)S(1)}, bf16[128,1024]{1,0:T(8,128)(2,1)S(1)}, u32[]{:S(2)}, u32[]{:S(2)}) collective-permute-start(bf16[128,1024]{1,0:T(8,128)(2,1)S(1)} %get-tuple-element.63), channel_id=1, source_target_pairs={{0,3},{1,0},{2,1},{3,2},{4,7},{5,4},{6,5},{7,6},{8,11},{9,8},{10,9... | collective-permute-start | bytes 786440 | tf_op jit(solution)/shard_map/ppermute | solution.py:87
  43.5 3.2 %collective-permute-start.2 = (bf16[128,1024]{1,0:T(8,128)(2,1)S(1)}, bf16[128,1024]{1,0:T(8,128)(2,1)S(1)}, u32[]{:S(2)}, u32[]{:S(2)}) collective-permute-start(bf16[128,1024]{1,0:T(8,128)(2,1)S(1)} %collective-permute-done.refs_1_), channel_id=1, source_target_pairs={{0,3},{1,0},{2,1},{3,2},{4,7},{5,4},{6,5},{7,6},{8,11},{9,8},{10,9... | collective-permute-start | bytes 786440 | tf_op jit(solution)/shard_map/ppermute | solution.py:89
  46.7 6.5 %collective-permute-done.6.refs_1_ = bf16[256,1024]{1,0:T(8,128)(2,1)S(1)} collective-permute-done((bf16[256,1024]{1,0:T(8,128)(2,1)S(1)}, bf16[256,1024]{1,0:T(8,128)(2,1)S(1)}, u32[]{:S(2)}, u32[]{:S(2)}) %collective-permute-start.6) | collective-permute-done | bytes 524320 | tf_op jit(solution)/shard_map/ppermute | solution.py:73
  53.2 2.1 %collective-permute-start.4 = (bf16[128,1024]{1,0:T(8,128)(2,1)S(1)}, bf16[128,1024]{1,0:T(8,128)(2,1)S(1)}, u32[]{:S(2)}, u32[]{:S(2)}) collective-permute-start(bf16[128,1024]{1,0:T(8,128)(2,1)S(1)} %collective-permute-done.3.refs_6_), channel_id=1, source_target_pairs={{0,1},{1,2},{2,3},{3,0},{4,5},{5,6},{6,7},{7,4},{8,9},{9,10},{10,1... | collective-permute-start | bytes 786440 | tf_op jit(solution)/shard_map/ppermute | solution.py:90
  65.2 2.1 %collective-permute-start.11 = (bf16[64,1792]{1,0:T(8,128)(2,1)}, bf16[64,1792]{1,0:T(8,128)(2,1)}, u32[]{:S(2)}, u32[]{:S(2)}) collective-permute-start(bf16[64,1792]{1,0:T(8,128)(2,1)} %copy-done.17), channel_id=1, source_target_pairs={{0,2},{1,3},{2,0},{3,1},{4,6},{5,7},{6,4},{7,5},{8,10},{9,11},{10,... | collective-permute-start | bytes 688136 | tf_op jit(solution)/shard_map/ppermute | solution.py:418
  71.4 2.2 %copy-done.2 = bf16[4096,512]{1,0:T(8,128)(2,1)S(1)} copy-done((bf16[4096,512]{1,0:T(8,128)(2,1)S(1)}, bf16[4096,512]{1,0:T(8,128)(2,1)}, u32[]{:S(2)}) %copy-start.2) | copy-done | bytes 4194328
  77.5 2.4 %query.1.refs_6_ = bf16[256,512]{1,0:T(8,128)(2,1)S(1)} custom-call(s32[2]{0:T(128)S(1)} %pad_add_fusion.s_ref, bf16[256,1024]{1,0:T(8,128)(2,1)S(1)} %copy-done, bf16[128,1024]{1,0:T(8,128)(2,1)S(1)} %collective-permute-done.refs_1_, bf16[128,1024]{1,0:T(8,128)(2,1)S(1)} %copy-done.7, bf16[128,1024]{1,0:T(8,128)(2,1)S(1)} %copy-done.11, ...), custom_call_target="tpu_custom_call" | custom-call | tf_op jit(solution)/shard_map/query/pallas_call | solution.py:426
  79.9 2.1 %collective-permute-done.12.c3 = bf16[64,1792]{1,0:T(8,128)(2,1)} collective-permute-done((bf16[64,1792]{1,0:T(8,128)(2,1)}, bf16[64,1792]{1,0:T(8,128)(2,1)}, u32[]{:S(2)}, u32[]{:S(2)}) %collective-permute-start.12) | collective-permute-done | bytes 229408 | tf_op jit(solution)/shard_map/ppermute | solution.py:418
  82.1 2.2 %fusion.2 = bf16[16,32,896]{2,0,1:T(8,128)(2,1)S(1)} fusion(bf16[32,32,896]{2,1,0:T(8,128)(2,1)} %all-to-all-done, s32[16]{0:T(128)S(1)} %eq.24, pred[16]{0:T(512)(128)(4,1)S(1)} %lt.78), kind=kOutput, calls=%fused_computation.2 | convolution fusion | flops 29819904 | bytes 2752592 | tf_op jit(solution)/shard_map/si,sre->ire/dot_general | solution.py:455
  85.5 4.2 %all-to-all-start.1 = ((bf16[4,128,896]{2,1,0:T(8,128)(2,1)}), bf16[4,128,896]{2,1,0:T(8,128)(2,1)}, u32[]{:S(2)}, u32[]{:S(2)}) async-start(bf16[4,128,896]{2,1,0:T(8,128)(2,1)} %bitcast.4), calls=%async_computation.1 | async-start | bytes 1835008 | tf_op jit(solution)/shard_map/all_to_all | solution.py:459
  89.8 2.2 %copy-done.1 = bf16[512,4096]{1,0:T(8,128)(2,1)S(1)} copy-done((bf16[512,4096]{1,0:T(8,128)(2,1)S(1)}, bf16[512,4096]{1,0:T(8,128)(2,1)}, u32[]{:S(2)}) %copy-start.1) | copy-done | bytes 4194328
  92.0 2.9 %d_ctx.1 = bf16[4,2,64,512]{3,2,1,0:T(8,128)(2,1)S(1)} custom-call(s32[2]{0:T(128)S(1)} %pad_add_fusion.s_ref, bf16[256,1024]{1,0:T(8,128)(2,1)S(1)} %copy-done.5, bf16[256,1024]{1,0:T(8,128)(2,1)S(1)} %collective-permute-done.6.refs_1_, bf16[128,1024]{1,0:T(8,128)(2,1)S(1)} %collective-permute-done.7.refs_2_, ...), custom_call_target="tpu_custom_call" | custom-call | tf_op jit(solution)/shard_map/d_ctx/pallas_call | solution.py:426
  95.6 3.2 %collective-permute-start.16 = (bf16[2,64,512]{2,1,0:T(8,128)(2,1)S(1)}, bf16[2,64,512]{2,1,0:T(8,128)(2,1)S(1)}, u32[]{:S(2)}, u32[]{:S(2)}) collective-permute-start(bf16[2,64,512]{2,1,0:T(8,128)(2,1)S(1)} %get-tuple-element.58), channel_id=1, source_target_pairs={{0,3},{1,0},{2,1},{3,2},{4,7},{5,4},{6,5},{7,6},{8,11},{9,8},{10,9... | collective-permute-start | bytes 393224 | tf_op jit(solution)/shard_map/ppermute | solution.py:58
  100.6 4.0 %all-to-all-done.1 = bf16[4,128,896]{2,1,0:T(8,128)(2,1)} async-done(((bf16[4,128,896]{2,1,0:T(8,128)(2,1)}), bf16[4,128,896]{2,1,0:T(8,128)(2,1)}, u32[]{:S(2)}, u32[]{:S(2)}) %all-to-all-start.1) | async-done | bytes 917536 | tf_op jit(solution)/shard_map/all_to_all | solution.py:459
  104.6 7.6 %encode.1 = (bf16[64,1792]{1,0:T(8,128)(2,1)}, bf16[512,896]{1,0:T(8,128)(2,1)}, f32[448,512]{1,0:T(8,128)}, bf16[512,896]{1,0:T(8,128)(2,1)}) custom-call(s32[2]{0:T(128)} %copy-done.15, bf16[512,896]{1,0:T(8,128)(2,1)} %bitcast.5.x_ref, bf16[64,1792]{1,0:T(8,128)(2,1)} %copy-done.14, bf16[64,1792]{1,0:T(8,128)(2,1)} %collective-permute-done.10.c1, ...), custom_call_target="tpu_custom_call" | custom-call | tf_op jit(solution)/shard_map/encode/pallas_call | solution.py:479
  112.9 12.2 %attention.1 = (bf16[4,256,512]{2,1,0:T(8,128)(2,1)}, bf16[4,256,512]{2,1,0:T(8,128)(2,1)}, bf16[2,64,2048]{2,1,0:T(8,128)(2,1)}) custom-call(s32[2]{0:T(128)} %copy-done.15, bf16[512,896]{1,0:T(8,128)(2,1)} %get-tuple-element.33.encoded_ref, bf16[32,4,64,512]{3,2,1,0:T(8,128)(2,1)} %bitcast.55, bf16[32,4,64,512]{3,2,1,0:T(8,128)(2,1)} %bitcast.56, ...), custom_call_target="tpu_custom_call" | custom-call | tf_op jit(solution)/shard_map/attention/pallas_call | solution.py:498
  128.2 14.6 %encoded_back.1 = bf16[64,1792]{1,0:T(8,128)(2,1)} custom-call(s32[2]{0:T(128)} %copy-done.15, bf16[4,256,512]{2,1,0:T(8,128)(2,1)} %get-tuple-element.44.d_scores_ref, bf16[4,256,512]{2,1,0:T(8,128)(2,1)} %get-tuple-element.45.probs_ref, bf16[2,64,512]{2,1,0:T(8,128)(2,1)} %get-tuple-element.59.q0, bf16[2,64,512]{2,1,0:T(8,128)(2,1)} %copy-done.20, ...), custom_call_target="tpu_custom_call" | custom-call | tf_op jit(solution)/shard_map/encoded_back/pallas_call | solution.py:518
  142.8 3.0 %collective-permute-start.22 = (bf16[64,1792]{1,0:T(8,128)(2,1)}, bf16[64,1792]{1,0:T(8,128)(2,1)S(1)}, u32[]{:S(2)}, u32[]{:S(2)}) collective-permute-start(bf16[64,1792]{1,0:T(8,128)(2,1)} %encoded_back.1), channel_id=1, source_target_pairs={{0,3},{1,0},{2,1},{3,2},{4,7},{5,4},{6,5},{7,6},{8,11},{9,8},{10,9... | collective-permute-start | bytes 688136 | tf_op jit(solution)/shard_map/ppermute | solution.py:64
  147.5 4.6 %collective-permute-done.21.c3 = bf16[2,64,2048]{2,1,0:T(8,128)(2,1)S(1)} collective-permute-done((bf16[2,64,2048]{2,1,0:T(8,128)(2,1)}, bf16[2,64,2048]{2,1,0:T(8,128)(2,1)S(1)}, u32[]{:S(2)}, u32[]{:S(2)}) %collective-permute-start.21) | collective-permute-done | bytes 524320 | tf_op jit(solution)/shard_map/ppermute | solution.py:64
  152.9 9.5 %outputs.1 = (bf16[256,1024]{1,0:T(8,128)(2,1)}, f32[256,1024]{1,0:T(8,128)}) custom-call(s32[2]{0:T(128)} %copy-done.15, bf16[2,64,2048]{2,1,0:T(8,128)(2,1)} %get-tuple-element.40.c0, bf16[2,64,2048]{2,1,0:T(8,128)(2,1)} %copy-done.23, bf16[2,64,2048]{2,1,0:T(8,128)(2,1)} %copy-done.24, bf16[2,64,2048]{2,1,0:T(8,128)(2,1)} %copy-done.25, ...), custom_call_target="tpu_custom_call" | custom-call | tf_op jit(solution)/shard_map/outputs/pallas_call | solution.py:545
  (137 shorter events, 48.0 us)
Async XLA Ops:
  7.2 105.1 %all-gather.5.cloned.1.call-start = ((), (), s32[]{:S(2)}) async-start(), calls=%async_computation.2 | async-start | bytes 8650752 | tf_op jit(solution)/shard_map/all_gather | solution.py:416
  9.0 21.1 %collective-permute-start = (bf16[128,1024]{1,0:T(8,128)(2,1)}, bf16[128,1024]{1,0:T(8,128)(2,1)S(1)}, u32[]{:S(2)}, u32[]{:S(2)}) collective-permute-start(bf16[128,1024]{1,0:T(8,128)(2,1)} %get-tuple-element.64), channel_id=1, source_target_pairs={{0,3},{1,0},{2,1},{3,2},{4,7},{5,4},{6,5},{7,6},{8,11},{9,8},{10,9... | collective-permute-start | bytes 786440 | tf_op jit(solution)/shard_map/ppermute | solution.py:85
  13.0 17.1 %collective-permute-start.3 = (bf16[128,1024]{1,0:T(8,128)(2,1)S(1)}, bf16[128,1024]{1,0:T(8,128)(2,1)S(1)}, u32[]{:S(2)}, u32[]{:S(2)}) collective-permute-start(bf16[128,1024]{1,0:T(8,128)(2,1)S(1)} %get-tuple-element.63), channel_id=1, source_target_pairs={{0,1},{1,2},{2,3},{3,0},{4,5},{5,6},{6,7},{7,4},{8,9},{9,10},{10,1... | collective-permute-start | bytes 786440 | tf_op jit(solution)/shard_map/ppermute | solution.py:86
  30.1 52.0 %all-to-all-start = ((bf16[32,32,896]{2,1,0:T(8,128)(2,1)}), bf16[32,32,896]{2,1,0:T(8,128)(2,1)}, u32[]{:S(2)}, u32[]{:S(2)}) async-start(bf16[32,32,896]{2,1,0:T(8,128)(2,1)} %param.16), calls=%async_computation | async-start | bytes 3670016 | tf_op jit(solution)/shard_map/all_to_all | solution.py:454
  37.9 114.2 %all-gather.7.cloned.1.call-start = ((), (), s32[]{:S(2)}) async-start(), calls=%async_computation.3 | async-start | bytes 8650752 | tf_op jit(solution)/shard_map/all_gather | solution.py:462
  37.9 15.3 %collective-permute-start.6 = (bf16[256,1024]{1,0:T(8,128)(2,1)S(1)}, bf16[256,1024]{1,0:T(8,128)(2,1)S(1)}, u32[]{:S(2)}, u32[]{:S(2)}) collective-permute-start(bf16[256,1024]{1,0:T(8,128)(2,1)S(1)} %copy-done.5), channel_id=1, source_target_pairs={{0,3},{1,0},{2,1},{3,2},{4,7},{5,4},{6,5},{7,6},{8,11},{9,8},{10,9... | collective-permute-start | bytes 1572872 | tf_op jit(solution)/shard_map/ppermute | solution.py:73
  40.3 16.0 %collective-permute-start.8 = (bf16[256,1024]{1,0:T(8,128)(2,1)S(1)}, bf16[256,1024]{1,0:T(8,128)(2,1)S(1)}, u32[]{:S(2)}, u32[]{:S(2)}) collective-permute-start(bf16[256,1024]{1,0:T(8,128)(2,1)S(1)} %copy-done.5), channel_id=1, source_target_pairs={{0,1},{1,2},{2,3},{3,0},{4,5},{5,6},{6,7},{7,4},{8,9},{9,10},{10,1... | collective-permute-start | bytes 1572872 | tf_op jit(solution)/shard_map/ppermute | solution.py:74
  40.6 18.2 %collective-permute-start.1 = (bf16[128,1024]{1,0:T(8,128)(2,1)S(1)}, bf16[128,1024]{1,0:T(8,128)(2,1)S(1)}, u32[]{:S(2)}, u32[]{:S(2)}) collective-permute-start(bf16[128,1024]{1,0:T(8,128)(2,1)S(1)} %get-tuple-element.63), channel_id=1, source_target_pairs={{0,3},{1,0},{2,1},{3,2},{4,7},{5,4},{6,5},{7,6},{8,11},{9,8},{10,9... | collective-permute-start | bytes 786440 | tf_op jit(solution)/shard_map/ppermute | solution.py:87
  43.5 18.4 %collective-permute-start.5 = (bf16[128,1024]{1,0:T(8,128)(2,1)}, bf16[128,1024]{1,0:T(8,128)(2,1)S(1)}, u32[]{:S(2)}, u32[]{:S(2)}) collective-permute-start(bf16[128,1024]{1,0:T(8,128)(2,1)} %get-tuple-element.64), channel_id=1, source_target_pairs={{0,1},{1,2},{2,3},{3,0},{4,5},{5,6},{6,7},{7,4},{8,9},{9,10},{10,1... | collective-permute-start | bytes 786440 | tf_op jit(solution)/shard_map/ppermute | solution.py:88
  43.5 21.0 %collective-permute-start.2 = (bf16[128,1024]{1,0:T(8,128)(2,1)S(1)}, bf16[128,1024]{1,0:T(8,128)(2,1)S(1)}, u32[]{:S(2)}, u32[]{:S(2)}) collective-permute-start(bf16[128,1024]{1,0:T(8,128)(2,1)S(1)} %collective-permute-done.refs_1_), channel_id=1, source_target_pairs={{0,3},{1,0},{2,1},{3,2},{4,7},{5,4},{6,5},{7,6},{8,11},{9,8},{10,9... | collective-permute-start | bytes 786440 | tf_op jit(solution)/shard_map/ppermute | solution.py:89
  53.2 14.3 %collective-permute-start.4 = (bf16[128,1024]{1,0:T(8,128)(2,1)S(1)}, bf16[128,1024]{1,0:T(8,128)(2,1)S(1)}, u32[]{:S(2)}, u32[]{:S(2)}) collective-permute-start(bf16[128,1024]{1,0:T(8,128)(2,1)S(1)} %collective-permute-done.3.refs_6_), channel_id=1, source_target_pairs={{0,1},{1,2},{2,3},{3,0},{4,5},{5,6},{6,7},{7,4},{8,9},{9,10},{10,1... | collective-permute-start | bytes 786440 | tf_op jit(solution)/shard_map/ppermute | solution.py:90
  56.3 25.7 %collective-permute-start.7 = (bf16[128,1024]{1,0:T(8,128)(2,1)}, bf16[128,1024]{1,0:T(8,128)(2,1)S(1)}, u32[]{:S(2)}, u32[]{:S(2)}) collective-permute-start(bf16[128,1024]{1,0:T(8,128)(2,1)} %slice.50), channel_id=1, source_target_pairs={{0,3},{1,0},{2,1},{3,2},{4,7},{5,4},{6,5},{7,6},{8,11},{9,8},{10,9... | collective-permute-start | bytes 786440 | tf_op jit(solution)/shard_map/ppermute | solution.py:75
  58.8 23.1 %collective-permute-start.9 = (bf16[128,1024]{1,0:T(8,128)(2,1)}, bf16[128,1024]{1,0:T(8,128)(2,1)S(1)}, u32[]{:S(2)}, u32[]{:S(2)}) collective-permute-start(bf16[128,1024]{1,0:T(8,128)(2,1)} %slice.51), channel_id=1, source_target_pairs={{0,1},{1,2},{2,3},{3,0},{4,5},{5,6},{6,7},{7,4},{8,9},{9,10},{10,1... | collective-permute-start | bytes 786440 | tf_op jit(solution)/shard_map/ppermute | solution.py:76
  62.6 17.3 %collective-permute-start.10 = (bf16[64,1792]{1,0:T(8,128)(2,1)}, bf16[64,1792]{1,0:T(8,128)(2,1)}, u32[]{:S(2)}, u32[]{:S(2)}) collective-permute-start(bf16[64,1792]{1,0:T(8,128)(2,1)} %copy-done.18), channel_id=1, source_target_pairs={{0,3},{1,0},{2,1},{3,2},{4,7},{5,4},{6,5},{7,6},{8,11},{9,8},{10,9... | collective-permute-start | bytes 688136 | tf_op jit(solution)/shard_map/ppermute | solution.py:418
  65.2 14.7 %collective-permute-start.11 = (bf16[64,1792]{1,0:T(8,128)(2,1)}, bf16[64,1792]{1,0:T(8,128)(2,1)}, u32[]{:S(2)}, u32[]{:S(2)}) collective-permute-start(bf16[64,1792]{1,0:T(8,128)(2,1)} %copy-done.17), channel_id=1, source_target_pairs={{0,2},{1,3},{2,0},{3,1},{4,6},{5,7},{6,4},{7,5},{8,10},{9,11},{10,... | collective-permute-start | bytes 688136 | tf_op jit(solution)/shard_map/ppermute | solution.py:418
  68.2 13.7 %collective-permute-start.12 = (bf16[64,1792]{1,0:T(8,128)(2,1)}, bf16[64,1792]{1,0:T(8,128)(2,1)}, u32[]{:S(2)}, u32[]{:S(2)}) collective-permute-start(bf16[64,1792]{1,0:T(8,128)(2,1)} %copy-done.16), channel_id=1, source_target_pairs={{0,1},{1,2},{2,3},{3,0},{4,5},{5,6},{6,7},{7,4},{8,9},{9,10},{10,1... | collective-permute-start | bytes 688136 | tf_op jit(solution)/shard_map/ppermute | solution.py:418
  85.5 19.0 %all-to-all-start.1 = ((bf16[4,128,896]{2,1,0:T(8,128)(2,1)}), bf16[4,128,896]{2,1,0:T(8,128)(2,1)}, u32[]{:S(2)}, u32[]{:S(2)}) async-start(bf16[4,128,896]{2,1,0:T(8,128)(2,1)} %bitcast.4), calls=%async_computation.1 | async-start | bytes 1835008 | tf_op jit(solution)/shard_map/all_to_all | solution.py:459
  95.6 16.5 %collective-permute-start.16 = (bf16[2,64,512]{2,1,0:T(8,128)(2,1)S(1)}, bf16[2,64,512]{2,1,0:T(8,128)(2,1)S(1)}, u32[]{:S(2)}, u32[]{:S(2)}) collective-permute-start(bf16[2,64,512]{2,1,0:T(8,128)(2,1)S(1)} %get-tuple-element.58), channel_id=1, source_target_pairs={{0,3},{1,0},{2,1},{3,2},{4,7},{5,4},{6,5},{7,6},{8,11},{9,8},{10,9... | collective-permute-start | bytes 393224 | tf_op jit(solution)/shard_map/ppermute | solution.py:58
  125.1 17.8 %collective-permute-start.19 = (bf16[2,64,2048]{2,1,0:T(8,128)(2,1)}, bf16[2,64,2048]{2,1,0:T(8,128)(2,1)S(1)}, u32[]{:S(2)}, u32[]{:S(2)}) collective-permute-start(bf16[2,64,2048]{2,1,0:T(8,128)(2,1)} %get-tuple-element.40.c0), channel_id=1, source_target_pairs={{0,3},{1,0},{2,1},{3,2},{4,7},{5,4},{6,5},{7,6},{8,11},{9,8},{10,9... | collective-permute-start | bytes 1572872 | tf_op jit(solution)/shard_map/ppermute | solution.py:64
  126.8 20.7 %collective-permute-start.20 = (bf16[2,64,2048]{2,1,0:T(8,128)(2,1)}, bf16[2,64,2048]{2,1,0:T(8,128)(2,1)S(1)}, u32[]{:S(2)}, u32[]{:S(2)}) collective-permute-start(bf16[2,64,2048]{2,1,0:T(8,128)(2,1)} %get-tuple-element.40.c0), channel_id=1, source_target_pairs={{0,2},{1,3},{2,0},{3,1},{4,6},{5,7},{6,4},{7,5},{8,10},{9,11},{10,... | collective-permute-start | bytes 1572872 | tf_op jit(solution)/shard_map/ppermute | solution.py:64
  128.2 23.8 %collective-permute-start.21 = (bf16[2,64,2048]{2,1,0:T(8,128)(2,1)}, bf16[2,64,2048]{2,1,0:T(8,128)(2,1)S(1)}, u32[]{:S(2)}, u32[]{:S(2)}) collective-permute-start(bf16[2,64,2048]{2,1,0:T(8,128)(2,1)} %get-tuple-element.40.c0), channel_id=1, source_target_pairs={{0,1},{1,2},{2,3},{3,0},{4,5},{5,6},{6,7},{7,4},{8,9},{9,10},{10,1... | collective-permute-start | bytes 1572872 | tf_op jit(solution)/shard_map/ppermute | solution.py:64
  142.8 19.5 %collective-permute-start.22 = (bf16[64,1792]{1,0:T(8,128)(2,1)}, bf16[64,1792]{1,0:T(8,128)(2,1)S(1)}, u32[]{:S(2)}, u32[]{:S(2)}) collective-permute-start(bf16[64,1792]{1,0:T(8,128)(2,1)} %encoded_back.1), channel_id=1, source_target_pairs={{0,3},{1,0},{2,1},{3,2},{4,7},{5,4},{6,5},{7,6},{8,11},{9,8},{10,9... | collective-permute-start | bytes 688136 | tf_op jit(solution)/shard_map/ppermute | solution.py:64
  145.9 16.5 %collective-permute-start.23 = (bf16[64,1792]{1,0:T(8,128)(2,1)}, bf16[64,1792]{1,0:T(8,128)(2,1)S(1)}, u32[]{:S(2)}, u32[]{:S(2)}) collective-permute-start(bf16[64,1792]{1,0:T(8,128)(2,1)} %encoded_back.1), channel_id=1, source_target_pairs={{0,2},{1,3},{2,0},{3,1},{4,6},{5,7},{6,4},{7,5},{8,10},{9,11},{10,... | collective-permute-start | bytes 688136 | tf_op jit(solution)/shard_map/ppermute | solution.py:64
  146.7 15.7 %collective-permute-start.24 = (bf16[64,1792]{1,0:T(8,128)(2,1)}, bf16[64,1792]{1,0:T(8,128)(2,1)S(1)}, u32[]{:S(2)}, u32[]{:S(2)}) collective-permute-start(bf16[64,1792]{1,0:T(8,128)(2,1)} %encoded_back.1), channel_id=1, source_target_pairs={{0,1},{1,2},{2,3},{3,0},{4,5},{5,6},{6,7},{7,4},{8,9},{9,10},{10,1... | collective-permute-start | bytes 688136 | tf_op jit(solution)/shard_map/ppermute | solution.py:64
  (34 other events, 253.1 us)
Sparse Core Ops, SparseCore 0:
  30.2 64.7 all-gather.4
  97.3 52.3 all-gather.6

commit v4 on v3

--- a/solution.py
+++ b/solution.py
@@ -123,9 +123,9 @@
 
 
 def project_kernel(dims, shift, counts, s_ref, *refs):
-    out_ref, total_ref = refs[-2:]
+    total_ref = refs[-1]
     weight_ref = refs[sum(counts)]
-    rest = refs[sum(counts) + 1 :]
+    rest = refs[sum(counts) + 1 : -1]
     step = pl.program_id(0)
     for k, size in enumerate(counts):
         first = sum(counts[:k])
@@ -142,15 +142,16 @@
         rows = total_ref.shape[0]
         moved = pltpu.roll(total_ref[...], rows - shift, 0)
         index = lax.broadcasted_iota(jnp.int32, moved.shape, 0)
-        result = jnp.where(index < rows - shift, moved, 0.0).astype(BF16)
-        if len(rest) == 2:
-            out_ref[...] = result
+        result = jnp.where(index < rows - shift, moved, 0.0)
+        if len(rest) == 1:
+            rest[0][...] = result.astype(BF16)
         else:
-            blocks, _, length, _ = out_ref.shape
-            for block in range(blocks):
-                span = slice(block * length, (block + 1) * length)
-                out_ref[block, 0] = rest[0][span, :]
-                out_ref[block, 1] = result[span, :]
+            total_ref[...] = result
+            for k, ref in enumerate(rest[1:]):
+                length = ref.shape[1]
+                start = pl.multiple_of(((s_ref[0] + 4 - k) % 4) * length, length)
+                ref[0] = rest[0][pl.ds(start, length), :]
+                ref[1] = total_ref[pl.ds(start, length), :].astype(BF16)
 
 
 def encode_kernel(
@@ -218,8 +219,8 @@
     length = out_ref.shape[1]
     pick((q0, q1, q2, q3), query_ref, d_ctx_ref)
     encoded = encoded_ref[...]
-    keys = dot(encoded, key_w_ref[...].reshape(-1, key_w_ref.shape[3])[:width]).astype(BF16)
-    vals = dot(encoded, val_w_ref[...].reshape(-1, val_w_ref.shape[3])[:width]).astype(BF16)
+    keys = dot(encoded, key_w_ref[...].reshape(width, -1)).astype(BF16)
+    vals = dot(encoded, val_w_ref[...].reshape(width, -1)).astype(BF16)
     count = s_ref[1]
     scores = dot(query_ref[...], keys, ROWS_T) * SCALING
     expd = jnp.where(live_columns(count, scores.shape), jnp.exp(scores), 0.0)
@@ -261,8 +262,8 @@
     pick((q0, q1, q2, q3), query_ref, d_ctx_ref)
     d_keys = dot(d_scores_ref[0], query_ref[...], COLS_T).astype(BF16)
     d_vals = dot(probs_ref[0], d_ctx_ref[...], COLS_T).astype(BF16)
-    term = dot(d_keys, key_w_ref[...].reshape(-1, key_w_ref.shape[3])[:width], ROWS_T)
-    term = term + dot(d_vals, val_w_ref[...].reshape(-1, val_w_ref.shape[3])[:width], ROWS_T)
+    term = dot(d_keys, key_w_ref[...].reshape(width, -1), ROWS_T)
+    term = term + dot(d_vals, val_w_ref[...].reshape(width, -1), ROWS_T)
     term = term.astype(BF16).astype(F32)
 
     @pl.when(step == 0)
@@ -384,19 +385,21 @@
     wo_part = lax.dynamic_slice_in_dim(out_weight, row * (SLICE // 2), SLICE // 2, 0)
     wo_part = wo_part.reshape(SLICE // 2, n_tensor, 2, head_width).transpose(1, 2, 0, 3)
     wo_part = wo_part.reshape(n_tensor, SLICE, head_width)
-    kv_part = jnp.concatenate(
-        [
-            lax.dynamic_slice_in_dim(key_weight, row * SLICE, SLICE, 0),
-            lax.dynamic_slice_in_dim(value_weight, row * SLICE, SLICE, 0),
-        ],
-        axis=0,
-    )
-    kv_part = jnp.broadcast_to(kv_part[None], (n_tensor, 2 * SLICE, head_width))
-    weight_parts = exchange(jnp.concatenate([kv_part, wq_part, wo_part], axis=1), here)
-    kv_parts = jnp.stack([part[: 2 * SLICE] for part in weight_parts])
-    qo_parts = jnp.stack([part[2 * SLICE :] for part in weight_parts])
+    kv_rows = 2 * enc_width // n_dp
+    kv_part = jnp.where(
+        row < n_dp // 2,
+        lax.dynamic_slice_in_dim(key_weight, row % (n_dp // 2) * kv_rows, kv_rows, 0),
+        lax.dynamic_slice_in_dim(value_weight, row % (n_dp // 2) * kv_rows, kv_rows, 0),
+    )
+    kv_part = jnp.broadcast_to(kv_part[None], (n_tensor, kv_rows, head_width))
+    weight_parts = exchange(jnp.concatenate([wq_part, wo_part, kv_part], axis=1), here)
+    qo_parts = jnp.stack([part[: 2 * SLICE] for part in weight_parts])
+    kv_parts = jnp.stack([part[2 * SLICE :] for part in weight_parts])
     hidden_parts = spread_halves(hidden)
     cot_parts = spread_ring(cotangent)
+
+    def kv_spec(index):
+        return pl.BlockSpec((n_dp // 2, 1, kv_rows, head_width), lambda g, s: (index, g, 0, 0))
 
     def weight_spec(index):
         return pl.BlockSpec((n_dp, 1, SLICE, head_width), lambda g, s: (0, g, index, 0))
@@ -419,21 +422,24 @@
         for k, array in enumerate(to_send, 1)
     ]
 
-    def projected(parts, counts, weight, dims, weight_block, weight_map, name, before=None):
-        out = (tokens, head_width)
-        if before is not None:
-            out = (blocks, 2, block_len, head_width)
+    def projected(parts, counts, weight, dims, weight_block, weight_map, name, vmem, before=None):
+        full = whole(tokens, head_width)
+        if before is None:
+            out_specs, out_shape = full, sds((tokens, head_width), BF16)
+        else:
+            out_specs = (whole(2, block_len, head_width),) * n_tensor
+            out_shape = (sds((2, block_len, head_width), BF16),) * n_tensor
         return call(
             functools.partial(project_kernel, dims, shift, counts),
             name,
             n_tensor,
             [whole(*part.shape) for part in parts]
             + [pl.BlockSpec(weight_block, weight_map)]
-            + ([] if before is None else [whole(tokens, head_width)]),
-            whole(*out),
-            sds(out, BF16),
+            + ([] if before is None else [full]),
+            out_specs,
+            out_shape,
             [pltpu.VMEM((tokens, head_width), F32)],
-            16,
+            vmem,
         )(scalars, *parts, weight, *([] if before is None else [before]))
 
     query = projected(
@@ -444,6 +450,7 @@
         (part_width, head_width),
         lambda g, s: ((s[0] + g) % 4, 0),
         "query",
+        60,
     )
 
     live = jnp.arange(slots_per)[None, :] < after(seq_counts, (query, cot_parts[1:], cond_parts[1:]))[:, None]
@@ -460,7 +467,7 @@
     x = x.reshape(rows, enc_width)
 
     qo_all = lax.all_gather(after(qo_parts, items), "dp", axis=0)
-    query_d_ctx = projected(
+    own_query, *to_send = projected(
         after(cot_parts, (items, cond_parts[1:])),
         (1, 1, 2, 1),
         out_weight,
@@ -468,9 +475,13 @@
         (head_width, part_width),
         lambda g, s: (0, (s[0] + g) % 4),
         "d_ctx",
+        16,
         before=query,
     )
-    query_parts = exchange(query_d_ctx, here)
+    query_parts = [own_query] + [
+        lax.ppermute(array, "tensor", [(i, (i - k) % n_tensor) for i in range(n_tensor)])
+        for k, array in enumerate(to_send, 1)
+    ]
 
     c_spec = whole(block_len, 2 * enc_width)
     w_spec = whole(enc_width, enc_width)
@@ -499,7 +510,7 @@
         attention_kernel,
         "attention",
         n_tensor,
-        [r_spec, weight_spec(0), weight_spec(1)] + [q_spec] * 4,
+        [r_spec, kv_spec(0), kv_spec(1)] + [q_spec] * 4,
         (
             group(head_rows, rows),
             group(head_rows, rows),
@@ -521,7 +532,7 @@
         n_tensor,
         [group(head_rows, rows), group(head_rows, rows)]
         + [q_spec] * 4
-        + [weight_spec(0), weight_spec(1), w_spec, p_spec, r_spec, c_spec],
+        + [kv_spec(0), kv_spec(1), w_spec, p_spec, r_spec, c_spec],
         c_spec,
         sds((block_len, 2 * enc_width), BF16),
         [big, big, pltpu.VMEM((rows, enc_width), F32)],

time: 175 us -> 172 us (0.983)
  local copies, waits for them, and re-layouts: 28.8 us -> 16.3 us
  waiting for transfers between devices: 21.3 us -> 32.3 us
  starting transfers between devices: 50.7 us -> 46 us
  Pallas kernels: 50.9 us -> 54.3 us
    unnamed x65 -> x51, local copies, waits for them, and re-layouts: 18.9 us -> 9.47 us
    ppermute x1, waiting for transfers between devices: 0.28 us -> 7.17 us  [spread_ring(): last_one = lax.ppermute(shard, axis, up)]
    ppermute x6 -> x3, starting transfers between devices: 9.21 us -> 4.76 us  [exchange(): lax.ppermute(piece, axis, [(i, (i - k) % size) for i in range(size)])]
    ppermute x3 -> x6, starting transfers between devices: 3.81 us -> 7.85 us  [shards(): lax.ppermute(array, 'tensor', [(i, (i - k) % n_tensor) for i in range(n_t...]
    ppermute x1, waiting for transfers between devices: 0.25 us -> 4.26 us  [spread_halves(): far_bottom = lax.ppermute(last_bottom, axis, up)]
    pallas_call x2, Pallas kernels: 5.34 us -> 8.87 us  [projected(): call(functools.partial(project_kernel, dims, shift, counts), name, n_tens...]
    ppermute x1, waiting for transfers between devices: 6.48 us -> 8.86 us  [spread_ring(): next_one = lax.ppermute(shard, axis, down)]
    ppermute x1, waiting for transfers between devices: 0.01 us -> 2.2 us  [spread_ring(): far_bottom = lax.ppermute(last_one[half:], axis, up)]
  transfers between devices with their start and end apart: 29 -> 29, of which waited for: 9 -> 8; matrix products, arithmetic and copies ran while one was open for 8% -> 6% of each run, Pallas kernels for 29% -> 32%
where the time goes in v4:
time: 172 us; the launch traced here: 171 us
  Pallas kernels  54.3 us (32%)
  starting transfers between devices  46 us (27%)
  waiting for transfers between devices  32.3 us (19%)
  local copies, waits for them, and re-layouts  16.3 us (9%)
  between operations  14.5 us (8%)
  matrix products  4.23 us (2%)
  other arithmetic  3.21 us (2%)
    pallas_call x1, Pallas kernels, shards(): call(encoded_back_kernel, 'encoded_back', n_tensor, [group(head_rows, row...  14.3 us
    pallas_call x1, Pallas kernels, shards(): call(attention_kernel, 'attention', n_tensor, [r_spec, kv_spec(0), kv_spe...  12.2 us
    pallas_call x1, Pallas kernels, shards(): call(functools.partial(outputs_kernel, shift), 'outputs', n_tensor, [both...  9.48 us
    unnamed x51, local copies, waits for them, and re-layouts  9.47 us
    pallas_call x2, Pallas kernels, projected(): call(functools.partial(project_kernel, dims, shift, counts), name, n_tens...  8.87 us
    ppermute x1, waiting for transfers between devices, spread_ring(): next_one = lax.ppermute(shard, axis, down)  8.86 us
    ppermute x6, starting transfers between devices, shards(): lax.ppermute(array, 'tensor', [(i, (i - k) % n_tensor) for i in range(n_t...  7.85 us
    ppermute x6, starting transfers between devices, spread(): lax.ppermute(shard, axis, [(i, (i - k) % size) for i in range(size)])  7.82 us
  transfers between devices with their start and end apart: 29, of which 8 were waited for; matrix products, arithmetic and copies ran while one was open for 6% of the time, Pallas kernels for 32%

profile of v4, /device:TPU:10, one launch (start us, length us, event | category | flops | bytes accessed | tf_op | source)
XLA Modules:
  0.0 170.9 jit_solution(17882101478813686904)
XLA Ops:
  9.1 4.0 %collective-permute-start = (bf16[128,1024]{1,0:T(8,128)(2,1)}, bf16[128,1024]{1,0:T(8,128)(2,1)}, u32[]{:S(2)}, u32[]{:S(2)}) collective-permute-start(bf16[128,1024]{1,0:T(8,128)(2,1)} %get-tuple-element.63), channel_id=1, source_target_pairs={{0,3},{1,0},{2,1},{3,2},{4,7},{5,4},{6,5},{7,6},{8,11},{9,8},{10,9... | collective-permute-start | bytes 786440 | tf_op jit(solution)/shard_map/ppermute | solution.py:85
  16.2 4.7 %collective-permute-start.14 = (bf16[120,512]{1,0:T(8,128)(2,1)S(1)}, bf16[120,512]{1,0:T(8,128)(2,1)S(1)}, u32[]{:S(2)}, u32[]{:S(2)}) collective-permute-start(bf16[120,512]{1,0:T(8,128)(2,1)S(1)} %get-tuple-element.66), channel_id=1, source_target_pairs={{0,2},{1,3},{2,0},{3,1},{4,6},{5,7},{6,4},{7,5},{8,10},{9,11},{10,... | collective-permute-start | bytes 368648 | tf_op jit(solution)/shard_map/ppermute | solution.py:58
  22.3 2.0 %copy-done.2 = bf16[1024,1792]{1,0:T(8,128)(2,1)S(1)} copy-done((bf16[1024,1792]{1,0:T(8,128)(2,1)S(1)}, bf16[1024,1792]{1,0:T(8,128)(2,1)}, u32[]{:S(2)}) %copy-start.2) | copy-done | bytes 3670040
  28.4 7.7 %all-to-all-start = ((bf16[32,32,896]{2,1,0:T(8,128)(2,1)}), bf16[32,32,896]{2,1,0:T(8,128)(2,1)}, u32[]{:S(2)}, u32[]{:S(2)}) async-start(bf16[32,32,896]{2,1,0:T(8,128)(2,1)} %param.16), calls=%async_computation | async-start | bytes 3670016 | tf_op jit(solution)/shard_map/all_to_all | solution.py:461
  42.2 8.9 %collective-permute-done.6.refs_1_ = bf16[256,1024]{1,0:T(8,128)(2,1)S(1)} collective-permute-done((bf16[256,1024]{1,0:T(8,128)(2,1)S(1)}, bf16[256,1024]{1,0:T(8,128)(2,1)S(1)}, u32[]{:S(2)}, u32[]{:S(2)}) %collective-permute-start.6) | collective-permute-done | bytes 524320 | tf_op jit(solution)/shard_map/ppermute | solution.py:73
  52.4 7.2 %collective-permute-done.8.refs_4_ = bf16[256,1024]{1,0:T(8,128)(2,1)S(1)} collective-permute-done((bf16[256,1024]{1,0:T(8,128)(2,1)S(1)}, bf16[256,1024]{1,0:T(8,128)(2,1)S(1)}, u32[]{:S(2)}, u32[]{:S(2)}) %collective-permute-start.8) | collective-permute-done | bytes 524320 | tf_op jit(solution)/shard_map/ppermute | solution.py:74
  62.6 2.3 %collective-permute-start.7 = (bf16[128,1024]{1,0:T(8,128)(2,1)S(1)}, bf16[128,1024]{1,0:T(8,128)(2,1)S(1)}, u32[]{:S(2)}, u32[]{:S(2)}) collective-permute-start(bf16[128,1024]{1,0:T(8,128)(2,1)S(1)} %slice.50), channel_id=1, source_target_pairs={{0,3},{1,0},{2,1},{3,2},{4,7},{5,4},{6,5},{7,6},{8,11},{9,8},{10,9... | collective-permute-start | bytes 786440 | tf_op jit(solution)/shard_map/ppermute | solution.py:75
  64.9 4.3 %collective-permute-done.4.refs_4_ = bf16[128,1024]{1,0:T(8,128)(2,1)} collective-permute-done((bf16[128,1024]{1,0:T(8,128)(2,1)}, bf16[128,1024]{1,0:T(8,128)(2,1)}, u32[]{:S(2)}, u32[]{:S(2)}) %collective-permute-start.4) | collective-permute-done | bytes 262176 | tf_op jit(solution)/shard_map/ppermute | solution.py:90
  70.7 5.9 %query.1.refs_6_ = bf16[256,512]{1,0:T(8,128)(2,1)} custom-call(s32[2]{0:T(128)} %copy-done.8, bf16[256,1024]{1,0:T(8,128)(2,1)} %hidden_ref.3, bf16[128,1024]{1,0:T(8,128)(2,1)} %collective-permute-done.refs_1_, bf16[128,1024]{1,0:T(8,128)(2,1)} %collective-permute-done.1.refs_2_, bf16[128,1024]{1,0:T(8,128)(2,1)} %collective-permute-done.2.refs_3_, ...), custom_call_target="tpu_custom_call" | custom-call | tf_op jit(solution)/shard_map/query/pallas_call | solution.py:432
  77.0 2.2 %collective-permute-done.9.refs_3_ = bf16[128,1024]{1,0:T(8,128)(2,1)S(1)} collective-permute-done((bf16[128,1024]{1,0:T(8,128)(2,1)S(1)}, bf16[128,1024]{1,0:T(8,128)(2,1)S(1)}, u32[]{:S(2)}, u32[]{:S(2)}) %collective-permute-start.9) | collective-permute-done | bytes 262176 | tf_op jit(solution)/shard_map/ppermute | solution.py:76
  79.3 2.3 %fusion.2 = bf16[16,32,896]{2,0,1:T(8,128)(2,1)S(1)} fusion(bf16[32,32,896]{2,1,0:T(8,128)(2,1)} %all-to-all-done, s32[16]{0:T(128)S(1)} %eq.23, pred[16]{0:T(512)(128)(4,1)S(1)} %lt.78), kind=kOutput, calls=%fused_computation.2 | convolution fusion | flops 29819904 | bytes 2752592 | tf_op jit(solution)/shard_map/si,sre->ire/dot_general | solution.py:462
  82.8 4.3 %all-to-all-start.1 = ((bf16[4,128,896]{2,1,0:T(8,128)(2,1)}), bf16[4,128,896]{2,1,0:T(8,128)(2,1)}, u32[]{:S(2)}, u32[]{:S(2)}) async-start(bf16[4,128,896]{2,1,0:T(8,128)(2,1)} %bitcast.53), calls=%async_computation.1 | async-start | bytes 1835008 | tf_op jit(solution)/shard_map/all_to_all | solution.py:466
  87.1 2.3 %copy-done.1 = bf16[512,4096]{1,0:T(8,128)(2,1)S(1)} copy-done((bf16[512,4096]{1,0:T(8,128)(2,1)S(1)}, bf16[512,4096]{1,0:T(8,128)(2,1)}, u32[]{:S(2)}) %copy-start.1) | copy-done | bytes 4194328
  89.4 2.9 %d_ctx.1 = (bf16[2,64,512]{2,1,0:T(8,128)(2,1)S(1)}, bf16[2,64,512]{2,1,0:T(8,128)(2,1)S(1)}, bf16[2,64,512]{2,1,0:T(8,128)(2,1)S(1)}, bf16[2,64,512]{2,1,0:T(8,128)(2,1)S(1)}) custom-call(s32[2]{0:T(128)S(1)} %copy-done.9, bf16[256,1024]{1,0:T(8,128)(2,1)S(1)} %copy-done.4, bf16[256,1024]{1,0:T(8,128)(2,1)S(1)} %collective-permute-done.6.refs_1_, ...), custom_call_target="tpu_custom_call" | custom-call | tf_op jit(solution)/shard_map/d_ctx/pallas_call | solution.py:432
  93.0 3.1 %collective-permute-start.16 = (bf16[2,64,512]{2,1,0:T(8,128)(2,1)S(1)}, bf16[2,64,512]{2,1,0:T(8,128)(2,1)S(1)}, u32[]{:S(2)}, u32[]{:S(2)}) collective-permute-start(bf16[2,64,512]{2,1,0:T(8,128)(2,1)S(1)} %get-tuple-element.45), channel_id=1, source_target_pairs={{0,3},{1,0},{2,1},{3,2},{4,7},{5,4},{6,5},{7,6},{8,11},{9,8},{10,9... | collective-permute-start | bytes 393224 | tf_op jit(solution)/shard_map/ppermute | solution.py:482
  97.8 3.6 %all-to-all-done.1 = bf16[4,128,896]{2,1,0:T(8,128)(2,1)} async-done(((bf16[4,128,896]{2,1,0:T(8,128)(2,1)}), bf16[4,128,896]{2,1,0:T(8,128)(2,1)}, u32[]{:S(2)}, u32[]{:S(2)}) %all-to-all-start.1) | async-done | bytes 917536 | tf_op jit(solution)/shard_map/all_to_all | solution.py:466
  101.5 7.7 %encode.1 = (bf16[64,1792]{1,0:T(8,128)(2,1)}, bf16[512,896]{1,0:T(8,128)(2,1)}, f32[448,512]{1,0:T(8,128)}, bf16[512,896]{1,0:T(8,128)(2,1)}) custom-call(s32[2]{0:T(128)} %copy-done.8, bf16[512,896]{1,0:T(8,128)(2,1)} %bitcast.5.x_ref, bf16[64,1792]{1,0:T(8,128)(2,1)} %copy-done.7, bf16[64,1792]{1,0:T(8,128)(2,1)} %copy-done.17, ...), custom_call_target="tpu_custom_call" | custom-call | tf_op jit(solution)/shard_map/encode/pallas_call | solution.py:490
  110.0 12.2 %attention.1 = (bf16[4,256,512]{2,1,0:T(8,128)(2,1)}, bf16[4,256,512]{2,1,0:T(8,128)(2,1)}, bf16[2,64,2048]{2,1,0:T(8,128)(2,1)}) custom-call(s32[2]{0:T(128)} %copy-done.8, bf16[512,896]{1,0:T(8,128)(2,1)} %get-tuple-element.37.encoded_ref, bf16[32,4,56,512]{3,2,1,0:T(8,128)(2,1)} %bitcast.46, bf16[32,4,56,512]{3,2,1,0:T(8,128)(2,1)} %bitcast.47, ...), custom_call_target="tpu_custom_call" | custom-call | tf_op jit(solution)/shard_map/attention/pallas_call | solution.py:509
  122.1 1.9 %collective-permute-start.19 = (bf16[2,64,2048]{2,1,0:T(8,128)(2,1)}, bf16[2,64,2048]{2,1,0:T(8,128)(2,1)S(1)}, u32[]{:S(2)}, u32[]{:S(2)}) collective-permute-start(bf16[2,64,2048]{2,1,0:T(8,128)(2,1)} %get-tuple-element.48.c0), channel_id=1, source_target_pairs={{0,3},{1,0},{2,1},{3,2},{4,7},{5,4},{6,5},{7,6},{8,11},{9,8},{10,9... | collective-permute-start | bytes 1572872 | tf_op jit(solution)/shard_map/ppermute | solution.py:64
  125.7 14.3 %encoded_back.1 = bf16[64,1792]{1,0:T(8,128)(2,1)} custom-call(s32[2]{0:T(128)} %copy-done.8, bf16[4,256,512]{2,1,0:T(8,128)(2,1)} %get-tuple-element.52.d_scores_ref, bf16[4,256,512]{2,1,0:T(8,128)(2,1)} %get-tuple-element.53.probs_ref, bf16[2,64,512]{2,1,0:T(8,128)(2,1)} %copy-done.6, bf16[2,64,512]{2,1,0:T(8,128)(2,1)} %copy-done.11, ...), custom_call_target="tpu_custom_call" | custom-call | tf_op jit(solution)/shard_map/encoded_back/pallas_call | solution.py:529
  140.0 3.4 %collective-permute-start.22 = (bf16[64,1792]{1,0:T(8,128)(2,1)}, bf16[64,1792]{1,0:T(8,128)(2,1)S(1)}, u32[]{:S(2)}, u32[]{:S(2)}) collective-permute-start(bf16[64,1792]{1,0:T(8,128)(2,1)} %encoded_back.1), channel_id=1, source_target_pairs={{0,3},{1,0},{2,1},{3,2},{4,7},{5,4},{6,5},{7,6},{8,11},{9,8},{10,9... | collective-permute-start | bytes 688136 | tf_op jit(solution)/shard_map/ppermute | solution.py:64
  144.3 5.1 %collective-permute-done.21.c3 = bf16[2,64,2048]{2,1,0:T(8,128)(2,1)S(1)} collective-permute-done((bf16[2,64,2048]{2,1,0:T(8,128)(2,1)}, bf16[2,64,2048]{2,1,0:T(8,128)(2,1)S(1)}, u32[]{:S(2)}, u32[]{:S(2)}) %collective-permute-start.21) | collective-permute-done | bytes 524320 | tf_op jit(solution)/shard_map/ppermute | solution.py:64
  150.2 9.5 %outputs.1 = (bf16[256,1024]{1,0:T(8,128)(2,1)}, f32[256,1024]{1,0:T(8,128)}) custom-call(s32[2]{0:T(128)} %copy-done.8, bf16[2,64,2048]{2,1,0:T(8,128)(2,1)} %get-tuple-element.48.c0, bf16[2,64,2048]{2,1,0:T(8,128)(2,1)} %copy-done.14, bf16[2,64,2048]{2,1,0:T(8,128)(2,1)} %copy-done.15, bf16[2,64,2048]{2,1,0:T(8,128)(2,1)} %copy-done.16, ...), custom_call_target="tpu_custom_call" | custom-call | tf_op jit(solution)/shard_map/outputs/pallas_call | solution.py:556
  162.1 1.9 %fusion.5 = bf16[256,1024]{1,0:T(8,128)(2,1)} fusion(f32[256,1024]{1,0:T(8,128)S(1)} %copy-done.20, bf16[256,1792]{1,0:T(8,128)(2,1)S(1)} %bitcast.54, bf16[1024,1792]{1,0:T(8,128)(2,1)S(1)} %copy-done.3), kind=kOutput, calls=%fused_computation.4 | convolution fusion | flops 940048384 | bytes 6160384 | tf_op jit(solution)/shard_map/dot_general | solution.py:24
  (125 shorter events, 32.6 us)
Async XLA Ops:
  7.2 102.1 %all-gather.5.cloned.1.call-start = ((), (), s32[]{:S(2)}) async-start(), calls=%async_computation.2 | async-start | bytes 7569408 | tf_op jit(solution)/shard_map/all_gather | solution.py:419
  9.1 19.3 %collective-permute-start = (bf16[128,1024]{1,0:T(8,128)(2,1)}, bf16[128,1024]{1,0:T(8,128)(2,1)}, u32[]{:S(2)}, u32[]{:S(2)}) collective-permute-start(bf16[128,1024]{1,0:T(8,128)(2,1)} %get-tuple-element.63), channel_id=1, source_target_pairs={{0,3},{1,0},{2,1},{3,2},{4,7},{5,4},{6,5},{7,6},{8,11},{9,8},{10,9... | collective-permute-start | bytes 786440 | tf_op jit(solution)/shard_map/ppermute | solution.py:85
  13.1 15.2 %collective-permute-start.3 = (bf16[128,1024]{1,0:T(8,128)(2,1)}, bf16[128,1024]{1,0:T(8,128)(2,1)}, u32[]{:S(2)}, u32[]{:S(2)}) collective-permute-start(bf16[128,1024]{1,0:T(8,128)(2,1)} %get-tuple-element.62), channel_id=1, source_target_pairs={{0,1},{1,2},{2,3},{3,0},{4,5},{5,6},{6,7},{7,4},{8,9},{9,10},{10,1... | collective-permute-start | bytes 786440 | tf_op jit(solution)/shard_map/ppermute | solution.py:86
  28.4 50.9 %all-to-all-start = ((bf16[32,32,896]{2,1,0:T(8,128)(2,1)}), bf16[32,32,896]{2,1,0:T(8,128)(2,1)}, u32[]{:S(2)}, u32[]{:S(2)}) async-start(bf16[32,32,896]{2,1,0:T(8,128)(2,1)} %param.16), calls=%async_computation | async-start | bytes 3670016 | tf_op jit(solution)/shard_map/all_to_all | solution.py:461
  36.1 113.3 %all-gather.7.cloned.1.call-start = ((), (), s32[]{:S(2)}) async-start(), calls=%async_computation.3 | async-start | bytes 8650752 | tf_op jit(solution)/shard_map/all_gather | solution.py:469
  36.2 14.9 %collective-permute-start.6 = (bf16[256,1024]{1,0:T(8,128)(2,1)S(1)}, bf16[256,1024]{1,0:T(8,128)(2,1)S(1)}, u32[]{:S(2)}, u32[]{:S(2)}) collective-permute-start(bf16[256,1024]{1,0:T(8,128)(2,1)S(1)} %copy-done.4), channel_id=1, source_target_pairs={{0,3},{1,0},{2,1},{3,2},{4,7},{5,4},{6,5},{7,6},{8,11},{9,8},{10,9... | collective-permute-start | bytes 1572872 | tf_op jit(solution)/shard_map/ppermute | solution.py:73
  36.8 24.1 %collective-permute-start.1 = (bf16[128,1024]{1,0:T(8,128)(2,1)}, bf16[128,1024]{1,0:T(8,128)(2,1)}, u32[]{:S(2)}, u32[]{:S(2)}) collective-permute-start(bf16[128,1024]{1,0:T(8,128)(2,1)} %get-tuple-element.62), channel_id=1, source_target_pairs={{0,3},{1,0},{2,1},{3,2},{4,7},{5,4},{6,5},{7,6},{8,11},{9,8},{10,9... | collective-permute-start | bytes 786440 | tf_op jit(solution)/shard_map/ppermute | solution.py:87
  37.6 24.0 %collective-permute-start.5 = (bf16[128,1024]{1,0:T(8,128)(2,1)}, bf16[128,1024]{1,0:T(8,128)(2,1)}, u32[]{:S(2)}, u32[]{:S(2)}) collective-permute-start(bf16[128,1024]{1,0:T(8,128)(2,1)} %get-tuple-element.63), channel_id=1, source_target_pairs={{0,1},{1,2},{2,3},{3,0},{4,5},{5,6},{6,7},{7,4},{8,9},{9,10},{10,1... | collective-permute-start | bytes 786440 | tf_op jit(solution)/shard_map/ppermute | solution.py:88
  38.8 20.7 %collective-permute-start.8 = (bf16[256,1024]{1,0:T(8,128)(2,1)S(1)}, bf16[256,1024]{1,0:T(8,128)(2,1)S(1)}, u32[]{:S(2)}, u32[]{:S(2)}) collective-permute-start(bf16[256,1024]{1,0:T(8,128)(2,1)S(1)} %copy-done.4), channel_id=1, source_target_pairs={{0,1},{1,2},{2,3},{3,0},{4,5},{5,6},{6,7},{7,4},{8,9},{9,10},{10,1... | collective-permute-start | bytes 1572872 | tf_op jit(solution)/shard_map/ppermute | solution.py:74
  40.4 22.2 %collective-permute-start.2 = (bf16[128,1024]{1,0:T(8,128)(2,1)}, bf16[128,1024]{1,0:T(8,128)(2,1)}, u32[]{:S(2)}, u32[]{:S(2)}) collective-permute-start(bf16[128,1024]{1,0:T(8,128)(2,1)} %collective-permute-done.refs_1_), channel_id=1, source_target_pairs={{0,3},{1,0},{2,1},{3,2},{4,7},{5,4},{6,5},{7,6},{8,11},{9,8},{10,9... | collective-permute-start | bytes 786440 | tf_op jit(solution)/shard_map/ppermute | solution.py:89
  51.1 18.1 %collective-permute-start.4 = (bf16[128,1024]{1,0:T(8,128)(2,1)}, bf16[128,1024]{1,0:T(8,128)(2,1)}, u32[]{:S(2)}, u32[]{:S(2)}) collective-permute-start(bf16[128,1024]{1,0:T(8,128)(2,1)} %collective-permute-done.3.refs_6_), channel_id=1, source_target_pairs={{0,1},{1,2},{2,3},{3,0},{4,5},{5,6},{6,7},{7,4},{8,9},{9,10},{10,1... | collective-permute-start | bytes 786440 | tf_op jit(solution)/shard_map/ppermute | solution.py:90
  59.5 17.2 %collective-permute-start.10 = (bf16[64,1792]{1,0:T(8,128)(2,1)S(1)}, bf16[64,1792]{1,0:T(8,128)(2,1)S(1)}, u32[]{:S(2)}, u32[]{:S(2)}) collective-permute-start(bf16[64,1792]{1,0:T(8,128)(2,1)S(1)} %get-tuple-element.32), channel_id=1, source_target_pairs={{0,3},{1,0},{2,1},{3,2},{4,7},{5,4},{6,5},{7,6},{8,11},{9,8},{10,9... | collective-permute-start | bytes 688136 | tf_op jit(solution)/shard_map/ppermute | solution.py:421
  60.9 15.8 %collective-permute-start.11 = (bf16[64,1792]{1,0:T(8,128)(2,1)S(1)}, bf16[64,1792]{1,0:T(8,128)(2,1)}, u32[]{:S(2)}, u32[]{:S(2)}) collective-permute-start(bf16[64,1792]{1,0:T(8,128)(2,1)S(1)} %get-tuple-element.33), channel_id=1, source_target_pairs={{0,2},{1,3},{2,0},{3,1},{4,6},{5,7},{6,4},{7,5},{8,10},{9,11},{10,... | collective-permute-start | bytes 688136 | tf_op jit(solution)/shard_map/ppermute | solution.py:421
  61.7 15.0 %collective-permute-start.12 = (bf16[64,1792]{1,0:T(8,128)(2,1)S(1)}, bf16[64,1792]{1,0:T(8,128)(2,1)}, u32[]{:S(2)}, u32[]{:S(2)}) collective-permute-start(bf16[64,1792]{1,0:T(8,128)(2,1)S(1)} %get-tuple-element.34), channel_id=1, source_target_pairs={{0,1},{1,2},{2,3},{3,0},{4,5},{5,6},{6,7},{7,4},{8,9},{9,10},{10,1... | collective-permute-start | bytes 688136 | tf_op jit(solution)/shard_map/ppermute | solution.py:421
  62.6 14.4 %collective-permute-start.7 = (bf16[128,1024]{1,0:T(8,128)(2,1)S(1)}, bf16[128,1024]{1,0:T(8,128)(2,1)S(1)}, u32[]{:S(2)}, u32[]{:S(2)}) collective-permute-start(bf16[128,1024]{1,0:T(8,128)(2,1)S(1)} %slice.50), channel_id=1, source_target_pairs={{0,3},{1,0},{2,1},{3,2},{4,7},{5,4},{6,5},{7,6},{8,11},{9,8},{10,9... | collective-permute-start | bytes 786440 | tf_op jit(solution)/shard_map/ppermute | solution.py:75
  82.8 18.7 %all-to-all-start.1 = ((bf16[4,128,896]{2,1,0:T(8,128)(2,1)}), bf16[4,128,896]{2,1,0:T(8,128)(2,1)}, u32[]{:S(2)}, u32[]{:S(2)}) async-start(bf16[4,128,896]{2,1,0:T(8,128)(2,1)} %bitcast.53), calls=%async_computation.1 | async-start | bytes 1835008 | tf_op jit(solution)/shard_map/all_to_all | solution.py:466
  93.0 16.2 %collective-permute-start.16 = (bf16[2,64,512]{2,1,0:T(8,128)(2,1)S(1)}, bf16[2,64,512]{2,1,0:T(8,128)(2,1)S(1)}, u32[]{:S(2)}, u32[]{:S(2)}) collective-permute-start(bf16[2,64,512]{2,1,0:T(8,128)(2,1)S(1)} %get-tuple-element.45), channel_id=1, source_target_pairs={{0,3},{1,0},{2,1},{3,2},{4,7},{5,4},{6,5},{7,6},{8,11},{9,8},{10,9... | collective-permute-start | bytes 393224 | tf_op jit(solution)/shard_map/ppermute | solution.py:482
  96.1 13.1 %collective-permute-start.17 = (bf16[2,64,512]{2,1,0:T(8,128)(2,1)S(1)}, bf16[2,64,512]{2,1,0:T(8,128)(2,1)S(1)}, u32[]{:S(2)}, u32[]{:S(2)}) collective-permute-start(bf16[2,64,512]{2,1,0:T(8,128)(2,1)S(1)} %get-tuple-element.46), channel_id=1, source_target_pairs={{0,2},{1,3},{2,0},{3,1},{4,6},{5,7},{6,4},{7,5},{8,10},{9,11},{10,... | collective-permute-start | bytes 393224 | tf_op jit(solution)/shard_map/ppermute | solution.py:482
  122.1 17.9 %collective-permute-start.19 = (bf16[2,64,2048]{2,1,0:T(8,128)(2,1)}, bf16[2,64,2048]{2,1,0:T(8,128)(2,1)S(1)}, u32[]{:S(2)}, u32[]{:S(2)}) collective-permute-start(bf16[2,64,2048]{2,1,0:T(8,128)(2,1)} %get-tuple-element.48.c0), channel_id=1, source_target_pairs={{0,3},{1,0},{2,1},{3,2},{4,7},{5,4},{6,5},{7,6},{8,11},{9,8},{10,9... | collective-permute-start | bytes 1572872 | tf_op jit(solution)/shard_map/ppermute | solution.py:64
  124.1 20.2 %collective-permute-start.20 = (bf16[2,64,2048]{2,1,0:T(8,128)(2,1)}, bf16[2,64,2048]{2,1,0:T(8,128)(2,1)S(1)}, u32[]{:S(2)}, u32[]{:S(2)}) collective-permute-start(bf16[2,64,2048]{2,1,0:T(8,128)(2,1)} %get-tuple-element.48.c0), channel_id=1, source_target_pairs={{0,2},{1,3},{2,0},{3,1},{4,6},{5,7},{6,4},{7,5},{8,10},{9,11},{10,... | collective-permute-start | bytes 1572872 | tf_op jit(solution)/shard_map/ppermute | solution.py:64
  125.6 23.8 %collective-permute-start.21 = (bf16[2,64,2048]{2,1,0:T(8,128)(2,1)}, bf16[2,64,2048]{2,1,0:T(8,128)(2,1)S(1)}, u32[]{:S(2)}, u32[]{:S(2)}) collective-permute-start(bf16[2,64,2048]{2,1,0:T(8,128)(2,1)} %get-tuple-element.48.c0), channel_id=1, source_target_pairs={{0,1},{1,2},{2,3},{3,0},{4,5},{5,6},{6,7},{7,4},{8,9},{9,10},{10,1... | collective-permute-start | bytes 1572872 | tf_op jit(solution)/shard_map/ppermute | solution.py:64
  140.0 19.7 %collective-permute-start.22 = (bf16[64,1792]{1,0:T(8,128)(2,1)}, bf16[64,1792]{1,0:T(8,128)(2,1)S(1)}, u32[]{:S(2)}, u32[]{:S(2)}) collective-permute-start(bf16[64,1792]{1,0:T(8,128)(2,1)} %encoded_back.1), channel_id=1, source_target_pairs={{0,3},{1,0},{2,1},{3,2},{4,7},{5,4},{6,5},{7,6},{8,11},{9,8},{10,9... | collective-permute-start | bytes 688136 | tf_op jit(solution)/shard_map/ppermute | solution.py:64
  143.4 16.3 %collective-permute-start.23 = (bf16[64,1792]{1,0:T(8,128)(2,1)}, bf16[64,1792]{1,0:T(8,128)(2,1)S(1)}, u32[]{:S(2)}, u32[]{:S(2)}) collective-permute-start(bf16[64,1792]{1,0:T(8,128)(2,1)} %encoded_back.1), channel_id=1, source_target_pairs={{0,2},{1,3},{2,0},{3,1},{4,6},{5,7},{6,4},{7,5},{8,10},{9,11},{10,... | collective-permute-start | bytes 688136 | tf_op jit(solution)/shard_map/ppermute | solution.py:64
  144.1 15.6 %collective-permute-start.24 = (bf16[64,1792]{1,0:T(8,128)(2,1)}, bf16[64,1792]{1,0:T(8,128)(2,1)S(1)}, u32[]{:S(2)}, u32[]{:S(2)}) collective-permute-start(bf16[64,1792]{1,0:T(8,128)(2,1)} %encoded_back.1), channel_id=1, source_target_pairs={{0,1},{1,2},{2,3},{3,0},{4,5},{5,6},{6,7},{7,4},{8,9},{9,10},{10,1... | collective-permute-start | bytes 688136 | tf_op jit(solution)/shard_map/ppermute | solution.py:64
  (27 other events, 154.4 us)
Sparse Core Ops, SparseCore 0:
  28.5 60.9 all-gather.4
  92.4 52.3 all-gather.6

commit v5 on v4

--- a/solution.py
+++ b/solution.py
@@ -120,6 +120,24 @@
     for k, ref in enumerate((c0, c1, c2, c3)):
         start = pl.multiple_of(((s_ref[0] + 4 - k) % 4) * length, length)
         ref[...] = total_ref[pl.ds(start, length), :].astype(BF16)
+
+
+def pick_kernel(slots_ref, stored_ref, out_ref, sems):
+    blocks, length, _ = out_ref.shape
+    tokens = stored_ref.shape[1]
+    per = length // tokens
+    copies = [
+        pltpu.make_async_copy(
+            stored_ref.at[slots_ref[item]],
+            out_ref.at[item // per, pl.ds(item % per * tokens, tokens), :],
+            sems.at[item],
+        )
+        for item in range(blocks * per)
+    ]
+    for copy in copies:
+        copy.start()
+    for copy in copies:
+        copy.wait()
 
 
 def project_kernel(dims, shift, counts, s_ref, *refs):
@@ -292,10 +310,8 @@
         d_cond_ref[...] = jnp.concatenate(d_keys + d_vals, axis=1).astype(BF16)
 
 
-def placed_rows(rows, by, shift):
-    moved = pltpu.roll(rows, by, 0)
-    if shift == 0:
-        return moved
+def shifted_down(rows, shift):
+    moved = pltpu.roll(rows, shift, 0)
     index = lax.broadcasted_iota(jnp.int32, rows.shape, 0)
     return jnp.where(index >= shift, moved, 0.0)
 
@@ -313,6 +329,7 @@
     cotangent_ref,
     mixed_ref,
     grad_ref,
+    rows_ref,
     mixed_sum_ref,
     grad_sum_ref,
 ):
@@ -320,9 +337,11 @@
     half = out_w_ref.shape[2] // 2
     wide = out_w_ref.shape[3]
     length = c0.shape[1]
-    parts = (c0, c1, c2, c3)
-    ctx = jnp.concatenate([ref[0] for ref in parts], axis=0)
-    d_query = jnp.concatenate([ref[1] for ref in parts], axis=0)
+    for k, ref in enumerate((c0, c1, c2, c3)):
+        start = pl.multiple_of(((s_ref[0] + k) % 4) * length, length)
+        rows_ref[:, pl.ds(start, length), :] = ref[...]
+    ctx = rows_ref[0]
+    d_query = rows_ref[1]
 
     @pl.when(step == 0)
     def _():
@@ -336,10 +355,9 @@
 
     @pl.when(step == pl.num_programs(0) - 1)
     def _():
-        by = (s_ref[0] * length + shift) % mixed_ref.shape[0]
-        moved = placed_rows(mixed_sum_ref[...], by, shift)
+        moved = shifted_down(mixed_sum_ref[...], shift)
         mixed_ref[...] = (hidden_ref[...].astype(F32) + moved).astype(mixed_ref.dtype)
-        moved = placed_rows(grad_sum_ref[...], by, shift)
+        moved = shifted_down(grad_sum_ref[...], shift)
         grad_ref[...] = cotangent_ref[...].astype(F32) + moved
 
 
@@ -453,16 +471,19 @@
         60,
     )
 
-    live = jnp.arange(slots_per)[None, :] < after(seq_counts, (query, cot_parts[1:], cond_parts[1:]))[:, None]
-    slot_flat = slot_of.reshape(item_total)
-    matches = (jnp.arange(slot_total)[:, None] == slot_flat[None, :]) & live.reshape(item_total)[
-        None, :
-    ]
+    slots = after(slot_of.reshape(item_total), (query, cot_parts[1:], cond_parts[1:]))
     returned = lax.all_to_all(neighbours, "dp", split_axis=0, concat_axis=0, tiled=True)
-    items = jnp.einsum(
-        "si,sre->ire", matches.astype(BF16), returned, preferred_element_type=F32
-    ).astype(BF16)
-    items = items.reshape(blocks, slots_per * quarter, enc_width)
+    anywhere = pl.BlockSpec(memory_space=pl.ANY)
+    items = call(
+        pick_kernel,
+        "pick",
+        1,
+        [anywhere],
+        anywhere,
+        sds((blocks, slots_per * quarter, enc_width), BF16),
+        [pltpu.SemaphoreType.DMA((item_total,))],
+        16,
+    )(slots, returned)
     x = lax.all_to_all(items, "tensor", split_axis=0, concat_axis=0, tiled=True)
     x = x.reshape(rows, enc_width)
 
@@ -560,7 +581,7 @@
         [both_spec] * 4 + [weight_spec(1), weight_spec(0), out_spec, out_spec],
         (out_spec, out_spec),
         (sds((tokens, part_width), BF16), sds((tokens, part_width), F32)),
-        [acc, acc],
+        [pltpu.VMEM((2, tokens, head_width), BF16), acc, acc],
         60,
     )(scalars, *both_parts, qo_all, qo_all, hidden, cotangent)
     d_cond_parts = after(d_cond_parts, from_query)

time: 172 us -> 173 us (level)
  waiting for transfers between devices: 32.3 us -> 26.8 us
  local copies, waits for them, and re-layouts: 16.3 us -> 21.4 us
  matrix products: 4.23 us -> 1.94 us
  Pallas kernels: 54.3 us -> 56.1 us
    ppermute x1, waiting for transfers between devices: 4.26 us -> 0.96 us  [spread_halves(): far_bottom = lax.ppermute(last_bottom, axis, up)]
    unnamed x51 -> x67, local copies, waits for them, and re-layouts: 9.47 us -> 12.8 us
    ppermute x1, waiting for transfers between devices: 7.17 us -> 4.8 us  [spread_ring(): last_one = lax.ppermute(shard, axis, up)]
    dot_general x1 -> x0, matrix products: 2.29 us -> none  [shards(): jnp.einsum('si,sre->ire', matches.astype(BF16), returned, preferred_eleme...]
    ppermute x1, waiting for transfers between devices: 0.26 us -> 1.99 us  [spread_ring(): far_top = lax.ppermute(next_one[:half], axis, down)]
  transfers between devices with their start and end apart: 29 -> 29, of which waited for: 8 -> 8; matrix products, arithmetic and copies ran while one was open for 6% -> 6% of each run, Pallas kernels for 32% -> 33%
where the time goes in v5:
time: 173 us; the launch traced here: 171 us
  Pallas kernels  56.1 us (32%)
  starting transfers between devices  47.1 us (27%)
  waiting for transfers between devices  26.8 us (15%)
  local copies, waits for them, and re-layouts  21.4 us (12%)
  between operations  14.6 us (8%)
  other arithmetic  3.1 us (2%)
  matrix products  1.94 us (1%)
    pallas_call x1, Pallas kernels, shards(): call(encoded_back_kernel, 'encoded_back', n_tensor, [group(head_rows, row...  14.2 us
    unnamed x67, local copies, waits for them, and re-layouts  12.8 us
    pallas_call x1, Pallas kernels, shards(): call(attention_kernel, 'attention', n_tensor, [r_spec, kv_spec(0), kv_spe...  12.1 us
    pallas_call x2, Pallas kernels, projected(): call(functools.partial(project_kernel, dims, shift, counts), name, n_tens...  9.91 us
    pallas_call x1, Pallas kernels, shards(): call(functools.partial(outputs_kernel, shift), 'outputs', n_tensor, [both...  8.84 us
    ppermute x6, starting transfers between devices, spread(): lax.ppermute(shard, axis, [(i, (i - k) % size) for i in range(size)])  8.56 us
    ppermute x1, waiting for transfers between devices, spread_ring(): next_one = lax.ppermute(shard, axis, down)  7.97 us
    pallas_call x1, Pallas kernels, shards(): call(encode_kernel, 'encode', 1, [r_spec] + [c_spec] * 4 + [w_spec] * 2,...  7.63 us
  transfers between devices with their start and end apart: 29, of which 8 were waited for; matrix products, arithmetic and copies ran while one was open for 6% of the time, Pallas kernels for 33%

profile of v5, /device:TPU:10, one launch (start us, length us, event | category | flops | bytes accessed | tf_op | source)
XLA Modules:
  0.0 171.0 jit_solution(14617477936574106641)
XLA Ops:
  9.1 4.0 %collective-permute-start = (bf16[128,1024]{1,0:T(8,128)(2,1)}, bf16[128,1024]{1,0:T(8,128)(2,1)S(1)}, u32[]{:S(2)}, u32[]{:S(2)}) collective-permute-start(bf16[128,1024]{1,0:T(8,128)(2,1)} %get-tuple-element.63), channel_id=1, source_target_pairs={{0,3},{1,0},{2,1},{3,2},{4,7},{5,4},{6,5},{7,6},{8,11},{9,8},{10,9... | collective-permute-start | bytes 786440 | tf_op jit(solution)/shard_map/ppermute | solution.py:85
  16.2 4.7 %collective-permute-start.14 = (bf16[120,512]{1,0:T(8,128)(2,1)S(1)}, bf16[120,512]{1,0:T(8,128)(2,1)S(1)}, u32[]{:S(2)}, u32[]{:S(2)}) collective-permute-start(bf16[120,512]{1,0:T(8,128)(2,1)S(1)} %get-tuple-element.66), channel_id=1, source_target_pairs={{0,2},{1,3},{2,0},{3,1},{4,6},{5,7},{6,4},{7,5},{8,10},{9,11},{10,... | collective-permute-start | bytes 368648 | tf_op jit(solution)/shard_map/ppermute | solution.py:58
  22.2 2.0 %copy-done.3 = bf16[1024,1792]{1,0:T(8,128)(2,1)S(1)} copy-done((bf16[1024,1792]{1,0:T(8,128)(2,1)S(1)}, bf16[1024,1792]{1,0:T(8,128)(2,1)}, u32[]{:S(2)}) %copy-start.3) | copy-done | bytes 3670040
  30.4 7.5 %all-to-all-start = ((bf16[32,32,896]{2,1,0:T(8,128)(2,1)}), bf16[32,32,896]{2,1,0:T(8,128)(2,1)S(1)}, u32[]{:S(2)}, u32[]{:S(2)}) async-start(bf16[32,32,896]{2,1,0:T(8,128)(2,1)} %param.16), calls=%async_computation | async-start | bytes 3670016 | tf_op jit(solution)/shard_map/all_to_all | solution.py:475
  44.8 8.0 %collective-permute-done.6.refs_1_ = bf16[256,1024]{1,0:T(8,128)(2,1)S(1)} collective-permute-done((bf16[256,1024]{1,0:T(8,128)(2,1)S(1)}, bf16[256,1024]{1,0:T(8,128)(2,1)S(1)}, u32[]{:S(2)}, u32[]{:S(2)}) %collective-permute-start.6) | collective-permute-done | bytes 524320 | tf_op jit(solution)/shard_map/ppermute | solution.py:73
  52.8 2.1 %collective-permute-start.4 = (bf16[128,1024]{1,0:T(8,128)(2,1)}, bf16[128,1024]{1,0:T(8,128)(2,1)S(1)}, u32[]{:S(2)}, u32[]{:S(2)}) collective-permute-start(bf16[128,1024]{1,0:T(8,128)(2,1)} %copy-done.23), channel_id=1, source_target_pairs={{0,1},{1,2},{2,3},{3,0},{4,5},{5,6},{6,7},{7,4},{8,9},{9,10},{10,1... | collective-permute-start | bytes 786440 | tf_op jit(solution)/shard_map/ppermute | solution.py:90
  57.3 4.8 %collective-permute-done.8.refs_4_ = bf16[256,1024]{1,0:T(8,128)(2,1)S(1)} collective-permute-done((bf16[256,1024]{1,0:T(8,128)(2,1)S(1)}, bf16[256,1024]{1,0:T(8,128)(2,1)S(1)}, u32[]{:S(2)}, u32[]{:S(2)}) %collective-permute-start.8) | collective-permute-done | bytes 524320 | tf_op jit(solution)/shard_map/ppermute | solution.py:74
  65.0 2.6 %collective-permute-start.7 = (bf16[128,1024]{1,0:T(8,128)(2,1)}, bf16[128,1024]{1,0:T(8,128)(2,1)}, u32[]{:S(2)}, u32[]{:S(2)}) collective-permute-start(bf16[128,1024]{1,0:T(8,128)(2,1)} %slice.50), channel_id=1, source_target_pairs={{0,3},{1,0},{2,1},{3,2},{4,7},{5,4},{6,5},{7,6},{8,11},{9,8},{10,9... | collective-permute-start | bytes 786440 | tf_op jit(solution)/shard_map/ppermute | solution.py:75
  70.0 6.0 %query.1.refs_6_ = bf16[256,512]{1,0:T(8,128)(2,1)} custom-call(s32[2]{0:T(128)} %copy-done.9, bf16[256,1024]{1,0:T(8,128)(2,1)} %hidden_ref.3, bf16[128,1024]{1,0:T(8,128)(2,1)} %copy-done.22, bf16[128,1024]{1,0:T(8,128)(2,1)} %collective-permute-done.1.refs_2_, bf16[128,1024]{1,0:T(8,128)(2,1)} %copy-done.24, bf16[128,1024]{1,0:T(8,128)(2,1)} %copy-done.25, ...), custom_call_target="tpu_custom_call" | custom-call | tf_op jit(solution)/shard_map/query/pallas_call | solution.py:450
  77.1 2.0 %collective-permute-done.7.refs_2_ = bf16[128,1024]{1,0:T(8,128)(2,1)} collective-permute-done((bf16[128,1024]{1,0:T(8,128)(2,1)}, bf16[128,1024]{1,0:T(8,128)(2,1)}, u32[]{:S(2)}, u32[]{:S(2)}) %collective-permute-start.7) | collective-permute-done | bytes 262176 | tf_op jit(solution)/shard_map/ppermute | solution.py:75
  79.1 2.7 %collective-permute-done.9.refs_3_ = bf16[128,1024]{1,0:T(8,128)(2,1)} collective-permute-done((bf16[128,1024]{1,0:T(8,128)(2,1)}, bf16[128,1024]{1,0:T(8,128)(2,1)}, u32[]{:S(2)}, u32[]{:S(2)}) %collective-permute-start.9) | collective-permute-done | bytes 262176 | tf_op jit(solution)/shard_map/ppermute | solution.py:76
  83.5 4.4 %all-to-all-start.1 = ((bf16[4,128,896]{2,1,0:T(8,128)(2,1)}), bf16[4,128,896]{2,1,0:T(8,128)(2,1)}, u32[]{:S(2)}, u32[]{:S(2)}) async-start(bf16[4,128,896]{2,1,0:T(8,128)(2,1)} %pick.1), calls=%async_computation.1 | async-start | bytes 1835008 | tf_op jit(solution)/shard_map/all_to_all | solution.py:487
  88.0 2.3 %copy-done.2 = bf16[512,4096]{1,0:T(8,128)(2,1)S(1)} copy-done((bf16[512,4096]{1,0:T(8,128)(2,1)S(1)}, bf16[512,4096]{1,0:T(8,128)(2,1)}, u32[]{:S(2)}) %copy-start.2) | copy-done | bytes 4194328
  90.3 3.9 %d_ctx.1 = (bf16[2,64,512]{2,1,0:T(8,128)(2,1)S(1)}, bf16[2,64,512]{2,1,0:T(8,128)(2,1)S(1)}, bf16[2,64,512]{2,1,0:T(8,128)(2,1)S(1)}, bf16[2,64,512]{2,1,0:T(8,128)(2,1)S(1)}) custom-call(s32[2]{0:T(128)S(1)} %copy-done.10, bf16[256,1024]{1,0:T(8,128)(2,1)S(1)} %copy-done.5, bf16[256,1024]{1,0:T(8,128)(2,1)S(1)} %collective-permute-done.6.refs_1_, ...), custom_call_target="tpu_custom_call" | custom-call | tf_op jit(solution)/shard_map/d_ctx/pallas_call | solution.py:450
  94.9 3.1 %collective-permute-start.16 = (bf16[2,64,512]{2,1,0:T(8,128)(2,1)S(1)}, bf16[2,64,512]{2,1,0:T(8,128)(2,1)S(1)}, u32[]{:S(2)}, u32[]{:S(2)}) collective-permute-start(bf16[2,64,512]{2,1,0:T(8,128)(2,1)S(1)} %get-tuple-element.45), channel_id=1, source_target_pairs={{0,3},{1,0},{2,1},{3,2},{4,7},{5,4},{6,5},{7,6},{8,11},{9,8},{10,9... | collective-permute-start | bytes 393224 | tf_op jit(solution)/shard_map/ppermute | solution.py:503
  99.7 2.0 %all-to-all-done.1 = bf16[4,128,896]{2,1,0:T(8,128)(2,1)} async-done(((bf16[4,128,896]{2,1,0:T(8,128)(2,1)}), bf16[4,128,896]{2,1,0:T(8,128)(2,1)}, u32[]{:S(2)}, u32[]{:S(2)}) %all-to-all-start.1) | async-done | bytes 917536 | tf_op jit(solution)/shard_map/all_to_all | solution.py:487
  101.7 7.6 %encode.1 = (bf16[64,1792]{1,0:T(8,128)(2,1)}, bf16[512,896]{1,0:T(8,128)(2,1)}, f32[448,512]{1,0:T(8,128)}, bf16[512,896]{1,0:T(8,128)(2,1)}) custom-call(s32[2]{0:T(128)} %copy-done.9, bf16[512,896]{1,0:T(8,128)(2,1)} %bitcast.2.x_ref, bf16[64,1792]{1,0:T(8,128)(2,1)} %copy-done.8, bf16[64,1792]{1,0:T(8,128)(2,1)} %collective-permute-done.10.c1, ...), custom_call_target="tpu_custom_call" | custom-call | tf_op jit(solution)/shard_map/encode/pallas_call | solution.py:511
  110.1 12.1 %attention.1 = (bf16[4,256,512]{2,1,0:T(8,128)(2,1)}, bf16[4,256,512]{2,1,0:T(8,128)(2,1)}, bf16[2,64,2048]{2,1,0:T(8,128)(2,1)}) custom-call(s32[2]{0:T(128)} %copy-done.9, bf16[512,896]{1,0:T(8,128)(2,1)} %get-tuple-element.37.encoded_ref, bf16[32,4,56,512]{3,2,1,0:T(8,128)(2,1)} %bitcast.41, bf16[32,4,56,512]{3,2,1,0:T(8,128)(2,1)} %bitcast.42, ...), custom_call_target="tpu_custom_call" | custom-call | tf_op jit(solution)/shard_map/attention/pallas_call | solution.py:530
  122.2 2.7 %collective-permute-start.19 = (bf16[2,64,2048]{2,1,0:T(8,128)(2,1)}, bf16[2,64,2048]{2,1,0:T(8,128)(2,1)S(1)}, u32[]{:S(2)}, u32[]{:S(2)}) collective-permute-start(bf16[2,64,2048]{2,1,0:T(8,128)(2,1)} %get-tuple-element.48.c0), channel_id=1, source_target_pairs={{0,3},{1,0},{2,1},{3,2},{4,7},{5,4},{6,5},{7,6},{8,11},{9,8},{10,9... | collective-permute-start | bytes 1572872 | tf_op jit(solution)/shard_map/ppermute | solution.py:64
  126.5 14.2 %encoded_back.1 = bf16[64,1792]{1,0:T(8,128)(2,1)} custom-call(s32[2]{0:T(128)} %copy-done.9, bf16[4,256,512]{2,1,0:T(8,128)(2,1)} %get-tuple-element.52.d_scores_ref, bf16[4,256,512]{2,1,0:T(8,128)(2,1)} %get-tuple-element.53.probs_ref, bf16[2,64,512]{2,1,0:T(8,128)(2,1)} %copy-done.7, bf16[2,64,512]{2,1,0:T(8,128)(2,1)} %copy-done.16, ...), custom_call_target="tpu_custom_call" | custom-call | tf_op jit(solution)/shard_map/encoded_back/pallas_call | solution.py:550
  140.7 3.3 %collective-permute-start.22 = (bf16[64,1792]{1,0:T(8,128)(2,1)}, bf16[64,1792]{1,0:T(8,128)(2,1)S(1)}, u32[]{:S(2)}, u32[]{:S(2)}) collective-permute-start(bf16[64,1792]{1,0:T(8,128)(2,1)} %encoded_back.1), channel_id=1, source_target_pairs={{0,3},{1,0},{2,1},{3,2},{4,7},{5,4},{6,5},{7,6},{8,11},{9,8},{10,9... | collective-permute-start | bytes 688136 | tf_op jit(solution)/shard_map/ppermute | solution.py:64
  145.0 5.2 %collective-permute-done.21.c3 = bf16[2,64,2048]{2,1,0:T(8,128)(2,1)S(1)} collective-permute-done((bf16[2,64,2048]{2,1,0:T(8,128)(2,1)}, bf16[2,64,2048]{2,1,0:T(8,128)(2,1)S(1)}, u32[]{:S(2)}, u32[]{:S(2)}) %collective-permute-start.21) | collective-permute-done | bytes 524320 | tf_op jit(solution)/shard_map/ppermute | solution.py:64
  151.0 8.8 %outputs.1 = (bf16[256,1024]{1,0:T(8,128)(2,1)}, f32[256,1024]{1,0:T(8,128)}) custom-call(s32[2]{0:T(128)} %copy-done.9, bf16[2,64,2048]{2,1,0:T(8,128)(2,1)} %get-tuple-element.48.c0, bf16[2,64,2048]{2,1,0:T(8,128)(2,1)} %copy-done.19, bf16[2,64,2048]{2,1,0:T(8,128)(2,1)} %copy-done.20, bf16[2,64,2048]{2,1,0:T(8,128)(2,1)} %copy-done.21, ...), custom_call_target="tpu_custom_call" | custom-call | tf_op jit(solution)/shard_map/outputs/pallas_call | solution.py:577
  162.2 1.9 %fusion = bf16[256,1024]{1,0:T(8,128)(2,1)} fusion(f32[256,1024]{1,0:T(8,128)S(1)} %copy-done.29, bf16[256,1792]{1,0:T(8,128)(2,1)S(1)} %bitcast.48, bf16[1024,1792]{1,0:T(8,128)(2,1)S(1)} %copy-done.4), kind=kOutput, calls=%fused_computation.1 | convolution fusion | flops 940048384 | bytes 6160384 | tf_op jit(solution)/shard_map/dot_general | solution.py:24
  (138 shorter events, 38.4 us)
Async XLA Ops:
  7.2 102.2 %all-gather.5.cloned.1.call-start = ((), (), s32[]{:S(2)}) async-start(), calls=%async_computation.2 | async-start | bytes 7569408 | tf_op jit(solution)/shard_map/all_gather | solution.py:437
  9.1 20.5 %collective-permute-start = (bf16[128,1024]{1,0:T(8,128)(2,1)}, bf16[128,1024]{1,0:T(8,128)(2,1)S(1)}, u32[]{:S(2)}, u32[]{:S(2)}) collective-permute-start(bf16[128,1024]{1,0:T(8,128)(2,1)} %get-tuple-element.63), channel_id=1, source_target_pairs={{0,3},{1,0},{2,1},{3,2},{4,7},{5,4},{6,5},{7,6},{8,11},{9,8},{10,9... | collective-permute-start | bytes 786440 | tf_op jit(solution)/shard_map/ppermute | solution.py:85
  13.1 16.5 %collective-permute-start.3 = (bf16[128,1024]{1,0:T(8,128)(2,1)}, bf16[128,1024]{1,0:T(8,128)(2,1)S(1)}, u32[]{:S(2)}, u32[]{:S(2)}) collective-permute-start(bf16[128,1024]{1,0:T(8,128)(2,1)} %get-tuple-element.62), channel_id=1, source_target_pairs={{0,1},{1,2},{2,3},{3,0},{4,5},{5,6},{6,7},{7,4},{8,9},{9,10},{10,1... | collective-permute-start | bytes 786440 | tf_op jit(solution)/shard_map/ppermute | solution.py:86
  16.1 12.7 %collective-permute-start.15 = (bf16[120,512]{1,0:T(8,128)(2,1)S(1)}, bf16[120,512]{1,0:T(8,128)(2,1)S(1)}, u32[]{:S(2)}, u32[]{:S(2)}) collective-permute-start(bf16[120,512]{1,0:T(8,128)(2,1)S(1)} %get-tuple-element.65), channel_id=1, source_target_pairs={{0,1},{1,2},{2,3},{3,0},{4,5},{5,6},{6,7},{7,4},{8,9},{9,10},{10,1... | collective-permute-start | bytes 368648 | tf_op jit(solution)/shard_map/ppermute | solution.py:58
  30.4 51.4 %all-to-all-start = ((bf16[32,32,896]{2,1,0:T(8,128)(2,1)}), bf16[32,32,896]{2,1,0:T(8,128)(2,1)S(1)}, u32[]{:S(2)}, u32[]{:S(2)}) async-start(bf16[32,32,896]{2,1,0:T(8,128)(2,1)} %param.16), calls=%async_computation | async-start | bytes 3670016 | tf_op jit(solution)/shard_map/all_to_all | solution.py:475
  37.9 112.2 %all-gather.7.cloned.1.call-start = ((), (), s32[]{:S(2)}) async-start(), calls=%async_computation.3 | async-start | bytes 8650752 | tf_op jit(solution)/shard_map/all_gather | solution.py:490
  38.0 14.8 %collective-permute-start.6 = (bf16[256,1024]{1,0:T(8,128)(2,1)S(1)}, bf16[256,1024]{1,0:T(8,128)(2,1)S(1)}, u32[]{:S(2)}, u32[]{:S(2)}) collective-permute-start(bf16[256,1024]{1,0:T(8,128)(2,1)S(1)} %copy-done.5), channel_id=1, source_target_pairs={{0,3},{1,0},{2,1},{3,2},{4,7},{5,4},{6,5},{7,6},{8,11},{9,8},{10,9... | collective-permute-start | bytes 1572872 | tf_op jit(solution)/shard_map/ppermute | solution.py:73
  38.6 25.5 %collective-permute-start.1 = (bf16[128,1024]{1,0:T(8,128)(2,1)}, bf16[128,1024]{1,0:T(8,128)(2,1)}, u32[]{:S(2)}, u32[]{:S(2)}) collective-permute-start(bf16[128,1024]{1,0:T(8,128)(2,1)} %get-tuple-element.62), channel_id=1, source_target_pairs={{0,3},{1,0},{2,1},{3,2},{4,7},{5,4},{6,5},{7,6},{8,11},{9,8},{10,9... | collective-permute-start | bytes 786440 | tf_op jit(solution)/shard_map/ppermute | solution.py:87
  40.2 23.9 %collective-permute-start.5 = (bf16[128,1024]{1,0:T(8,128)(2,1)}, bf16[128,1024]{1,0:T(8,128)(2,1)}, u32[]{:S(2)}, u32[]{:S(2)}) collective-permute-start(bf16[128,1024]{1,0:T(8,128)(2,1)} %get-tuple-element.63), channel_id=1, source_target_pairs={{0,1},{1,2},{2,3},{3,0},{4,5},{5,6},{6,7},{7,4},{8,9},{9,10},{10,1... | collective-permute-start | bytes 786440 | tf_op jit(solution)/shard_map/ppermute | solution.py:88
  40.6 21.4 %collective-permute-start.8 = (bf16[256,1024]{1,0:T(8,128)(2,1)S(1)}, bf16[256,1024]{1,0:T(8,128)(2,1)S(1)}, u32[]{:S(2)}, u32[]{:S(2)}) collective-permute-start(bf16[256,1024]{1,0:T(8,128)(2,1)S(1)} %copy-done.5), channel_id=1, source_target_pairs={{0,1},{1,2},{2,3},{3,0},{4,5},{5,6},{6,7},{7,4},{8,9},{9,10},{10,1... | collective-permute-start | bytes 1572872 | tf_op jit(solution)/shard_map/ppermute | solution.py:74
  43.1 21.9 %collective-permute-start.2 = (bf16[128,1024]{1,0:T(8,128)(2,1)}, bf16[128,1024]{1,0:T(8,128)(2,1)S(1)}, u32[]{:S(2)}, u32[]{:S(2)}) collective-permute-start(bf16[128,1024]{1,0:T(8,128)(2,1)} %copy-done.22), channel_id=1, source_target_pairs={{0,3},{1,0},{2,1},{3,2},{4,7},{5,4},{6,5},{7,6},{8,11},{9,8},{10,9... | collective-permute-start | bytes 786440 | tf_op jit(solution)/shard_map/ppermute | solution.py:89
  52.8 15.7 %collective-permute-start.4 = (bf16[128,1024]{1,0:T(8,128)(2,1)}, bf16[128,1024]{1,0:T(8,128)(2,1)S(1)}, u32[]{:S(2)}, u32[]{:S(2)}) collective-permute-start(bf16[128,1024]{1,0:T(8,128)(2,1)} %copy-done.23), channel_id=1, source_target_pairs={{0,1},{1,2},{2,3},{3,0},{4,5},{5,6},{6,7},{7,4},{8,9},{9,10},{10,1... | collective-permute-start | bytes 786440 | tf_op jit(solution)/shard_map/ppermute | solution.py:90
  62.1 13.9 %collective-permute-start.10 = (bf16[64,1792]{1,0:T(8,128)(2,1)}, bf16[64,1792]{1,0:T(8,128)(2,1)}, u32[]{:S(2)}, u32[]{:S(2)}) collective-permute-start(bf16[64,1792]{1,0:T(8,128)(2,1)} %copy-done.13), channel_id=1, source_target_pairs={{0,3},{1,0},{2,1},{3,2},{4,7},{5,4},{6,5},{7,6},{8,11},{9,8},{10,9... | collective-permute-start | bytes 688136 | tf_op jit(solution)/shard_map/ppermute | solution.py:439
  64.1 13.0 %collective-permute-start.12 = (bf16[64,1792]{1,0:T(8,128)(2,1)}, bf16[64,1792]{1,0:T(8,128)(2,1)}, u32[]{:S(2)}, u32[]{:S(2)}) collective-permute-start(bf16[64,1792]{1,0:T(8,128)(2,1)} %copy-done.11), channel_id=1, source_target_pairs={{0,1},{1,2},{2,3},{3,0},{4,5},{5,6},{6,7},{7,4},{8,9},{9,10},{10,1... | collective-permute-start | bytes 688136 | tf_op jit(solution)/shard_map/ppermute | solution.py:439
  65.0 14.1 %collective-permute-start.7 = (bf16[128,1024]{1,0:T(8,128)(2,1)}, bf16[128,1024]{1,0:T(8,128)(2,1)}, u32[]{:S(2)}, u32[]{:S(2)}) collective-permute-start(bf16[128,1024]{1,0:T(8,128)(2,1)} %slice.50), channel_id=1, source_target_pairs={{0,3},{1,0},{2,1},{3,2},{4,7},{5,4},{6,5},{7,6},{8,11},{9,8},{10,9... | collective-permute-start | bytes 786440 | tf_op jit(solution)/shard_map/ppermute | solution.py:75
  68.5 13.3 %collective-permute-start.9 = (bf16[128,1024]{1,0:T(8,128)(2,1)}, bf16[128,1024]{1,0:T(8,128)(2,1)}, u32[]{:S(2)}, u32[]{:S(2)}) collective-permute-start(bf16[128,1024]{1,0:T(8,128)(2,1)} %slice.51), channel_id=1, source_target_pairs={{0,1},{1,2},{2,3},{3,0},{4,5},{5,6},{6,7},{7,4},{8,9},{9,10},{10,1... | collective-permute-start | bytes 786440 | tf_op jit(solution)/shard_map/ppermute | solution.py:76
  83.5 18.2 %all-to-all-start.1 = ((bf16[4,128,896]{2,1,0:T(8,128)(2,1)}), bf16[4,128,896]{2,1,0:T(8,128)(2,1)}, u32[]{:S(2)}, u32[]{:S(2)}) async-start(bf16[4,128,896]{2,1,0:T(8,128)(2,1)} %pick.1), calls=%async_computation.1 | async-start | bytes 1835008 | tf_op jit(solution)/shard_map/all_to_all | solution.py:487
  94.9 14.4 %collective-permute-start.16 = (bf16[2,64,512]{2,1,0:T(8,128)(2,1)S(1)}, bf16[2,64,512]{2,1,0:T(8,128)(2,1)S(1)}, u32[]{:S(2)}, u32[]{:S(2)}) collective-permute-start(bf16[2,64,512]{2,1,0:T(8,128)(2,1)S(1)} %get-tuple-element.45), channel_id=1, source_target_pairs={{0,3},{1,0},{2,1},{3,2},{4,7},{5,4},{6,5},{7,6},{8,11},{9,8},{10,9... | collective-permute-start | bytes 393224 | tf_op jit(solution)/shard_map/ppermute | solution.py:503
  122.2 18.5 %collective-permute-start.19 = (bf16[2,64,2048]{2,1,0:T(8,128)(2,1)}, bf16[2,64,2048]{2,1,0:T(8,128)(2,1)S(1)}, u32[]{:S(2)}, u32[]{:S(2)}) collective-permute-start(bf16[2,64,2048]{2,1,0:T(8,128)(2,1)} %get-tuple-element.48.c0), channel_id=1, source_target_pairs={{0,3},{1,0},{2,1},{3,2},{4,7},{5,4},{6,5},{7,6},{8,11},{9,8},{10,9... | collective-permute-start | bytes 1572872 | tf_op jit(solution)/shard_map/ppermute | solution.py:64
  124.9 20.1 %collective-permute-start.20 = (bf16[2,64,2048]{2,1,0:T(8,128)(2,1)}, bf16[2,64,2048]{2,1,0:T(8,128)(2,1)S(1)}, u32[]{:S(2)}, u32[]{:S(2)}) collective-permute-start(bf16[2,64,2048]{2,1,0:T(8,128)(2,1)} %get-tuple-element.48.c0), channel_id=1, source_target_pairs={{0,2},{1,3},{2,0},{3,1},{4,6},{5,7},{6,4},{7,5},{8,10},{9,11},{10,... | collective-permute-start | bytes 1572872 | tf_op jit(solution)/shard_map/ppermute | solution.py:64
  126.5 23.7 %collective-permute-start.21 = (bf16[2,64,2048]{2,1,0:T(8,128)(2,1)}, bf16[2,64,2048]{2,1,0:T(8,128)(2,1)S(1)}, u32[]{:S(2)}, u32[]{:S(2)}) collective-permute-start(bf16[2,64,2048]{2,1,0:T(8,128)(2,1)} %get-tuple-element.48.c0), channel_id=1, source_target_pairs={{0,1},{1,2},{2,3},{3,0},{4,5},{5,6},{6,7},{7,4},{8,9},{9,10},{10,1... | collective-permute-start | bytes 1572872 | tf_op jit(solution)/shard_map/ppermute | solution.py:64
  140.7 19.1 %collective-permute-start.22 = (bf16[64,1792]{1,0:T(8,128)(2,1)}, bf16[64,1792]{1,0:T(8,128)(2,1)S(1)}, u32[]{:S(2)}, u32[]{:S(2)}) collective-permute-start(bf16[64,1792]{1,0:T(8,128)(2,1)} %encoded_back.1), channel_id=1, source_target_pairs={{0,3},{1,0},{2,1},{3,2},{4,7},{5,4},{6,5},{7,6},{8,11},{9,8},{10,9... | collective-permute-start | bytes 688136 | tf_op jit(solution)/shard_map/ppermute | solution.py:64
  144.0 15.8 %collective-permute-start.23 = (bf16[64,1792]{1,0:T(8,128)(2,1)}, bf16[64,1792]{1,0:T(8,128)(2,1)S(1)}, u32[]{:S(2)}, u32[]{:S(2)}) collective-permute-start(bf16[64,1792]{1,0:T(8,128)(2,1)} %encoded_back.1), channel_id=1, source_target_pairs={{0,2},{1,3},{2,0},{3,1},{4,6},{5,7},{6,4},{7,5},{8,10},{9,11},{10,... | collective-permute-start | bytes 688136 | tf_op jit(solution)/shard_map/ppermute | solution.py:64
  144.8 15.0 %collective-permute-start.24 = (bf16[64,1792]{1,0:T(8,128)(2,1)}, bf16[64,1792]{1,0:T(8,128)(2,1)S(1)}, u32[]{:S(2)}, u32[]{:S(2)}) collective-permute-start(bf16[64,1792]{1,0:T(8,128)(2,1)} %encoded_back.1), channel_id=1, source_target_pairs={{0,1},{1,2},{2,3},{3,0},{4,5},{5,6},{6,7},{7,4},{8,9},{9,10},{10,1... | collective-permute-start | bytes 688136 | tf_op jit(solution)/shard_map/ppermute | solution.py:64
  (35 other events, 177.3 us)
Sparse Core Ops, SparseCore 0:
  29.8 61.6 all-gather.4
  93.8 52.3 all-gather.6

commit v6 on v4

--- a/solution.py
+++ b/solution.py
@@ -292,10 +292,8 @@
         d_cond_ref[...] = jnp.concatenate(d_keys + d_vals, axis=1).astype(BF16)
 
 
-def placed_rows(rows, by, shift):
-    moved = pltpu.roll(rows, by, 0)
-    if shift == 0:
-        return moved
+def shifted_down(rows, shift):
+    moved = pltpu.roll(rows, shift, 0)
     index = lax.broadcasted_iota(jnp.int32, rows.shape, 0)
     return jnp.where(index >= shift, moved, 0.0)
 
@@ -313,6 +311,7 @@
     cotangent_ref,
     mixed_ref,
     grad_ref,
+    rows_ref,
     mixed_sum_ref,
     grad_sum_ref,
 ):
@@ -320,9 +319,11 @@
     half = out_w_ref.shape[2] // 2
     wide = out_w_ref.shape[3]
     length = c0.shape[1]
-    parts = (c0, c1, c2, c3)
-    ctx = jnp.concatenate([ref[0] for ref in parts], axis=0)
-    d_query = jnp.concatenate([ref[1] for ref in parts], axis=0)
+    for k, ref in enumerate((c0, c1, c2, c3)):
+        start = pl.multiple_of(((s_ref[0] + k) % 4) * length, length)
+        rows_ref[:, pl.ds(start, length), :] = ref[...]
+    ctx = rows_ref[0]
+    d_query = rows_ref[1]
 
     @pl.when(step == 0)
     def _():
@@ -336,10 +337,9 @@
 
     @pl.when(step == pl.num_programs(0) - 1)
     def _():
-        by = (s_ref[0] * length + shift) % mixed_ref.shape[0]
-        moved = placed_rows(mixed_sum_ref[...], by, shift)
+        moved = shifted_down(mixed_sum_ref[...], shift)
         mixed_ref[...] = (hidden_ref[...].astype(F32) + moved).astype(mixed_ref.dtype)
-        moved = placed_rows(grad_sum_ref[...], by, shift)
+        moved = shifted_down(grad_sum_ref[...], shift)
         grad_ref[...] = cotangent_ref[...].astype(F32) + moved
 
 
@@ -560,7 +560,7 @@
         [both_spec] * 4 + [weight_spec(1), weight_spec(0), out_spec, out_spec],
         (out_spec, out_spec),
         (sds((tokens, part_width), BF16), sds((tokens, part_width), F32)),
-        [acc, acc],
+        [pltpu.VMEM((2, tokens, head_width), BF16), acc, acc],
         60,
     )(scalars, *both_parts, qo_all, qo_all, hidden, cotangent)
     d_cond_parts = after(d_cond_parts, from_query)

time: 172 us -> 171 us (level)
  no operation moved by 1% of the time
where the time goes in v6:
time: 171 us; the launch traced here: 170 us
  Pallas kernels  53.7 us (31%)
  starting transfers between devices  46 us (27%)
  waiting for transfers between devices  32.3 us (19%)
  local copies, waits for them, and re-layouts  16.3 us (10%)
  between operations  14.5 us (8%)
  matrix products  4.23 us (2%)
  other arithmetic  3.21 us (2%)
    pallas_call x1, Pallas kernels, shards(): call(encoded_back_kernel, 'encoded_back', n_tensor, [group(head_rows, row...  14.3 us
    pallas_call x1, Pallas kernels, shards(): call(attention_kernel, 'attention', n_tensor, [r_spec, kv_spec(0), kv_spe...  12.2 us
    unnamed x51, local copies, waits for them, and re-layouts  9.47 us
    pallas_call x2, Pallas kernels, projected(): call(functools.partial(project_kernel, dims, shift, counts), name, n_tens...  8.87 us
    ppermute x1, waiting for transfers between devices, spread_ring(): next_one = lax.ppermute(shard, axis, down)  8.86 us
    pallas_call x1, Pallas kernels, shards(): call(functools.partial(outputs_kernel, shift), 'outputs', n_tensor, [both...  8.85 us
    ppermute x6, starting transfers between devices, shards(): lax.ppermute(array, 'tensor', [(i, (i - k) % n_tensor) for i in range(n_t...  7.85 us
    ppermute x6, starting transfers between devices, spread(): lax.ppermute(shard, axis, [(i, (i - k) % size) for i in range(size)])  7.82 us
  transfers between devices with their start and end apart: 29, of which 8 were waited for; matrix products, arithmetic and copies ran while one was open for 6% of the time, Pallas kernels for 32%

profile of v6, /device:TPU:10, one launch (start us, length us, event | category | flops | bytes accessed | tf_op | source)
XLA Modules:
  0.0 170.3 jit_solution(2804579479764456787)
XLA Ops:
  9.1 4.0 %collective-permute-start = (bf16[128,1024]{1,0:T(8,128)(2,1)}, bf16[128,1024]{1,0:T(8,128)(2,1)}, u32[]{:S(2)}, u32[]{:S(2)}) collective-permute-start(bf16[128,1024]{1,0:T(8,128)(2,1)} %get-tuple-element.63), channel_id=1, source_target_pairs={{0,3},{1,0},{2,1},{3,2},{4,7},{5,4},{6,5},{7,6},{8,11},{9,8},{10,9... | collective-permute-start | bytes 786440 | tf_op jit(solution)/shard_map/ppermute | solution.py:85
  16.2 4.7 %collective-permute-start.14 = (bf16[120,512]{1,0:T(8,128)(2,1)S(1)}, bf16[120,512]{1,0:T(8,128)(2,1)S(1)}, u32[]{:S(2)}, u32[]{:S(2)}) collective-permute-start(bf16[120,512]{1,0:T(8,128)(2,1)S(1)} %get-tuple-element.66), channel_id=1, source_target_pairs={{0,2},{1,3},{2,0},{3,1},{4,6},{5,7},{6,4},{7,5},{8,10},{9,11},{10,... | collective-permute-start | bytes 368648 | tf_op jit(solution)/shard_map/ppermute | solution.py:58
  22.3 2.0 %copy-done.2 = bf16[1024,1792]{1,0:T(8,128)(2,1)S(1)} copy-done((bf16[1024,1792]{1,0:T(8,128)(2,1)S(1)}, bf16[1024,1792]{1,0:T(8,128)(2,1)}, u32[]{:S(2)}) %copy-start.2) | copy-done | bytes 3670040
  28.4 7.7 %all-to-all-start = ((bf16[32,32,896]{2,1,0:T(8,128)(2,1)}), bf16[32,32,896]{2,1,0:T(8,128)(2,1)}, u32[]{:S(2)}, u32[]{:S(2)}) async-start(bf16[32,32,896]{2,1,0:T(8,128)(2,1)} %param.16), calls=%async_computation | async-start | bytes 3670016 | tf_op jit(solution)/shard_map/all_to_all | solution.py:461
  42.2 8.9 %collective-permute-done.6.refs_1_ = bf16[256,1024]{1,0:T(8,128)(2,1)S(1)} collective-permute-done((bf16[256,1024]{1,0:T(8,128)(2,1)S(1)}, bf16[256,1024]{1,0:T(8,128)(2,1)S(1)}, u32[]{:S(2)}, u32[]{:S(2)}) %collective-permute-start.6) | collective-permute-done | bytes 524320 | tf_op jit(solution)/shard_map/ppermute | solution.py:73
  52.4 7.2 %collective-permute-done.8.refs_4_ = bf16[256,1024]{1,0:T(8,128)(2,1)S(1)} collective-permute-done((bf16[256,1024]{1,0:T(8,128)(2,1)S(1)}, bf16[256,1024]{1,0:T(8,128)(2,1)S(1)}, u32[]{:S(2)}, u32[]{:S(2)}) %collective-permute-start.8) | collective-permute-done | bytes 524320 | tf_op jit(solution)/shard_map/ppermute | solution.py:74
  62.6 2.3 %collective-permute-start.7 = (bf16[128,1024]{1,0:T(8,128)(2,1)S(1)}, bf16[128,1024]{1,0:T(8,128)(2,1)S(1)}, u32[]{:S(2)}, u32[]{:S(2)}) collective-permute-start(bf16[128,1024]{1,0:T(8,128)(2,1)S(1)} %slice.50), channel_id=1, source_target_pairs={{0,3},{1,0},{2,1},{3,2},{4,7},{5,4},{6,5},{7,6},{8,11},{9,8},{10,9... | collective-permute-start | bytes 786440 | tf_op jit(solution)/shard_map/ppermute | solution.py:75
  64.9 4.3 %collective-permute-done.4.refs_4_ = bf16[128,1024]{1,0:T(8,128)(2,1)} collective-permute-done((bf16[128,1024]{1,0:T(8,128)(2,1)}, bf16[128,1024]{1,0:T(8,128)(2,1)}, u32[]{:S(2)}, u32[]{:S(2)}) %collective-permute-start.4) | collective-permute-done | bytes 262176 | tf_op jit(solution)/shard_map/ppermute | solution.py:90
  70.7 5.9 %query.1.refs_6_ = bf16[256,512]{1,0:T(8,128)(2,1)} custom-call(s32[2]{0:T(128)} %copy-done.8, bf16[256,1024]{1,0:T(8,128)(2,1)} %hidden_ref.3, bf16[128,1024]{1,0:T(8,128)(2,1)} %collective-permute-done.refs_1_, bf16[128,1024]{1,0:T(8,128)(2,1)} %collective-permute-done.1.refs_2_, bf16[128,1024]{1,0:T(8,128)(2,1)} %collective-permute-done.2.refs_3_, ...), custom_call_target="tpu_custom_call" | custom-call | tf_op jit(solution)/shard_map/query/pallas_call | solution.py:432
  77.0 2.2 %collective-permute-done.9.refs_3_ = bf16[128,1024]{1,0:T(8,128)(2,1)S(1)} collective-permute-done((bf16[128,1024]{1,0:T(8,128)(2,1)S(1)}, bf16[128,1024]{1,0:T(8,128)(2,1)S(1)}, u32[]{:S(2)}, u32[]{:S(2)}) %collective-permute-start.9) | collective-permute-done | bytes 262176 | tf_op jit(solution)/shard_map/ppermute | solution.py:76
  79.3 2.3 %fusion.2 = bf16[16,32,896]{2,0,1:T(8,128)(2,1)S(1)} fusion(bf16[32,32,896]{2,1,0:T(8,128)(2,1)} %all-to-all-done, s32[16]{0:T(128)S(1)} %eq.23, pred[16]{0:T(512)(128)(4,1)S(1)} %lt.78), kind=kOutput, calls=%fused_computation.2 | convolution fusion | flops 29819904 | bytes 2752592 | tf_op jit(solution)/shard_map/si,sre->ire/dot_general | solution.py:462
  82.8 4.3 %all-to-all-start.1 = ((bf16[4,128,896]{2,1,0:T(8,128)(2,1)}), bf16[4,128,896]{2,1,0:T(8,128)(2,1)}, u32[]{:S(2)}, u32[]{:S(2)}) async-start(bf16[4,128,896]{2,1,0:T(8,128)(2,1)} %bitcast.53), calls=%async_computation.1 | async-start | bytes 1835008 | tf_op jit(solution)/shard_map/all_to_all | solution.py:466
  87.1 2.3 %copy-done.1 = bf16[512,4096]{1,0:T(8,128)(2,1)S(1)} copy-done((bf16[512,4096]{1,0:T(8,128)(2,1)S(1)}, bf16[512,4096]{1,0:T(8,128)(2,1)}, u32[]{:S(2)}) %copy-start.1) | copy-done | bytes 4194328
  89.4 2.9 %d_ctx.1 = (bf16[2,64,512]{2,1,0:T(8,128)(2,1)S(1)}, bf16[2,64,512]{2,1,0:T(8,128)(2,1)S(1)}, bf16[2,64,512]{2,1,0:T(8,128)(2,1)S(1)}, bf16[2,64,512]{2,1,0:T(8,128)(2,1)S(1)}) custom-call(s32[2]{0:T(128)S(1)} %copy-done.9, bf16[256,1024]{1,0:T(8,128)(2,1)S(1)} %copy-done.4, bf16[256,1024]{1,0:T(8,128)(2,1)S(1)} %collective-permute-done.6.refs_1_, ...), custom_call_target="tpu_custom_call" | custom-call | tf_op jit(solution)/shard_map/d_ctx/pallas_call | solution.py:432
  93.0 3.1 %collective-permute-start.16 = (bf16[2,64,512]{2,1,0:T(8,128)(2,1)S(1)}, bf16[2,64,512]{2,1,0:T(8,128)(2,1)S(1)}, u32[]{:S(2)}, u32[]{:S(2)}) collective-permute-start(bf16[2,64,512]{2,1,0:T(8,128)(2,1)S(1)} %get-tuple-element.45), channel_id=1, source_target_pairs={{0,3},{1,0},{2,1},{3,2},{4,7},{5,4},{6,5},{7,6},{8,11},{9,8},{10,9... | collective-permute-start | bytes 393224 | tf_op jit(solution)/shard_map/ppermute | solution.py:482
  97.8 3.6 %all-to-all-done.1 = bf16[4,128,896]{2,1,0:T(8,128)(2,1)} async-done(((bf16[4,128,896]{2,1,0:T(8,128)(2,1)}), bf16[4,128,896]{2,1,0:T(8,128)(2,1)}, u32[]{:S(2)}, u32[]{:S(2)}) %all-to-all-start.1) | async-done | bytes 917536 | tf_op jit(solution)/shard_map/all_to_all | solution.py:466
  101.5 7.7 %encode.1 = (bf16[64,1792]{1,0:T(8,128)(2,1)}, bf16[512,896]{1,0:T(8,128)(2,1)}, f32[448,512]{1,0:T(8,128)}, bf16[512,896]{1,0:T(8,128)(2,1)}) custom-call(s32[2]{0:T(128)} %copy-done.8, bf16[512,896]{1,0:T(8,128)(2,1)} %bitcast.5.x_ref, bf16[64,1792]{1,0:T(8,128)(2,1)} %copy-done.7, bf16[64,1792]{1,0:T(8,128)(2,1)} %copy-done.17, ...), custom_call_target="tpu_custom_call" | custom-call | tf_op jit(solution)/shard_map/encode/pallas_call | solution.py:490
  110.0 12.2 %attention.1 = (bf16[4,256,512]{2,1,0:T(8,128)(2,1)}, bf16[4,256,512]{2,1,0:T(8,128)(2,1)}, bf16[2,64,2048]{2,1,0:T(8,128)(2,1)}) custom-call(s32[2]{0:T(128)} %copy-done.8, bf16[512,896]{1,0:T(8,128)(2,1)} %get-tuple-element.37.encoded_ref, bf16[32,4,56,512]{3,2,1,0:T(8,128)(2,1)} %bitcast.46, bf16[32,4,56,512]{3,2,1,0:T(8,128)(2,1)} %bitcast.47, ...), custom_call_target="tpu_custom_call" | custom-call | tf_op jit(solution)/shard_map/attention/pallas_call | solution.py:509
  122.1 1.9 %collective-permute-start.19 = (bf16[2,64,2048]{2,1,0:T(8,128)(2,1)}, bf16[2,64,2048]{2,1,0:T(8,128)(2,1)S(1)}, u32[]{:S(2)}, u32[]{:S(2)}) collective-permute-start(bf16[2,64,2048]{2,1,0:T(8,128)(2,1)} %get-tuple-element.48.c0), channel_id=1, source_target_pairs={{0,3},{1,0},{2,1},{3,2},{4,7},{5,4},{6,5},{7,6},{8,11},{9,8},{10,9... | collective-permute-start | bytes 1572872 | tf_op jit(solution)/shard_map/ppermute | solution.py:64
  125.7 14.3 %encoded_back.1 = bf16[64,1792]{1,0:T(8,128)(2,1)} custom-call(s32[2]{0:T(128)} %copy-done.8, bf16[4,256,512]{2,1,0:T(8,128)(2,1)} %get-tuple-element.52.d_scores_ref, bf16[4,256,512]{2,1,0:T(8,128)(2,1)} %get-tuple-element.53.probs_ref, bf16[2,64,512]{2,1,0:T(8,128)(2,1)} %copy-done.6, bf16[2,64,512]{2,1,0:T(8,128)(2,1)} %copy-done.11, ...), custom_call_target="tpu_custom_call" | custom-call | tf_op jit(solution)/shard_map/encoded_back/pallas_call | solution.py:529
  140.0 3.4 %collective-permute-start.22 = (bf16[64,1792]{1,0:T(8,128)(2,1)}, bf16[64,1792]{1,0:T(8,128)(2,1)S(1)}, u32[]{:S(2)}, u32[]{:S(2)}) collective-permute-start(bf16[64,1792]{1,0:T(8,128)(2,1)} %encoded_back.1), channel_id=1, source_target_pairs={{0,3},{1,0},{2,1},{3,2},{4,7},{5,4},{6,5},{7,6},{8,11},{9,8},{10,9... | collective-permute-start | bytes 688136 | tf_op jit(solution)/shard_map/ppermute | solution.py:64
  144.3 5.1 %collective-permute-done.21.c3 = bf16[2,64,2048]{2,1,0:T(8,128)(2,1)S(1)} collective-permute-done((bf16[2,64,2048]{2,1,0:T(8,128)(2,1)}, bf16[2,64,2048]{2,1,0:T(8,128)(2,1)S(1)}, u32[]{:S(2)}, u32[]{:S(2)}) %collective-permute-start.21) | collective-permute-done | bytes 524320 | tf_op jit(solution)/shard_map/ppermute | solution.py:64
  150.2 8.9 %outputs.1 = (bf16[256,1024]{1,0:T(8,128)(2,1)}, f32[256,1024]{1,0:T(8,128)}) custom-call(s32[2]{0:T(128)} %copy-done.8, bf16[2,64,2048]{2,1,0:T(8,128)(2,1)} %get-tuple-element.48.c0, bf16[2,64,2048]{2,1,0:T(8,128)(2,1)} %copy-done.14, bf16[2,64,2048]{2,1,0:T(8,128)(2,1)} %copy-done.15, bf16[2,64,2048]{2,1,0:T(8,128)(2,1)} %copy-done.16, ...), custom_call_target="tpu_custom_call" | custom-call | tf_op jit(solution)/shard_map/outputs/pallas_call | solution.py:556
  161.5 1.9 %fusion.5 = bf16[256,1024]{1,0:T(8,128)(2,1)} fusion(f32[256,1024]{1,0:T(8,128)S(1)} %copy-done.20, bf16[256,1792]{1,0:T(8,128)(2,1)S(1)} %bitcast.54, bf16[1024,1792]{1,0:T(8,128)(2,1)S(1)} %copy-done.3), kind=kOutput, calls=%fused_computation.4 | convolution fusion | flops 940048384 | bytes 6160384 | tf_op jit(solution)/shard_map/dot_general | solution.py:24
  (125 shorter events, 32.6 us)
Async XLA Ops:
  7.2 102.1 %all-gather.5.cloned.1.call-start = ((), (), s32[]{:S(2)}) async-start(), calls=%async_computation.2 | async-start | bytes 7569408 | tf_op jit(solution)/shard_map/all_gather | solution.py:419
  9.1 19.3 %collective-permute-start = (bf16[128,1024]{1,0:T(8,128)(2,1)}, bf16[128,1024]{1,0:T(8,128)(2,1)}, u32[]{:S(2)}, u32[]{:S(2)}) collective-permute-start(bf16[128,1024]{1,0:T(8,128)(2,1)} %get-tuple-element.63), channel_id=1, source_target_pairs={{0,3},{1,0},{2,1},{3,2},{4,7},{5,4},{6,5},{7,6},{8,11},{9,8},{10,9... | collective-permute-start | bytes 786440 | tf_op jit(solution)/shard_map/ppermute | solution.py:85
  13.1 15.2 %collective-permute-start.3 = (bf16[128,1024]{1,0:T(8,128)(2,1)}, bf16[128,1024]{1,0:T(8,128)(2,1)}, u32[]{:S(2)}, u32[]{:S(2)}) collective-permute-start(bf16[128,1024]{1,0:T(8,128)(2,1)} %get-tuple-element.62), channel_id=1, source_target_pairs={{0,1},{1,2},{2,3},{3,0},{4,5},{5,6},{6,7},{7,4},{8,9},{9,10},{10,1... | collective-permute-start | bytes 786440 | tf_op jit(solution)/shard_map/ppermute | solution.py:86
  28.4 50.9 %all-to-all-start = ((bf16[32,32,896]{2,1,0:T(8,128)(2,1)}), bf16[32,32,896]{2,1,0:T(8,128)(2,1)}, u32[]{:S(2)}, u32[]{:S(2)}) async-start(bf16[32,32,896]{2,1,0:T(8,128)(2,1)} %param.16), calls=%async_computation | async-start | bytes 3670016 | tf_op jit(solution)/shard_map/all_to_all | solution.py:461
  36.1 113.3 %all-gather.7.cloned.1.call-start = ((), (), s32[]{:S(2)}) async-start(), calls=%async_computation.3 | async-start | bytes 8650752 | tf_op jit(solution)/shard_map/all_gather | solution.py:469
  36.2 14.9 %collective-permute-start.6 = (bf16[256,1024]{1,0:T(8,128)(2,1)S(1)}, bf16[256,1024]{1,0:T(8,128)(2,1)S(1)}, u32[]{:S(2)}, u32[]{:S(2)}) collective-permute-start(bf16[256,1024]{1,0:T(8,128)(2,1)S(1)} %copy-done.4), channel_id=1, source_target_pairs={{0,3},{1,0},{2,1},{3,2},{4,7},{5,4},{6,5},{7,6},{8,11},{9,8},{10,9... | collective-permute-start | bytes 1572872 | tf_op jit(solution)/shard_map/ppermute | solution.py:73
  36.8 24.1 %collective-permute-start.1 = (bf16[128,1024]{1,0:T(8,128)(2,1)}, bf16[128,1024]{1,0:T(8,128)(2,1)}, u32[]{:S(2)}, u32[]{:S(2)}) collective-permute-start(bf16[128,1024]{1,0:T(8,128)(2,1)} %get-tuple-element.62), channel_id=1, source_target_pairs={{0,3},{1,0},{2,1},{3,2},{4,7},{5,4},{6,5},{7,6},{8,11},{9,8},{10,9... | collective-permute-start | bytes 786440 | tf_op jit(solution)/shard_map/ppermute | solution.py:87
  37.6 24.0 %collective-permute-start.5 = (bf16[128,1024]{1,0:T(8,128)(2,1)}, bf16[128,1024]{1,0:T(8,128)(2,1)}, u32[]{:S(2)}, u32[]{:S(2)}) collective-permute-start(bf16[128,1024]{1,0:T(8,128)(2,1)} %get-tuple-element.63), channel_id=1, source_target_pairs={{0,1},{1,2},{2,3},{3,0},{4,5},{5,6},{6,7},{7,4},{8,9},{9,10},{10,1... | collective-permute-start | bytes 786440 | tf_op jit(solution)/shard_map/ppermute | solution.py:88
  38.8 20.7 %collective-permute-start.8 = (bf16[256,1024]{1,0:T(8,128)(2,1)S(1)}, bf16[256,1024]{1,0:T(8,128)(2,1)S(1)}, u32[]{:S(2)}, u32[]{:S(2)}) collective-permute-start(bf16[256,1024]{1,0:T(8,128)(2,1)S(1)} %copy-done.4), channel_id=1, source_target_pairs={{0,1},{1,2},{2,3},{3,0},{4,5},{5,6},{6,7},{7,4},{8,9},{9,10},{10,1... | collective-permute-start | bytes 1572872 | tf_op jit(solution)/shard_map/ppermute | solution.py:74
  40.4 22.2 %collective-permute-start.2 = (bf16[128,1024]{1,0:T(8,128)(2,1)}, bf16[128,1024]{1,0:T(8,128)(2,1)}, u32[]{:S(2)}, u32[]{:S(2)}) collective-permute-start(bf16[128,1024]{1,0:T(8,128)(2,1)} %collective-permute-done.refs_1_), channel_id=1, source_target_pairs={{0,3},{1,0},{2,1},{3,2},{4,7},{5,4},{6,5},{7,6},{8,11},{9,8},{10,9... | collective-permute-start | bytes 786440 | tf_op jit(solution)/shard_map/ppermute | solution.py:89
  51.1 18.1 %collective-permute-start.4 = (bf16[128,1024]{1,0:T(8,128)(2,1)}, bf16[128,1024]{1,0:T(8,128)(2,1)}, u32[]{:S(2)}, u32[]{:S(2)}) collective-permute-start(bf16[128,1024]{1,0:T(8,128)(2,1)} %collective-permute-done.3.refs_6_), channel_id=1, source_target_pairs={{0,1},{1,2},{2,3},{3,0},{4,5},{5,6},{6,7},{7,4},{8,9},{9,10},{10,1... | collective-permute-start | bytes 786440 | tf_op jit(solution)/shard_map/ppermute | solution.py:90
  59.5 17.2 %collective-permute-start.10 = (bf16[64,1792]{1,0:T(8,128)(2,1)S(1)}, bf16[64,1792]{1,0:T(8,128)(2,1)S(1)}, u32[]{:S(2)}, u32[]{:S(2)}) collective-permute-start(bf16[64,1792]{1,0:T(8,128)(2,1)S(1)} %get-tuple-element.32), channel_id=1, source_target_pairs={{0,3},{1,0},{2,1},{3,2},{4,7},{5,4},{6,5},{7,6},{8,11},{9,8},{10,9... | collective-permute-start | bytes 688136 | tf_op jit(solution)/shard_map/ppermute | solution.py:421
  60.9 15.8 %collective-permute-start.11 = (bf16[64,1792]{1,0:T(8,128)(2,1)S(1)}, bf16[64,1792]{1,0:T(8,128)(2,1)}, u32[]{:S(2)}, u32[]{:S(2)}) collective-permute-start(bf16[64,1792]{1,0:T(8,128)(2,1)S(1)} %get-tuple-element.33), channel_id=1, source_target_pairs={{0,2},{1,3},{2,0},{3,1},{4,6},{5,7},{6,4},{7,5},{8,10},{9,11},{10,... | collective-permute-start | bytes 688136 | tf_op jit(solution)/shard_map/ppermute | solution.py:421
  61.7 15.0 %collective-permute-start.12 = (bf16[64,1792]{1,0:T(8,128)(2,1)S(1)}, bf16[64,1792]{1,0:T(8,128)(2,1)}, u32[]{:S(2)}, u32[]{:S(2)}) collective-permute-start(bf16[64,1792]{1,0:T(8,128)(2,1)S(1)} %get-tuple-element.34), channel_id=1, source_target_pairs={{0,1},{1,2},{2,3},{3,0},{4,5},{5,6},{6,7},{7,4},{8,9},{9,10},{10,1... | collective-permute-start | bytes 688136 | tf_op jit(solution)/shard_map/ppermute | solution.py:421
  62.6 14.4 %collective-permute-start.7 = (bf16[128,1024]{1,0:T(8,128)(2,1)S(1)}, bf16[128,1024]{1,0:T(8,128)(2,1)S(1)}, u32[]{:S(2)}, u32[]{:S(2)}) collective-permute-start(bf16[128,1024]{1,0:T(8,128)(2,1)S(1)} %slice.50), channel_id=1, source_target_pairs={{0,3},{1,0},{2,1},{3,2},{4,7},{5,4},{6,5},{7,6},{8,11},{9,8},{10,9... | collective-permute-start | bytes 786440 | tf_op jit(solution)/shard_map/ppermute | solution.py:75
  82.8 18.7 %all-to-all-start.1 = ((bf16[4,128,896]{2,1,0:T(8,128)(2,1)}), bf16[4,128,896]{2,1,0:T(8,128)(2,1)}, u32[]{:S(2)}, u32[]{:S(2)}) async-start(bf16[4,128,896]{2,1,0:T(8,128)(2,1)} %bitcast.53), calls=%async_computation.1 | async-start | bytes 1835008 | tf_op jit(solution)/shard_map/all_to_all | solution.py:466
  93.0 16.2 %collective-permute-start.16 = (bf16[2,64,512]{2,1,0:T(8,128)(2,1)S(1)}, bf16[2,64,512]{2,1,0:T(8,128)(2,1)S(1)}, u32[]{:S(2)}, u32[]{:S(2)}) collective-permute-start(bf16[2,64,512]{2,1,0:T(8,128)(2,1)S(1)} %get-tuple-element.45), channel_id=1, source_target_pairs={{0,3},{1,0},{2,1},{3,2},{4,7},{5,4},{6,5},{7,6},{8,11},{9,8},{10,9... | collective-permute-start | bytes 393224 | tf_op jit(solution)/shard_map/ppermute | solution.py:482
  96.1 13.1 %collective-permute-start.17 = (bf16[2,64,512]{2,1,0:T(8,128)(2,1)S(1)}, bf16[2,64,512]{2,1,0:T(8,128)(2,1)S(1)}, u32[]{:S(2)}, u32[]{:S(2)}) collective-permute-start(bf16[2,64,512]{2,1,0:T(8,128)(2,1)S(1)} %get-tuple-element.46), channel_id=1, source_target_pairs={{0,2},{1,3},{2,0},{3,1},{4,6},{5,7},{6,4},{7,5},{8,10},{9,11},{10,... | collective-permute-start | bytes 393224 | tf_op jit(solution)/shard_map/ppermute | solution.py:482
  122.1 17.9 %collective-permute-start.19 = (bf16[2,64,2048]{2,1,0:T(8,128)(2,1)}, bf16[2,64,2048]{2,1,0:T(8,128)(2,1)S(1)}, u32[]{:S(2)}, u32[]{:S(2)}) collective-permute-start(bf16[2,64,2048]{2,1,0:T(8,128)(2,1)} %get-tuple-element.48.c0), channel_id=1, source_target_pairs={{0,3},{1,0},{2,1},{3,2},{4,7},{5,4},{6,5},{7,6},{8,11},{9,8},{10,9... | collective-permute-start | bytes 1572872 | tf_op jit(solution)/shard_map/ppermute | solution.py:64
  124.1 20.2 %collective-permute-start.20 = (bf16[2,64,2048]{2,1,0:T(8,128)(2,1)}, bf16[2,64,2048]{2,1,0:T(8,128)(2,1)S(1)}, u32[]{:S(2)}, u32[]{:S(2)}) collective-permute-start(bf16[2,64,2048]{2,1,0:T(8,128)(2,1)} %get-tuple-element.48.c0), channel_id=1, source_target_pairs={{0,2},{1,3},{2,0},{3,1},{4,6},{5,7},{6,4},{7,5},{8,10},{9,11},{10,... | collective-permute-start | bytes 1572872 | tf_op jit(solution)/shard_map/ppermute | solution.py:64
  125.6 23.8 %collective-permute-start.21 = (bf16[2,64,2048]{2,1,0:T(8,128)(2,1)}, bf16[2,64,2048]{2,1,0:T(8,128)(2,1)S(1)}, u32[]{:S(2)}, u32[]{:S(2)}) collective-permute-start(bf16[2,64,2048]{2,1,0:T(8,128)(2,1)} %get-tuple-element.48.c0), channel_id=1, source_target_pairs={{0,1},{1,2},{2,3},{3,0},{4,5},{5,6},{6,7},{7,4},{8,9},{9,10},{10,1... | collective-permute-start | bytes 1572872 | tf_op jit(solution)/shard_map/ppermute | solution.py:64
  140.0 19.0 %collective-permute-start.22 = (bf16[64,1792]{1,0:T(8,128)(2,1)}, bf16[64,1792]{1,0:T(8,128)(2,1)S(1)}, u32[]{:S(2)}, u32[]{:S(2)}) collective-permute-start(bf16[64,1792]{1,0:T(8,128)(2,1)} %encoded_back.1), channel_id=1, source_target_pairs={{0,3},{1,0},{2,1},{3,2},{4,7},{5,4},{6,5},{7,6},{8,11},{9,8},{10,9... | collective-permute-start | bytes 688136 | tf_op jit(solution)/shard_map/ppermute | solution.py:64
  143.4 15.7 %collective-permute-start.23 = (bf16[64,1792]{1,0:T(8,128)(2,1)}, bf16[64,1792]{1,0:T(8,128)(2,1)S(1)}, u32[]{:S(2)}, u32[]{:S(2)}) collective-permute-start(bf16[64,1792]{1,0:T(8,128)(2,1)} %encoded_back.1), channel_id=1, source_target_pairs={{0,2},{1,3},{2,0},{3,1},{4,6},{5,7},{6,4},{7,5},{8,10},{9,11},{10,... | collective-permute-start | bytes 688136 | tf_op jit(solution)/shard_map/ppermute | solution.py:64
  144.1 14.9 %collective-permute-start.24 = (bf16[64,1792]{1,0:T(8,128)(2,1)}, bf16[64,1792]{1,0:T(8,128)(2,1)S(1)}, u32[]{:S(2)}, u32[]{:S(2)}) collective-permute-start(bf16[64,1792]{1,0:T(8,128)(2,1)} %encoded_back.1), channel_id=1, source_target_pairs={{0,1},{1,2},{2,3},{3,0},{4,5},{5,6},{6,7},{7,4},{8,9},{9,10},{10,1... | collective-permute-start | bytes 688136 | tf_op jit(solution)/shard_map/ppermute | solution.py:64
  (27 other events, 153.8 us)
Sparse Core Ops, SparseCore 0:
  28.5 60.9 all-gather.4
  92.4 52.3 all-gather.6

commit v7 on v6

--- a/solution.py
+++ b/solution.py
@@ -561,7 +561,7 @@
         (out_spec, out_spec),
         (sds((tokens, part_width), BF16), sds((tokens, part_width), F32)),
         [pltpu.VMEM((2, tokens, head_width), BF16), acc, acc],
-        60,
+        40,
     )(scalars, *both_parts, qo_all, qo_all, hidden, cotangent)
     d_cond_parts = after(d_cond_parts, from_query)
     d_cond_all = lax.dynamic_slice_in_dim(

time: 171 us -> 172 us (level)
  local copies, waits for them, and re-layouts: 16.3 us -> 20.7 us
  Pallas kernels: 53.7 us -> 50.8 us
    unnamed x51, local copies, waits for them, and re-layouts: 9.47 us -> 12.9 us
    pallas_call x1, Pallas kernels: 8.85 us -> 5.79 us  [shards(): call(functools.partial(outputs_kernel, shift), 'outputs', n_tensor, [both...]
  transfers between devices with their start and end apart: 29 -> 29, of which waited for: 8 -> 8; matrix products, arithmetic and copies ran while one was open for 6% -> 6% of each run, Pallas kernels for 32% -> 30%
where the time goes in v7:
time: 172 us
  Pallas kernels  50.8 us (30%)
  starting transfers between devices  46 us (27%)
  waiting for transfers between devices  32.2 us (19%)
  local copies, waits for them, and re-layouts  20.7 us (12%)
  between operations  14.5 us (8%)
  matrix products  4.24 us (2%)
  other arithmetic  3.21 us (2%)
    pallas_call x1, Pallas kernels, shards(): call(encoded_back_kernel, 'encoded_back', n_tensor, [group(head_rows, row...  14.5 us
    unnamed x51, local copies, waits for them, and re-layouts  12.9 us
    pallas_call x1, Pallas kernels, shards(): call(attention_kernel, 'attention', n_tensor, [r_spec, kv_spec(0), kv_spe...  12.2 us
    pallas_call x2, Pallas kernels, projected(): call(functools.partial(project_kernel, dims, shift, counts), name, n_tens...  8.87 us
    ppermute x1, waiting for transfers between devices, spread_ring(): next_one = lax.ppermute(shard, axis, down)  8.86 us
    ppermute x6, starting transfers between devices, shards(): lax.ppermute(array, 'tensor', [(i, (i - k) % n_tensor) for i in range(n_t...  7.85 us
    ppermute x6, starting transfers between devices, spread(): lax.ppermute(shard, axis, [(i, (i - k) % size) for i in range(size)])  7.82 us
    pallas_call x1, Pallas kernels, shards(): call(encode_kernel, 'encode', 1, [r_spec] + [c_spec] * 4 + [w_spec] * 2,...  7.74 us
  transfers between devices with their start and end apart: 29, of which 8 were waited for; matrix products, arithmetic and copies ran while one was open for 6% of the time, Pallas kernels for 30%

profile of v7, /device:TPU:10, one launch (start us, length us, event | category | flops | bytes accessed | tf_op | source)
XLA Modules:
  0.0 171.6 jit_solution(13866108101401932008)
XLA Ops:
  9.1 4.0 %collective-permute-start = (bf16[128,1024]{1,0:T(8,128)(2,1)}, bf16[128,1024]{1,0:T(8,128)(2,1)}, u32[]{:S(2)}, u32[]{:S(2)}) collective-permute-start(bf16[128,1024]{1,0:T(8,128)(2,1)} %get-tuple-element.63), channel_id=1, source_target_pairs={{0,3},{1,0},{2,1},{3,2},{4,7},{5,4},{6,5},{7,6},{8,11},{9,8},{10,9... | collective-permute-start | bytes 786440 | tf_op jit(solution)/shard_map/ppermute | solution.py:85
  16.2 4.7 %collective-permute-start.14 = (bf16[120,512]{1,0:T(8,128)(2,1)S(1)}, bf16[120,512]{1,0:T(8,128)(2,1)S(1)}, u32[]{:S(2)}, u32[]{:S(2)}) collective-permute-start(bf16[120,512]{1,0:T(8,128)(2,1)S(1)} %get-tuple-element.66), channel_id=1, source_target_pairs={{0,2},{1,3},{2,0},{3,1},{4,6},{5,7},{6,4},{7,5},{8,10},{9,11},{10,... | collective-permute-start | bytes 368648 | tf_op jit(solution)/shard_map/ppermute | solution.py:58
  22.3 2.0 %copy-done.4 = bf16[1024,1792]{1,0:T(8,128)(2,1)S(1)} copy-done((bf16[1024,1792]{1,0:T(8,128)(2,1)S(1)}, bf16[1024,1792]{1,0:T(8,128)(2,1)}, u32[]{:S(2)}) %copy-start.4) | copy-done | bytes 3670040
  28.4 7.7 %all-to-all-start = ((bf16[32,32,896]{2,1,0:T(8,128)(2,1)}), bf16[32,32,896]{2,1,0:T(8,128)(2,1)}, u32[]{:S(2)}, u32[]{:S(2)}) async-start(bf16[32,32,896]{2,1,0:T(8,128)(2,1)} %param.16), calls=%async_computation | async-start | bytes 3670016 | tf_op jit(solution)/shard_map/all_to_all | solution.py:461
  42.2 8.9 %collective-permute-done.6.refs_1_ = bf16[256,1024]{1,0:T(8,128)(2,1)S(1)} collective-permute-done((bf16[256,1024]{1,0:T(8,128)(2,1)S(1)}, bf16[256,1024]{1,0:T(8,128)(2,1)S(1)}, u32[]{:S(2)}, u32[]{:S(2)}) %collective-permute-start.6) | collective-permute-done | bytes 524320 | tf_op jit(solution)/shard_map/ppermute | solution.py:73
  52.4 7.2 %collective-permute-done.8.refs_4_ = bf16[256,1024]{1,0:T(8,128)(2,1)S(1)} collective-permute-done((bf16[256,1024]{1,0:T(8,128)(2,1)S(1)}, bf16[256,1024]{1,0:T(8,128)(2,1)S(1)}, u32[]{:S(2)}, u32[]{:S(2)}) %collective-permute-start.8) | collective-permute-done | bytes 524320 | tf_op jit(solution)/shard_map/ppermute | solution.py:74
  62.6 2.3 %collective-permute-start.7 = (bf16[128,1024]{1,0:T(8,128)(2,1)S(1)}, bf16[128,1024]{1,0:T(8,128)(2,1)S(1)}, u32[]{:S(2)}, u32[]{:S(2)}) collective-permute-start(bf16[128,1024]{1,0:T(8,128)(2,1)S(1)} %slice.50), channel_id=1, source_target_pairs={{0,3},{1,0},{2,1},{3,2},{4,7},{5,4},{6,5},{7,6},{8,11},{9,8},{10,9... | collective-permute-start | bytes 786440 | tf_op jit(solution)/shard_map/ppermute | solution.py:75
  64.9 4.3 %collective-permute-done.4.refs_4_ = bf16[128,1024]{1,0:T(8,128)(2,1)} collective-permute-done((bf16[128,1024]{1,0:T(8,128)(2,1)}, bf16[128,1024]{1,0:T(8,128)(2,1)}, u32[]{:S(2)}, u32[]{:S(2)}) %collective-permute-start.4) | collective-permute-done | bytes 262176 | tf_op jit(solution)/shard_map/ppermute | solution.py:90
  70.7 5.9 %query.1.refs_6_ = bf16[256,512]{1,0:T(8,128)(2,1)} custom-call(s32[2]{0:T(128)} %copy-done.11, bf16[256,1024]{1,0:T(8,128)(2,1)} %hidden_ref.3, bf16[128,1024]{1,0:T(8,128)(2,1)} %collective-permute-done.refs_1_, bf16[128,1024]{1,0:T(8,128)(2,1)} %collective-permute-done.1.refs_2_, bf16[128,1024]{1,0:T(8,128)(2,1)} %collective-permute-done.2.refs_3_, ...), custom_call_target="tpu_custom_call" | custom-call | tf_op jit(solution)/shard_map/query/pallas_call | solution.py:432
  77.0 2.2 %collective-permute-done.9.refs_3_ = bf16[128,1024]{1,0:T(8,128)(2,1)S(1)} collective-permute-done((bf16[128,1024]{1,0:T(8,128)(2,1)S(1)}, bf16[128,1024]{1,0:T(8,128)(2,1)S(1)}, u32[]{:S(2)}, u32[]{:S(2)}) %collective-permute-start.9) | collective-permute-done | bytes 262176 | tf_op jit(solution)/shard_map/ppermute | solution.py:76
  79.3 2.3 %fusion.2 = bf16[16,32,896]{2,0,1:T(8,128)(2,1)S(1)} fusion(bf16[32,32,896]{2,1,0:T(8,128)(2,1)} %all-to-all-done, s32[16]{0:T(128)S(1)} %eq.23, pred[16]{0:T(512)(128)(4,1)S(1)} %lt.78), kind=kOutput, calls=%fused_computation.2 | convolution fusion | flops 29819904 | bytes 2752592 | tf_op jit(solution)/shard_map/si,sre->ire/dot_general | solution.py:462
  82.8 4.3 %all-to-all-start.1 = ((bf16[4,128,896]{2,1,0:T(8,128)(2,1)}), bf16[4,128,896]{2,1,0:T(8,128)(2,1)}, u32[]{:S(2)}, u32[]{:S(2)}) async-start(bf16[4,128,896]{2,1,0:T(8,128)(2,1)} %bitcast.53), calls=%async_computation.1 | async-start | bytes 1835008 | tf_op jit(solution)/shard_map/all_to_all | solution.py:466
  87.1 2.3 %copy-done.3 = bf16[512,4096]{1,0:T(8,128)(2,1)S(1)} copy-done((bf16[512,4096]{1,0:T(8,128)(2,1)S(1)}, bf16[512,4096]{1,0:T(8,128)(2,1)}, u32[]{:S(2)}) %copy-start.3) | copy-done | bytes 4194328
  89.4 2.9 %d_ctx.1 = (bf16[2,64,512]{2,1,0:T(8,128)(2,1)S(1)}, bf16[2,64,512]{2,1,0:T(8,128)(2,1)S(1)}, bf16[2,64,512]{2,1,0:T(8,128)(2,1)S(1)}, bf16[2,64,512]{2,1,0:T(8,128)(2,1)S(1)}) custom-call(s32[2]{0:T(128)S(1)} %copy-done.12, bf16[256,1024]{1,0:T(8,128)(2,1)S(1)} %copy-done.6, bf16[256,1024]{1,0:T(8,128)(2,1)S(1)} %collective-permute-done.6.refs_1_, ...), custom_call_target="tpu_custom_call" | custom-call | tf_op jit(solution)/shard_map/d_ctx/pallas_call | solution.py:432
  93.0 3.1 %collective-permute-start.16 = (bf16[2,64,512]{2,1,0:T(8,128)(2,1)S(1)}, bf16[2,64,512]{2,1,0:T(8,128)(2,1)S(1)}, u32[]{:S(2)}, u32[]{:S(2)}) collective-permute-start(bf16[2,64,512]{2,1,0:T(8,128)(2,1)S(1)} %get-tuple-element.45), channel_id=1, source_target_pairs={{0,3},{1,0},{2,1},{3,2},{4,7},{5,4},{6,5},{7,6},{8,11},{9,8},{10,9... | collective-permute-start | bytes 393224 | tf_op jit(solution)/shard_map/ppermute | solution.py:482
  97.8 3.6 %all-to-all-done.1 = bf16[4,128,896]{2,1,0:T(8,128)(2,1)} async-done(((bf16[4,128,896]{2,1,0:T(8,128)(2,1)}), bf16[4,128,896]{2,1,0:T(8,128)(2,1)}, u32[]{:S(2)}, u32[]{:S(2)}) %all-to-all-start.1) | async-done | bytes 917536 | tf_op jit(solution)/shard_map/all_to_all | solution.py:466
  101.5 7.7 %encode.1 = (bf16[64,1792]{1,0:T(8,128)(2,1)}, bf16[512,896]{1,0:T(8,128)(2,1)}, f32[448,512]{1,0:T(8,128)}, bf16[512,896]{1,0:T(8,128)(2,1)}) custom-call(s32[2]{0:T(128)} %copy-done.11, bf16[512,896]{1,0:T(8,128)(2,1)} %bitcast.5.x_ref, bf16[64,1792]{1,0:T(8,128)(2,1)} %copy-done.10, bf16[64,1792]{1,0:T(8,128)(2,1)} %copy-done.18, ...), custom_call_target="tpu_custom_call" | custom-call | tf_op jit(solution)/shard_map/encode/pallas_call | solution.py:490
  110.0 12.2 %attention.1 = (bf16[4,256,512]{2,1,0:T(8,128)(2,1)}, bf16[4,256,512]{2,1,0:T(8,128)(2,1)}, bf16[2,64,2048]{2,1,0:T(8,128)(2,1)}) custom-call(s32[2]{0:T(128)} %copy-done.11, bf16[512,896]{1,0:T(8,128)(2,1)} %get-tuple-element.37.encoded_ref, bf16[32,4,56,512]{3,2,1,0:T(8,128)(2,1)} %bitcast.48, bf16[32,4,56,512]{3,2,1,0:T(8,128)(2,1)} %bitcast.49, ...), custom_call_target="tpu_custom_call" | custom-call | tf_op jit(solution)/shard_map/attention/pallas_call | solution.py:509
  125.7 14.5 %encoded_back.1 = bf16[64,1792]{1,0:T(8,128)(2,1)} custom-call(s32[2]{0:T(128)} %copy-done.11, bf16[4,256,512]{2,1,0:T(8,128)(2,1)} %get-tuple-element.52.d_scores_ref, bf16[4,256,512]{2,1,0:T(8,128)(2,1)} %get-tuple-element.53.probs_ref, bf16[2,64,512]{2,1,0:T(8,128)(2,1)} %copy-done.8, bf16[2,64,512]{2,1,0:T(8,128)(2,1)} %copy-done.15, ...), custom_call_target="tpu_custom_call" | custom-call | tf_op jit(solution)/shard_map/encoded_back/pallas_call | solution.py:529
  140.2 3.4 %collective-permute-start.22 = (bf16[64,1792]{1,0:T(8,128)(2,1)}, bf16[64,1792]{1,0:T(8,128)(2,1)S(1)}, u32[]{:S(2)}, u32[]{:S(2)}) collective-permute-start(bf16[64,1792]{1,0:T(8,128)(2,1)} %encoded_back.1), channel_id=1, source_target_pairs={{0,3},{1,0},{2,1},{3,2},{4,7},{5,4},{6,5},{7,6},{8,11},{9,8},{10,9... | collective-permute-start | bytes 688136 | tf_op jit(solution)/shard_map/ppermute | solution.py:64
  144.5 4.9 %collective-permute-done.21.c3 = bf16[2,64,2048]{2,1,0:T(8,128)(2,1)S(1)} collective-permute-done((bf16[2,64,2048]{2,1,0:T(8,128)(2,1)}, bf16[2,64,2048]{2,1,0:T(8,128)(2,1)S(1)}, u32[]{:S(2)}, u32[]{:S(2)}) %collective-permute-start.21) | collective-permute-done | bytes 524320 | tf_op jit(solution)/shard_map/ppermute | solution.py:64
  149.4 3.4 %copy-done = bf16[128,64,512]{2,1,0:T(8,128)(2,1)S(1)} copy-done((bf16[128,64,512]{2,1,0:T(8,128)(2,1)S(1)}, bf16[128,64,512]{2,1,0:T(8,128)(2,1)}, u32[]{:S(2)}) %copy-start) | copy-done | bytes 8388632
  152.8 5.8 %outputs.1 = (bf16[256,1024]{1,0:T(8,128)(2,1)}, f32[256,1024]{1,0:T(8,128)S(1)}) custom-call(s32[2]{0:T(128)S(1)} %copy-done.13, bf16[2,64,2048]{2,1,0:T(8,128)(2,1)S(1)} %copy-done.9, bf16[2,64,2048]{2,1,0:T(8,128)(2,1)S(1)} %collective-permute-done.19.c1, bf16[2,64,2048]{2,1,0:T(8,128)(2,1)S(1)} %collective-permute-done.20.c2, ...), custom_call_target="tpu_custom_call" | custom-call | tf_op jit(solution)/shard_map/outputs/pallas_call | solution.py:556
  162.8 1.9 %fusion.5 = bf16[256,1024]{1,0:T(8,128)(2,1)} fusion(f32[256,1024]{1,0:T(8,128)S(1)} %get-tuple-element.51, bf16[256,1792]{1,0:T(8,128)(2,1)S(1)} %bitcast.54, bf16[1024,1792]{1,0:T(8,128)(2,1)S(1)} %copy-done.5), kind=kOutput, calls=%fused_computation.4 | convolution fusion | flops 940048384 | bytes 6160384 | tf_op jit(solution)/shard_map/dot_general | solution.py:24
  (125 shorter events, 35.6 us)
Async XLA Ops:
  7.2 102.1 %all-gather.5.cloned.1.call-start = ((), (), s32[]{:S(2)}) async-start(), calls=%async_computation.2 | async-start | bytes 7569408 | tf_op jit(solution)/shard_map/all_gather | solution.py:419
  9.1 19.3 %collective-permute-start = (bf16[128,1024]{1,0:T(8,128)(2,1)}, bf16[128,1024]{1,0:T(8,128)(2,1)}, u32[]{:S(2)}, u32[]{:S(2)}) collective-permute-start(bf16[128,1024]{1,0:T(8,128)(2,1)} %get-tuple-element.63), channel_id=1, source_target_pairs={{0,3},{1,0},{2,1},{3,2},{4,7},{5,4},{6,5},{7,6},{8,11},{9,8},{10,9... | collective-permute-start | bytes 786440 | tf_op jit(solution)/shard_map/ppermute | solution.py:85
  13.1 15.2 %collective-permute-start.3 = (bf16[128,1024]{1,0:T(8,128)(2,1)}, bf16[128,1024]{1,0:T(8,128)(2,1)}, u32[]{:S(2)}, u32[]{:S(2)}) collective-permute-start(bf16[128,1024]{1,0:T(8,128)(2,1)} %get-tuple-element.62), channel_id=1, source_target_pairs={{0,1},{1,2},{2,3},{3,0},{4,5},{5,6},{6,7},{7,4},{8,9},{9,10},{10,1... | collective-permute-start | bytes 786440 | tf_op jit(solution)/shard_map/ppermute | solution.py:86
  28.4 50.9 %all-to-all-start = ((bf16[32,32,896]{2,1,0:T(8,128)(2,1)}), bf16[32,32,896]{2,1,0:T(8,128)(2,1)}, u32[]{:S(2)}, u32[]{:S(2)}) async-start(bf16[32,32,896]{2,1,0:T(8,128)(2,1)} %param.16), calls=%async_computation | async-start | bytes 3670016 | tf_op jit(solution)/shard_map/all_to_all | solution.py:461
  36.1 113.3 %all-gather.7.cloned.1.call-start = ((), (), s32[]{:S(2)}) async-start(), calls=%async_computation.3 | async-start | bytes 8650752 | tf_op jit(solution)/shard_map/all_gather | solution.py:469
  36.2 14.9 %collective-permute-start.6 = (bf16[256,1024]{1,0:T(8,128)(2,1)S(1)}, bf16[256,1024]{1,0:T(8,128)(2,1)S(1)}, u32[]{:S(2)}, u32[]{:S(2)}) collective-permute-start(bf16[256,1024]{1,0:T(8,128)(2,1)S(1)} %copy-done.6), channel_id=1, source_target_pairs={{0,3},{1,0},{2,1},{3,2},{4,7},{5,4},{6,5},{7,6},{8,11},{9,8},{10,9... | collective-permute-start | bytes 1572872 | tf_op jit(solution)/shard_map/ppermute | solution.py:73
  36.8 24.1 %collective-permute-start.1 = (bf16[128,1024]{1,0:T(8,128)(2,1)}, bf16[128,1024]{1,0:T(8,128)(2,1)}, u32[]{:S(2)}, u32[]{:S(2)}) collective-permute-start(bf16[128,1024]{1,0:T(8,128)(2,1)} %get-tuple-element.62), channel_id=1, source_target_pairs={{0,3},{1,0},{2,1},{3,2},{4,7},{5,4},{6,5},{7,6},{8,11},{9,8},{10,9... | collective-permute-start | bytes 786440 | tf_op jit(solution)/shard_map/ppermute | solution.py:87
  37.6 24.0 %collective-permute-start.5 = (bf16[128,1024]{1,0:T(8,128)(2,1)}, bf16[128,1024]{1,0:T(8,128)(2,1)}, u32[]{:S(2)}, u32[]{:S(2)}) collective-permute-start(bf16[128,1024]{1,0:T(8,128)(2,1)} %get-tuple-element.63), channel_id=1, source_target_pairs={{0,1},{1,2},{2,3},{3,0},{4,5},{5,6},{6,7},{7,4},{8,9},{9,10},{10,1... | collective-permute-start | bytes 786440 | tf_op jit(solution)/shard_map/ppermute | solution.py:88
  38.8 20.7 %collective-permute-start.8 = (bf16[256,1024]{1,0:T(8,128)(2,1)S(1)}, bf16[256,1024]{1,0:T(8,128)(2,1)S(1)}, u32[]{:S(2)}, u32[]{:S(2)}) collective-permute-start(bf16[256,1024]{1,0:T(8,128)(2,1)S(1)} %copy-done.6), channel_id=1, source_target_pairs={{0,1},{1,2},{2,3},{3,0},{4,5},{5,6},{6,7},{7,4},{8,9},{9,10},{10,1... | collective-permute-start | bytes 1572872 | tf_op jit(solution)/shard_map/ppermute | solution.py:74
  40.4 22.2 %collective-permute-start.2 = (bf16[128,1024]{1,0:T(8,128)(2,1)}, bf16[128,1024]{1,0:T(8,128)(2,1)}, u32[]{:S(2)}, u32[]{:S(2)}) collective-permute-start(bf16[128,1024]{1,0:T(8,128)(2,1)} %collective-permute-done.refs_1_), channel_id=1, source_target_pairs={{0,3},{1,0},{2,1},{3,2},{4,7},{5,4},{6,5},{7,6},{8,11},{9,8},{10,9... | collective-permute-start | bytes 786440 | tf_op jit(solution)/shard_map/ppermute | solution.py:89
  51.1 18.1 %collective-permute-start.4 = (bf16[128,1024]{1,0:T(8,128)(2,1)}, bf16[128,1024]{1,0:T(8,128)(2,1)}, u32[]{:S(2)}, u32[]{:S(2)}) collective-permute-start(bf16[128,1024]{1,0:T(8,128)(2,1)} %collective-permute-done.3.refs_6_), channel_id=1, source_target_pairs={{0,1},{1,2},{2,3},{3,0},{4,5},{5,6},{6,7},{7,4},{8,9},{9,10},{10,1... | collective-permute-start | bytes 786440 | tf_op jit(solution)/shard_map/ppermute | solution.py:90
  59.5 17.2 %collective-permute-start.10 = (bf16[64,1792]{1,0:T(8,128)(2,1)S(1)}, bf16[64,1792]{1,0:T(8,128)(2,1)S(1)}, u32[]{:S(2)}, u32[]{:S(2)}) collective-permute-start(bf16[64,1792]{1,0:T(8,128)(2,1)S(1)} %get-tuple-element.32), channel_id=1, source_target_pairs={{0,3},{1,0},{2,1},{3,2},{4,7},{5,4},{6,5},{7,6},{8,11},{9,8},{10,9... | collective-permute-start | bytes 688136 | tf_op jit(solution)/shard_map/ppermute | solution.py:421
  60.9 15.8 %collective-permute-start.11 = (bf16[64,1792]{1,0:T(8,128)(2,1)S(1)}, bf16[64,1792]{1,0:T(8,128)(2,1)}, u32[]{:S(2)}, u32[]{:S(2)}) collective-permute-start(bf16[64,1792]{1,0:T(8,128)(2,1)S(1)} %get-tuple-element.33), channel_id=1, source_target_pairs={{0,2},{1,3},{2,0},{3,1},{4,6},{5,7},{6,4},{7,5},{8,10},{9,11},{10,... | collective-permute-start | bytes 688136 | tf_op jit(solution)/shard_map/ppermute | solution.py:421
  61.7 15.0 %collective-permute-start.12 = (bf16[64,1792]{1,0:T(8,128)(2,1)S(1)}, bf16[64,1792]{1,0:T(8,128)(2,1)}, u32[]{:S(2)}, u32[]{:S(2)}) collective-permute-start(bf16[64,1792]{1,0:T(8,128)(2,1)S(1)} %get-tuple-element.34), channel_id=1, source_target_pairs={{0,1},{1,2},{2,3},{3,0},{4,5},{5,6},{6,7},{7,4},{8,9},{9,10},{10,1... | collective-permute-start | bytes 688136 | tf_op jit(solution)/shard_map/ppermute | solution.py:421
  62.6 14.4 %collective-permute-start.7 = (bf16[128,1024]{1,0:T(8,128)(2,1)S(1)}, bf16[128,1024]{1,0:T(8,128)(2,1)S(1)}, u32[]{:S(2)}, u32[]{:S(2)}) collective-permute-start(bf16[128,1024]{1,0:T(8,128)(2,1)S(1)} %slice.50), channel_id=1, source_target_pairs={{0,3},{1,0},{2,1},{3,2},{4,7},{5,4},{6,5},{7,6},{8,11},{9,8},{10,9... | collective-permute-start | bytes 786440 | tf_op jit(solution)/shard_map/ppermute | solution.py:75
  82.8 18.7 %all-to-all-start.1 = ((bf16[4,128,896]{2,1,0:T(8,128)(2,1)}), bf16[4,128,896]{2,1,0:T(8,128)(2,1)}, u32[]{:S(2)}, u32[]{:S(2)}) async-start(bf16[4,128,896]{2,1,0:T(8,128)(2,1)} %bitcast.53), calls=%async_computation.1 | async-start | bytes 1835008 | tf_op jit(solution)/shard_map/all_to_all | solution.py:466
  93.0 16.2 %collective-permute-start.16 = (bf16[2,64,512]{2,1,0:T(8,128)(2,1)S(1)}, bf16[2,64,512]{2,1,0:T(8,128)(2,1)S(1)}, u32[]{:S(2)}, u32[]{:S(2)}) collective-permute-start(bf16[2,64,512]{2,1,0:T(8,128)(2,1)S(1)} %get-tuple-element.45), channel_id=1, source_target_pairs={{0,3},{1,0},{2,1},{3,2},{4,7},{5,4},{6,5},{7,6},{8,11},{9,8},{10,9... | collective-permute-start | bytes 393224 | tf_op jit(solution)/shard_map/ppermute | solution.py:482
  96.1 13.1 %collective-permute-start.17 = (bf16[2,64,512]{2,1,0:T(8,128)(2,1)S(1)}, bf16[2,64,512]{2,1,0:T(8,128)(2,1)S(1)}, u32[]{:S(2)}, u32[]{:S(2)}) collective-permute-start(bf16[2,64,512]{2,1,0:T(8,128)(2,1)S(1)} %get-tuple-element.46), channel_id=1, source_target_pairs={{0,2},{1,3},{2,0},{3,1},{4,6},{5,7},{6,4},{7,5},{8,10},{9,11},{10,... | collective-permute-start | bytes 393224 | tf_op jit(solution)/shard_map/ppermute | solution.py:482
  122.1 18.0 %collective-permute-start.19 = (bf16[2,64,2048]{2,1,0:T(8,128)(2,1)}, bf16[2,64,2048]{2,1,0:T(8,128)(2,1)S(1)}, u32[]{:S(2)}, u32[]{:S(2)}) collective-permute-start(bf16[2,64,2048]{2,1,0:T(8,128)(2,1)} %get-tuple-element.48.c0), channel_id=1, source_target_pairs={{0,3},{1,0},{2,1},{3,2},{4,7},{5,4},{6,5},{7,6},{8,11},{9,8},{10,9... | collective-permute-start | bytes 1572872 | tf_op jit(solution)/shard_map/ppermute | solution.py:64
  124.1 20.4 %collective-permute-start.20 = (bf16[2,64,2048]{2,1,0:T(8,128)(2,1)}, bf16[2,64,2048]{2,1,0:T(8,128)(2,1)S(1)}, u32[]{:S(2)}, u32[]{:S(2)}) collective-permute-start(bf16[2,64,2048]{2,1,0:T(8,128)(2,1)} %get-tuple-element.48.c0), channel_id=1, source_target_pairs={{0,2},{1,3},{2,0},{3,1},{4,6},{5,7},{6,4},{7,5},{8,10},{9,11},{10,... | collective-permute-start | bytes 1572872 | tf_op jit(solution)/shard_map/ppermute | solution.py:64
  125.6 23.8 %collective-permute-start.21 = (bf16[2,64,2048]{2,1,0:T(8,128)(2,1)}, bf16[2,64,2048]{2,1,0:T(8,128)(2,1)S(1)}, u32[]{:S(2)}, u32[]{:S(2)}) collective-permute-start(bf16[2,64,2048]{2,1,0:T(8,128)(2,1)} %get-tuple-element.48.c0), channel_id=1, source_target_pairs={{0,1},{1,2},{2,3},{3,0},{4,5},{5,6},{6,7},{7,4},{8,9},{9,10},{10,1... | collective-permute-start | bytes 1572872 | tf_op jit(solution)/shard_map/ppermute | solution.py:64
  140.2 18.4 %collective-permute-start.22 = (bf16[64,1792]{1,0:T(8,128)(2,1)}, bf16[64,1792]{1,0:T(8,128)(2,1)S(1)}, u32[]{:S(2)}, u32[]{:S(2)}) collective-permute-start(bf16[64,1792]{1,0:T(8,128)(2,1)} %encoded_back.1), channel_id=1, source_target_pairs={{0,3},{1,0},{2,1},{3,2},{4,7},{5,4},{6,5},{7,6},{8,11},{9,8},{10,9... | collective-permute-start | bytes 688136 | tf_op jit(solution)/shard_map/ppermute | solution.py:64
  143.5 15.1 %collective-permute-start.23 = (bf16[64,1792]{1,0:T(8,128)(2,1)}, bf16[64,1792]{1,0:T(8,128)(2,1)}, u32[]{:S(2)}, u32[]{:S(2)}) collective-permute-start(bf16[64,1792]{1,0:T(8,128)(2,1)} %encoded_back.1), channel_id=1, source_target_pairs={{0,2},{1,3},{2,0},{3,1},{4,6},{5,7},{6,4},{7,5},{8,10},{9,11},{10,... | collective-permute-start | bytes 688136 | tf_op jit(solution)/shard_map/ppermute | solution.py:64
  144.3 14.3 %collective-permute-start.24 = (bf16[64,1792]{1,0:T(8,128)(2,1)}, bf16[64,1792]{1,0:T(8,128)(2,1)}, u32[]{:S(2)}, u32[]{:S(2)}) collective-permute-start(bf16[64,1792]{1,0:T(8,128)(2,1)} %encoded_back.1), channel_id=1, source_target_pairs={{0,1},{1,2},{2,3},{3,0},{4,5},{5,6},{6,7},{7,4},{8,9},{9,10},{10,1... | collective-permute-start | bytes 688136 | tf_op jit(solution)/shard_map/ppermute | solution.py:64
  (27 other events, 208.8 us)
Sparse Core Ops, SparseCore 0:
  28.5 60.9 all-gather.4
  92.4 52.3 all-gather.6

commit v8 on v7

--- a/solution.py
+++ b/solution.py
@@ -561,12 +561,13 @@
         (out_spec, out_spec),
         (sds((tokens, part_width), BF16), sds((tokens, part_width), F32)),
         [pltpu.VMEM((2, tokens, head_width), BF16), acc, acc],
-        40,
+        24,
     )(scalars, *both_parts, qo_all, qo_all, hidden, cotangent)
     d_cond_parts = after(d_cond_parts, from_query)
-    d_cond_all = lax.dynamic_slice_in_dim(
-        jnp.stack(d_cond_parts * 2), (n_tensor - here) % n_tensor, n_tensor, 0
-    ).reshape(tokens, 2 * enc_width)
+    d_cond_all = jnp.zeros((n_tensor, block_len, 2 * enc_width), BF16)
+    for k, part in enumerate(d_cond_parts):
+        d_cond_all = lax.dynamic_update_index_in_dim(d_cond_all, part, (here + k) % n_tensor, 0)
+    d_cond_all = d_cond_all.reshape(tokens, 2 * enc_width)
     grad_hidden = (from_query + dot(d_cond_all, cond_weight, ROWS_T)).astype(BF16)
     return (mixed, grad_hidden)
 

time: 172 us -> 171 us (level)
  waiting for transfers between devices: 32.2 us -> 28.7 us
    ppermute x1, waiting for transfers between devices: 4.26 us -> 0.01 us  [spread_halves(): far_bottom = lax.ppermute(last_bottom, axis, up)]
    unnamed x51 -> x46, local copies, waits for them, and re-layouts: 12.9 us -> 10.4 us
    dynamic_update_slice x0 -> x4, local copies, waits for them, and re-layouts: none -> 1.97 us  [shards(): lax.dynamic_update_index_in_dim(d_cond_all, part, (here + k) % n_tensor, 0)]
  transfers between devices with their start and end apart: 29 -> 29, of which waited for: 8 -> 7; matrix products, arithmetic and copies ran while one was open for 6% -> 6% of each run, Pallas kernels for 30% -> 30%
where the time goes in v8:
time: 171 us; the launch traced here: 169 us
  Pallas kernels  51.3 us (30%)
  starting transfers between devices  47.4 us (28%)
  waiting for transfers between devices  28.7 us (17%)
  local copies, waits for them, and re-layouts  19.8 us (12%)
  between operations  14.5 us (8%)
  matrix products  4.16 us (2%)
  other arithmetic  3.19 us (2%)
    pallas_call x1, Pallas kernels, shards(): call(encoded_back_kernel, 'encoded_back', n_tensor, [group(head_rows, row...  14.6 us
    pallas_call x1, Pallas kernels, shards(): call(attention_kernel, 'attention', n_tensor, [r_spec, kv_spec(0), kv_spe...  12.1 us
    unnamed x46, local copies, waits for them, and re-layouts  10.4 us
    pallas_call x2, Pallas kernels, projected(): call(functools.partial(project_kernel, dims, shift, counts), name, n_tens...  9.33 us
    ppermute x1, waiting for transfers between devices, spread_ring(): next_one = lax.ppermute(shard, axis, down)  8.82 us
    ppermute x6, starting transfers between devices, shards(): lax.ppermute(array, 'tensor', [(i, (i - k) % n_tensor) for i in range(n_t...  8.05 us
    ppermute x6, starting transfers between devices, spread(): lax.ppermute(shard, axis, [(i, (i - k) % size) for i in range(size)])  7.71 us
    pallas_call x1, Pallas kernels, shards(): call(encode_kernel, 'encode', 1, [r_spec] + [c_spec] * 4 + [w_spec] * 2,...  7.67 us
  transfers between devices with their start and end apart: 29, of which 7 were waited for; matrix products, arithmetic and copies ran while one was open for 6% of the time, Pallas kernels for 30%

profile of v8, /device:TPU:10, one launch (start us, length us, event | category | flops | bytes accessed | tf_op | source)
XLA Modules:
  0.0 169.0 jit_solution(865644947647299653)
XLA Ops:
  7.2 1.8 %fusion.11 = (bf16[128,1024]{1,0:T(8,128)(2,1)}, bf16[128,1024]{1,0:T(8,128)(2,1)S(1)}) fusion(bf16[256,1024]{1,0:T(8,128)(2,1)} %hidden_ref.3), kind=kLoop, calls=%fused_computation.34 | loop fusion | bytes 1048576 | tf_op jit(solution)/shard_map/slice | solution.py:84
  9.0 4.0 %collective-permute-start = (bf16[128,1024]{1,0:T(8,128)(2,1)S(1)}, bf16[128,1024]{1,0:T(8,128)(2,1)}, u32[]{:S(2)}, u32[]{:S(2)}) collective-permute-start(bf16[128,1024]{1,0:T(8,128)(2,1)S(1)} %get-tuple-element.63), channel_id=1, source_target_pairs={{0,3},{1,0},{2,1},{3,2},{4,7},{5,4},{6,5},{7,6},{8,11},{9,8},{10,9... | collective-permute-start | bytes 786440 | tf_op jit(solution)/shard_map/ppermute | solution.py:85
  16.2 4.7 %collective-permute-start.14 = (bf16[120,512]{1,0:T(8,128)(2,1)S(1)}, bf16[120,512]{1,0:T(8,128)(2,1)S(1)}, u32[]{:S(2)}, u32[]{:S(2)}) collective-permute-start(bf16[120,512]{1,0:T(8,128)(2,1)S(1)} %get-tuple-element.66), channel_id=1, source_target_pairs={{0,2},{1,3},{2,0},{3,1},{4,6},{5,7},{6,4},{7,5},{8,10},{9,11},{10,... | collective-permute-start | bytes 368648 | tf_op jit(solution)/shard_map/ppermute | solution.py:58
  22.2 2.0 %copy-done.4 = bf16[1024,1792]{1,0:T(8,128)(2,1)S(1)} copy-done((bf16[1024,1792]{1,0:T(8,128)(2,1)S(1)}, bf16[1024,1792]{1,0:T(8,128)(2,1)}, u32[]{:S(2)}) %copy-start.4) | copy-done | bytes 3670040
  28.4 7.6 %all-to-all-start = ((bf16[32,32,896]{2,1,0:T(8,128)(2,1)}), bf16[32,32,896]{2,1,0:T(8,128)(2,1)}, u32[]{:S(2)}, u32[]{:S(2)}) async-start(bf16[32,32,896]{2,1,0:T(8,128)(2,1)} %param.16), calls=%async_computation | async-start | bytes 3670016 | tf_op jit(solution)/shard_map/all_to_all | solution.py:461
  42.0 8.8 %collective-permute-done.6.refs_1_ = bf16[256,1024]{1,0:T(8,128)(2,1)S(1)} collective-permute-done((bf16[256,1024]{1,0:T(8,128)(2,1)S(1)}, bf16[256,1024]{1,0:T(8,128)(2,1)S(1)}, u32[]{:S(2)}, u32[]{:S(2)}) %collective-permute-start.6) | collective-permute-done | bytes 524320 | tf_op jit(solution)/shard_map/ppermute | solution.py:73
  52.0 6.9 %collective-permute-done.8.refs_4_ = bf16[256,1024]{1,0:T(8,128)(2,1)S(1)} collective-permute-done((bf16[256,1024]{1,0:T(8,128)(2,1)S(1)}, bf16[256,1024]{1,0:T(8,128)(2,1)S(1)}, u32[]{:S(2)}, u32[]{:S(2)}) %collective-permute-start.8) | collective-permute-done | bytes 524320 | tf_op jit(solution)/shard_map/ppermute | solution.py:74
  62.8 2.3 %collective-permute-start.7 = (bf16[128,1024]{1,0:T(8,128)(2,1)S(1)}, bf16[128,1024]{1,0:T(8,128)(2,1)S(1)}, u32[]{:S(2)}, u32[]{:S(2)}) collective-permute-start(bf16[128,1024]{1,0:T(8,128)(2,1)S(1)} %slice.50), channel_id=1, source_target_pairs={{0,3},{1,0},{2,1},{3,2},{4,7},{5,4},{6,5},{7,6},{8,11},{9,8},{10,9... | collective-permute-start | bytes 786440 | tf_op jit(solution)/shard_map/ppermute | solution.py:75
  69.0 6.4 %query.1.refs_6_ = bf16[256,512]{1,0:T(8,128)(2,1)} custom-call(s32[2]{0:T(128)} %copy-done.11, bf16[256,1024]{1,0:T(8,128)(2,1)} %hidden_ref.3, bf16[128,1024]{1,0:T(8,128)(2,1)} %collective-permute-done.refs_1_, bf16[128,1024]{1,0:T(8,128)(2,1)} %collective-permute-done.1.refs_2_, bf16[128,1024]{1,0:T(8,128)(2,1)} %collective-permute-done.2.refs_3_, ...), custom_call_target="tpu_custom_call" | custom-call | tf_op jit(solution)/shard_map/query/pallas_call | solution.py:432
  76.8 1.8 %collective-permute-done.9.refs_3_ = bf16[128,1024]{1,0:T(8,128)(2,1)S(1)} collective-permute-done((bf16[128,1024]{1,0:T(8,128)(2,1)}, bf16[128,1024]{1,0:T(8,128)(2,1)S(1)}, u32[]{:S(2)}, u32[]{:S(2)}) %collective-permute-start.9) | collective-permute-done | bytes 262176 | tf_op jit(solution)/shard_map/ppermute | solution.py:76
  78.8 2.2 %fusion.2 = bf16[16,32,896]{2,0,1:T(8,128)(2,1)S(1)} fusion(bf16[32,32,896]{2,1,0:T(8,128)(2,1)} %all-to-all-done, s32[16]{0:T(128)S(1)} %eq.26, pred[16]{0:T(512)(128)(4,1)S(1)} %lt.100), kind=kOutput, calls=%fused_computation.2 | convolution fusion | flops 29819904 | bytes 2752592 | tf_op jit(solution)/shard_map/si,sre->ire/dot_general | solution.py:462
  82.2 4.2 %all-to-all-start.1 = ((bf16[4,128,896]{2,1,0:T(8,128)(2,1)}), bf16[4,128,896]{2,1,0:T(8,128)(2,1)}, u32[]{:S(2)}, u32[]{:S(2)}) async-start(bf16[4,128,896]{2,1,0:T(8,128)(2,1)} %bitcast.49), calls=%async_computation.1 | async-start | bytes 1835008 | tf_op jit(solution)/shard_map/all_to_all | solution.py:466
  86.4 2.3 %copy-done.3 = bf16[512,4096]{1,0:T(8,128)(2,1)S(1)} copy-done((bf16[512,4096]{1,0:T(8,128)(2,1)S(1)}, bf16[512,4096]{1,0:T(8,128)(2,1)}, u32[]{:S(2)}) %copy-start.3) | copy-done | bytes 4194328
  88.7 2.9 %d_ctx.1 = (bf16[2,64,512]{2,1,0:T(8,128)(2,1)S(1)}, bf16[2,64,512]{2,1,0:T(8,128)(2,1)S(1)}, bf16[2,64,512]{2,1,0:T(8,128)(2,1)S(1)}, bf16[2,64,512]{2,1,0:T(8,128)(2,1)S(1)}) custom-call(s32[2]{0:T(128)S(1)} %copy-done.12, bf16[256,1024]{1,0:T(8,128)(2,1)S(1)} %copy-done.6, bf16[256,1024]{1,0:T(8,128)(2,1)S(1)} %collective-permute-done.6.refs_1_, ...), custom_call_target="tpu_custom_call" | custom-call | tf_op jit(solution)/shard_map/d_ctx/pallas_call | solution.py:432
  92.3 3.2 %collective-permute-start.16 = (bf16[2,64,512]{2,1,0:T(8,128)(2,1)S(1)}, bf16[2,64,512]{2,1,0:T(8,128)(2,1)S(1)}, u32[]{:S(2)}, u32[]{:S(2)}) collective-permute-start(bf16[2,64,512]{2,1,0:T(8,128)(2,1)S(1)} %get-tuple-element.45), channel_id=1, source_target_pairs={{0,3},{1,0},{2,1},{3,2},{4,7},{5,4},{6,5},{7,6},{8,11},{9,8},{10,9... | collective-permute-start | bytes 393224 | tf_op jit(solution)/shard_map/ppermute | solution.py:482
  97.2 4.1 %all-to-all-done.1 = bf16[4,128,896]{2,1,0:T(8,128)(2,1)} async-done(((bf16[4,128,896]{2,1,0:T(8,128)(2,1)}), bf16[4,128,896]{2,1,0:T(8,128)(2,1)}, u32[]{:S(2)}, u32[]{:S(2)}) %all-to-all-start.1) | async-done | bytes 917536 | tf_op jit(solution)/shard_map/all_to_all | solution.py:466
  101.4 7.7 %encode.1 = (bf16[64,1792]{1,0:T(8,128)(2,1)}, bf16[512,896]{1,0:T(8,128)(2,1)}, f32[448,512]{1,0:T(8,128)}, bf16[512,896]{1,0:T(8,128)(2,1)}) custom-call(s32[2]{0:T(128)} %copy-done.11, bf16[512,896]{1,0:T(8,128)(2,1)} %bitcast.5.x_ref, bf16[64,1792]{1,0:T(8,128)(2,1)} %copy-done.10, bf16[64,1792]{1,0:T(8,128)(2,1)} %copy-done.19, ...), custom_call_target="tpu_custom_call" | custom-call | tf_op jit(solution)/shard_map/encode/pallas_call | solution.py:490
  109.8 12.1 %attention.1 = (bf16[4,256,512]{2,1,0:T(8,128)(2,1)}, bf16[4,256,512]{2,1,0:T(8,128)(2,1)}, bf16[2,64,2048]{2,1,0:T(8,128)(2,1)}) custom-call(s32[2]{0:T(128)} %copy-done.11, bf16[512,896]{1,0:T(8,128)(2,1)} %get-tuple-element.37.encoded_ref, bf16[32,4,56,512]{3,2,1,0:T(8,128)(2,1)} %bitcast.44, bf16[32,4,56,512]{3,2,1,0:T(8,128)(2,1)} %bitcast.45, ...), custom_call_target="tpu_custom_call" | custom-call | tf_op jit(solution)/shard_map/attention/pallas_call | solution.py:509
  125.1 14.6 %encoded_back.1 = bf16[64,1792]{1,0:T(8,128)(2,1)} custom-call(s32[2]{0:T(128)} %copy-done.11, bf16[4,256,512]{2,1,0:T(8,128)(2,1)} %get-tuple-element.52.d_scores_ref, bf16[4,256,512]{2,1,0:T(8,128)(2,1)} %get-tuple-element.53.probs_ref, bf16[2,64,512]{2,1,0:T(8,128)(2,1)} %copy-done.8, bf16[2,64,512]{2,1,0:T(8,128)(2,1)} %copy-done.15, ...), custom_call_target="tpu_custom_call" | custom-call | tf_op jit(solution)/shard_map/encoded_back/pallas_call | solution.py:529
  139.6 3.3 %collective-permute-start.22 = (bf16[64,1792]{1,0:T(8,128)(2,1)}, bf16[64,1792]{1,0:T(8,128)(2,1)S(1)}, u32[]{:S(2)}, u32[]{:S(2)}) collective-permute-start(bf16[64,1792]{1,0:T(8,128)(2,1)} %encoded_back.1), channel_id=1, source_target_pairs={{0,3},{1,0},{2,1},{3,2},{4,7},{5,4},{6,5},{7,6},{8,11},{9,8},{10,9... | collective-permute-start | bytes 688136 | tf_op jit(solution)/shard_map/ppermute | solution.py:64
  144.3 4.7 %collective-permute-done.21.c3 = bf16[2,64,2048]{2,1,0:T(8,128)(2,1)S(1)} collective-permute-done((bf16[2,64,2048]{2,1,0:T(8,128)(2,1)}, bf16[2,64,2048]{2,1,0:T(8,128)(2,1)S(1)}, u32[]{:S(2)}, u32[]{:S(2)}) %collective-permute-start.21) | collective-permute-done | bytes 524320 | tf_op jit(solution)/shard_map/ppermute | solution.py:64
  148.9 3.4 %copy-done = bf16[128,64,512]{2,1,0:T(8,128)(2,1)S(1)} copy-done((bf16[128,64,512]{2,1,0:T(8,128)(2,1)S(1)}, bf16[128,64,512]{2,1,0:T(8,128)(2,1)}, u32[]{:S(2)}) %copy-start) | copy-done | bytes 8388632
  152.3 5.8 %outputs.1 = (bf16[256,1024]{1,0:T(8,128)(2,1)}, f32[256,1024]{1,0:T(8,128)S(1)}) custom-call(s32[2]{0:T(128)S(1)} %copy-done.13, bf16[2,64,2048]{2,1,0:T(8,128)(2,1)S(1)} %copy-done.9, bf16[2,64,2048]{2,1,0:T(8,128)(2,1)S(1)} %collective-permute-done.19.c1, bf16[2,64,2048]{2,1,0:T(8,128)(2,1)S(1)} %collective-permute-done.20.c2, ...), custom_call_target="tpu_custom_call" | custom-call | tf_op jit(solution)/shard_map/outputs/pallas_call | solution.py:556
  160.2 1.9 %fusion.5 = bf16[256,1024]{1,0:T(8,128)(2,1)} fusion(f32[256,1024]{1,0:T(8,128)S(1)} %get-tuple-element.51, bf16[256,1792]{1,0:T(8,128)(2,1)S(1)} %bitcast.50, bf16[1024,1792]{1,0:T(8,128)(2,1)S(1)} %copy-done.5), kind=kOutput, calls=%fused_computation.4 | convolution fusion | flops 940048384 | bytes 6160384 | tf_op jit(solution)/shard_map/dot_general | solution.py:24
  (123 shorter events, 35.6 us)
Async XLA Ops:
  7.2 101.9 %all-gather.5.cloned.1.call-start = ((), (), s32[]{:S(2)}) async-start(), calls=%async_computation.2 | async-start | bytes 7569408 | tf_op jit(solution)/shard_map/all_gather | solution.py:419
  9.0 19.3 %collective-permute-start = (bf16[128,1024]{1,0:T(8,128)(2,1)S(1)}, bf16[128,1024]{1,0:T(8,128)(2,1)}, u32[]{:S(2)}, u32[]{:S(2)}) collective-permute-start(bf16[128,1024]{1,0:T(8,128)(2,1)S(1)} %get-tuple-element.63), channel_id=1, source_target_pairs={{0,3},{1,0},{2,1},{3,2},{4,7},{5,4},{6,5},{7,6},{8,11},{9,8},{10,9... | collective-permute-start | bytes 786440 | tf_op jit(solution)/shard_map/ppermute | solution.py:85
  13.1 15.2 %collective-permute-start.3 = (bf16[128,1024]{1,0:T(8,128)(2,1)}, bf16[128,1024]{1,0:T(8,128)(2,1)}, u32[]{:S(2)}, u32[]{:S(2)}) collective-permute-start(bf16[128,1024]{1,0:T(8,128)(2,1)} %get-tuple-element.62), channel_id=1, source_target_pairs={{0,1},{1,2},{2,3},{3,0},{4,5},{5,6},{6,7},{7,4},{8,9},{9,10},{10,1... | collective-permute-start | bytes 786440 | tf_op jit(solution)/shard_map/ppermute | solution.py:86
  28.4 50.4 %all-to-all-start = ((bf16[32,32,896]{2,1,0:T(8,128)(2,1)}), bf16[32,32,896]{2,1,0:T(8,128)(2,1)}, u32[]{:S(2)}, u32[]{:S(2)}) async-start(bf16[32,32,896]{2,1,0:T(8,128)(2,1)} %param.16), calls=%async_computation | async-start | bytes 3670016 | tf_op jit(solution)/shard_map/all_to_all | solution.py:461
  35.9 113.0 %all-gather.7.cloned.1.call-start = ((), (), s32[]{:S(2)}) async-start(), calls=%async_computation.3 | async-start | bytes 8650752 | tf_op jit(solution)/shard_map/all_gather | solution.py:469
  36.0 14.8 %collective-permute-start.6 = (bf16[256,1024]{1,0:T(8,128)(2,1)S(1)}, bf16[256,1024]{1,0:T(8,128)(2,1)S(1)}, u32[]{:S(2)}, u32[]{:S(2)}) collective-permute-start(bf16[256,1024]{1,0:T(8,128)(2,1)S(1)} %copy-done.6), channel_id=1, source_target_pairs={{0,3},{1,0},{2,1},{3,2},{4,7},{5,4},{6,5},{7,6},{8,11},{9,8},{10,9... | collective-permute-start | bytes 1572872 | tf_op jit(solution)/shard_map/ppermute | solution.py:73
  36.6 24.4 %collective-permute-start.1 = (bf16[128,1024]{1,0:T(8,128)(2,1)}, bf16[128,1024]{1,0:T(8,128)(2,1)}, u32[]{:S(2)}, u32[]{:S(2)}) collective-permute-start(bf16[128,1024]{1,0:T(8,128)(2,1)} %get-tuple-element.62), channel_id=1, source_target_pairs={{0,3},{1,0},{2,1},{3,2},{4,7},{5,4},{6,5},{7,6},{8,11},{9,8},{10,9... | collective-permute-start | bytes 786440 | tf_op jit(solution)/shard_map/ppermute | solution.py:87
  37.3 24.6 %collective-permute-start.5 = (bf16[128,1024]{1,0:T(8,128)(2,1)S(1)}, bf16[128,1024]{1,0:T(8,128)(2,1)}, u32[]{:S(2)}, u32[]{:S(2)}) collective-permute-start(bf16[128,1024]{1,0:T(8,128)(2,1)S(1)} %get-tuple-element.63), channel_id=1, source_target_pairs={{0,1},{1,2},{2,3},{3,0},{4,5},{5,6},{6,7},{7,4},{8,9},{9,10},{10,1... | collective-permute-start | bytes 786440 | tf_op jit(solution)/shard_map/ppermute | solution.py:88
  38.6 20.3 %collective-permute-start.8 = (bf16[256,1024]{1,0:T(8,128)(2,1)S(1)}, bf16[256,1024]{1,0:T(8,128)(2,1)S(1)}, u32[]{:S(2)}, u32[]{:S(2)}) collective-permute-start(bf16[256,1024]{1,0:T(8,128)(2,1)S(1)} %copy-done.6), channel_id=1, source_target_pairs={{0,1},{1,2},{2,3},{3,0},{4,5},{5,6},{6,7},{7,4},{8,9},{9,10},{10,1... | collective-permute-start | bytes 1572872 | tf_op jit(solution)/shard_map/ppermute | solution.py:74
  40.2 22.6 %collective-permute-start.2 = (bf16[128,1024]{1,0:T(8,128)(2,1)}, bf16[128,1024]{1,0:T(8,128)(2,1)}, u32[]{:S(2)}, u32[]{:S(2)}) collective-permute-start(bf16[128,1024]{1,0:T(8,128)(2,1)} %collective-permute-done.refs_1_), channel_id=1, source_target_pairs={{0,3},{1,0},{2,1},{3,2},{4,7},{5,4},{6,5},{7,6},{8,11},{9,8},{10,9... | collective-permute-start | bytes 786440 | tf_op jit(solution)/shard_map/ppermute | solution.py:89
  50.8 14.3 %collective-permute-start.4 = (bf16[128,1024]{1,0:T(8,128)(2,1)}, bf16[128,1024]{1,0:T(8,128)(2,1)S(1)}, u32[]{:S(2)}, u32[]{:S(2)}) collective-permute-start(bf16[128,1024]{1,0:T(8,128)(2,1)} %collective-permute-done.3.refs_6_), channel_id=1, source_target_pairs={{0,1},{1,2},{2,3},{3,0},{4,5},{5,6},{6,7},{7,4},{8,9},{9,10},{10,1... | collective-permute-start | bytes 786440 | tf_op jit(solution)/shard_map/ppermute | solution.py:90
  59.0 16.5 %collective-permute-start.10 = (bf16[64,1792]{1,0:T(8,128)(2,1)S(1)}, bf16[64,1792]{1,0:T(8,128)(2,1)S(1)}, u32[]{:S(2)}, u32[]{:S(2)}) collective-permute-start(bf16[64,1792]{1,0:T(8,128)(2,1)S(1)} %get-tuple-element.32), channel_id=1, source_target_pairs={{0,3},{1,0},{2,1},{3,2},{4,7},{5,4},{6,5},{7,6},{8,11},{9,8},{10,9... | collective-permute-start | bytes 688136 | tf_op jit(solution)/shard_map/ppermute | solution.py:421
  61.0 14.4 %collective-permute-start.11 = (bf16[64,1792]{1,0:T(8,128)(2,1)S(1)}, bf16[64,1792]{1,0:T(8,128)(2,1)}, u32[]{:S(2)}, u32[]{:S(2)}) collective-permute-start(bf16[64,1792]{1,0:T(8,128)(2,1)S(1)} %get-tuple-element.33), channel_id=1, source_target_pairs={{0,2},{1,3},{2,0},{3,1},{4,6},{5,7},{6,4},{7,5},{8,10},{9,11},{10,... | collective-permute-start | bytes 688136 | tf_op jit(solution)/shard_map/ppermute | solution.py:421
  61.9 13.6 %collective-permute-start.12 = (bf16[64,1792]{1,0:T(8,128)(2,1)S(1)}, bf16[64,1792]{1,0:T(8,128)(2,1)}, u32[]{:S(2)}, u32[]{:S(2)}) collective-permute-start(bf16[64,1792]{1,0:T(8,128)(2,1)S(1)} %get-tuple-element.34), channel_id=1, source_target_pairs={{0,1},{1,2},{2,3},{3,0},{4,5},{5,6},{6,7},{7,4},{8,9},{9,10},{10,1... | collective-permute-start | bytes 688136 | tf_op jit(solution)/shard_map/ppermute | solution.py:421
  62.8 14.0 %collective-permute-start.7 = (bf16[128,1024]{1,0:T(8,128)(2,1)S(1)}, bf16[128,1024]{1,0:T(8,128)(2,1)S(1)}, u32[]{:S(2)}, u32[]{:S(2)}) collective-permute-start(bf16[128,1024]{1,0:T(8,128)(2,1)S(1)} %slice.50), channel_id=1, source_target_pairs={{0,3},{1,0},{2,1},{3,2},{4,7},{5,4},{6,5},{7,6},{8,11},{9,8},{10,9... | collective-permute-start | bytes 786440 | tf_op jit(solution)/shard_map/ppermute | solution.py:75
  82.2 19.2 %all-to-all-start.1 = ((bf16[4,128,896]{2,1,0:T(8,128)(2,1)}), bf16[4,128,896]{2,1,0:T(8,128)(2,1)}, u32[]{:S(2)}, u32[]{:S(2)}) async-start(bf16[4,128,896]{2,1,0:T(8,128)(2,1)} %bitcast.49), calls=%async_computation.1 | async-start | bytes 1835008 | tf_op jit(solution)/shard_map/all_to_all | solution.py:466
  92.3 16.8 %collective-permute-start.16 = (bf16[2,64,512]{2,1,0:T(8,128)(2,1)S(1)}, bf16[2,64,512]{2,1,0:T(8,128)(2,1)S(1)}, u32[]{:S(2)}, u32[]{:S(2)}) collective-permute-start(bf16[2,64,512]{2,1,0:T(8,128)(2,1)S(1)} %get-tuple-element.45), channel_id=1, source_target_pairs={{0,3},{1,0},{2,1},{3,2},{4,7},{5,4},{6,5},{7,6},{8,11},{9,8},{10,9... | collective-permute-start | bytes 393224 | tf_op jit(solution)/shard_map/ppermute | solution.py:482
  95.5 13.5 %collective-permute-start.17 = (bf16[2,64,512]{2,1,0:T(8,128)(2,1)S(1)}, bf16[2,64,512]{2,1,0:T(8,128)(2,1)S(1)}, u32[]{:S(2)}, u32[]{:S(2)}) collective-permute-start(bf16[2,64,512]{2,1,0:T(8,128)(2,1)S(1)} %get-tuple-element.46), channel_id=1, source_target_pairs={{0,2},{1,3},{2,0},{3,1},{4,6},{5,7},{6,4},{7,5},{8,10},{9,11},{10,... | collective-permute-start | bytes 393224 | tf_op jit(solution)/shard_map/ppermute | solution.py:482
  122.0 17.7 %collective-permute-start.19 = (bf16[2,64,2048]{2,1,0:T(8,128)(2,1)}, bf16[2,64,2048]{2,1,0:T(8,128)(2,1)S(1)}, u32[]{:S(2)}, u32[]{:S(2)}) collective-permute-start(bf16[2,64,2048]{2,1,0:T(8,128)(2,1)} %get-tuple-element.48.c0), channel_id=1, source_target_pairs={{0,3},{1,0},{2,1},{3,2},{4,7},{5,4},{6,5},{7,6},{8,11},{9,8},{10,9... | collective-permute-start | bytes 1572872 | tf_op jit(solution)/shard_map/ppermute | solution.py:64
  123.4 20.8 %collective-permute-start.20 = (bf16[2,64,2048]{2,1,0:T(8,128)(2,1)}, bf16[2,64,2048]{2,1,0:T(8,128)(2,1)S(1)}, u32[]{:S(2)}, u32[]{:S(2)}) collective-permute-start(bf16[2,64,2048]{2,1,0:T(8,128)(2,1)} %get-tuple-element.48.c0), channel_id=1, source_target_pairs={{0,2},{1,3},{2,0},{3,1},{4,6},{5,7},{6,4},{7,5},{8,10},{9,11},{10,... | collective-permute-start | bytes 1572872 | tf_op jit(solution)/shard_map/ppermute | solution.py:64
  125.0 23.9 %collective-permute-start.21 = (bf16[2,64,2048]{2,1,0:T(8,128)(2,1)}, bf16[2,64,2048]{2,1,0:T(8,128)(2,1)S(1)}, u32[]{:S(2)}, u32[]{:S(2)}) collective-permute-start(bf16[2,64,2048]{2,1,0:T(8,128)(2,1)} %get-tuple-element.48.c0), channel_id=1, source_target_pairs={{0,1},{1,2},{2,3},{3,0},{4,5},{5,6},{6,7},{7,4},{8,9},{9,10},{10,1... | collective-permute-start | bytes 1572872 | tf_op jit(solution)/shard_map/ppermute | solution.py:64
  139.6 18.5 %collective-permute-start.22 = (bf16[64,1792]{1,0:T(8,128)(2,1)}, bf16[64,1792]{1,0:T(8,128)(2,1)S(1)}, u32[]{:S(2)}, u32[]{:S(2)}) collective-permute-start(bf16[64,1792]{1,0:T(8,128)(2,1)} %encoded_back.1), channel_id=1, source_target_pairs={{0,3},{1,0},{2,1},{3,2},{4,7},{5,4},{6,5},{7,6},{8,11},{9,8},{10,9... | collective-permute-start | bytes 688136 | tf_op jit(solution)/shard_map/ppermute | solution.py:64
  142.9 15.2 %collective-permute-start.23 = (bf16[64,1792]{1,0:T(8,128)(2,1)}, bf16[64,1792]{1,0:T(8,128)(2,1)}, u32[]{:S(2)}, u32[]{:S(2)}) collective-permute-start(bf16[64,1792]{1,0:T(8,128)(2,1)} %encoded_back.1), channel_id=1, source_target_pairs={{0,2},{1,3},{2,0},{3,1},{4,6},{5,7},{6,4},{7,5},{8,10},{9,11},{10,... | collective-permute-start | bytes 688136 | tf_op jit(solution)/shard_map/ppermute | solution.py:64
  144.3 13.9 %collective-permute-start.24 = (bf16[64,1792]{1,0:T(8,128)(2,1)}, bf16[64,1792]{1,0:T(8,128)(2,1)}, u32[]{:S(2)}, u32[]{:S(2)}) collective-permute-start(bf16[64,1792]{1,0:T(8,128)(2,1)} %encoded_back.1), channel_id=1, source_target_pairs={{0,1},{1,2},{2,3},{3,0},{4,5},{5,6},{6,7},{7,4},{8,9},{9,10},{10,1... | collective-permute-start | bytes 688136 | tf_op jit(solution)/shard_map/ppermute | solution.py:64
  (28 other events, 277.5 us)
Sparse Core Ops, SparseCore 0:
  28.5 60.6 all-gather.4
  91.5 52.3 all-gather.6
